TPU v7x, 256 devices: a whole 4x4x8 slice. The times are simulated.
256 devices in a mesh: pipe: 8 (over x_hi, y), expert: 32 (over z, x_lo, core).
Axes of the slice: x: 4 (x_hi: 2, x_lo: 2; x = x_hi * 2 + x_lo), y: 4, z: 8, core: 2. Of those that a mesh axis runs over, the one named last changes fastest.
Arguments:
- grads_sent: bfloat16 [8, 2, 2048, 3584], P('pipe', None, 'expert'), may hold values from -6 to 6
- saved_in: bfloat16 [8, 2, 2048, 3584], P('pipe', None, 'expert'), may hold values from -41 to 41
- routes: int32 [8, 2, 2048, 2], P('pipe', None, 'expert'), may hold values from 0 to 7, as said below
- capacity: int32 [8, 8], P('pipe'), may hold values from 8 to 16, as said below
- saved_pre: bfloat16 [8, 2, 32, 16, 2, 8192], P('pipe', None, None, None, None, 'expert'), may hold values from -6 to 6
- w_gate: bfloat16 [8, 3584, 8192], P('pipe', None, 'expert'), may hold values from -0.09375 to 0.09375
- w_up: bfloat16 [8, 3584, 8192], P('pipe', None, 'expert'), may hold values from -0.09375 to 0.09375
- w_down: bfloat16 [8, 8192, 3584], P('pipe', 'expert'), may hold values from -0.1875 to 0.1875
- router: float32 [8, 3584, 8], P('pipe'), may hold values from -0.09375 to 0.09375
- norm_gain: float32 [8, 3584], P('pipe'), may hold values from 0.25 to 1.75
Outputs:
- grads_in: bfloat16 [8, 2, 2048, 3584], P('pipe', None, 'expert')
Inputs may be any that keep to these rules, and one draw needn't show every extreme that they name: `routes`: every row names 2 different experts. In every block of 64 rows that one device holds for one micro-batch, one and the same expert of the section is named by exactly 24 rows, for both micro-batches and all blocks of the section. In every section the expert that all blocks of the section name most often has capacity 16.
All inputs are finite; a program needn't handle non-finite values.
Results may differ from a plain program's by a relative error of at most 0.0061.
Values may be sent and summed in bfloat16 or wider, within the bound.
No kernel may reach another device: no remote copies, remote signals or barrier semaphores. Data moves between devices by JAX's collectives and lax.ppermute only.
A program may use at most 128 MiB of HBM per device.

v0:
```python
import functools

import jax
import jax.numpy as jnp
from jax import lax
from jax.experimental import pallas as pl
from jax.experimental.pallas import tpu as pltpu
from jax.sharding import PartitionSpec as P

ROUTE_SCALE = 2.5
EPSILON = 1e-06
HIGHEST = lax.Precision.HIGHEST
F32 = jnp.float32
BF16 = jnp.bfloat16
D = 3584
EXPERTS = 8
CAP = 16
TOKENS = 64
SLOTS = EXPERTS * CAP
SLICE = 256
WIDE = D + 128
UNIT = 2 * CAP
NT = (((1,), (1,)), ((), ()))
TN = (((0,), (0,)), ((), ()))
COST = 100_000
WORK = 2_000_000_000
LIMIT = 24 * 1024 * 1024

VMEM = pl.BlockSpec(memory_space=pltpu.VMEM)
SMEM = pl.BlockSpec(memory_space=pltpu.SMEM)


def pipe_shift(value, by):
    return lax.ppermute(value, "pipe", [(i, (i + by) % 8) for i in range(8)])


def z_shift(value, by):
    pairs = [(i, ((i // 4 + by) % 8) * 4 + i % 4) for i in range(32)]
    return lax.ppermute(value, "expert", pairs)


def x_swap(value):
    return lax.ppermute(value, "expert", [(i, i ^ 2) for i in range(32)])


def core_swap(value):
    return lax.ppermute(value, "expert", [(i, i ^ 1) for i in range(32)])


def call(kernel, outs, specs, flops, moved):
    return pl.pallas_call(
        kernel,
        out_shape=outs,
        in_specs=specs,
        out_specs=jax.tree.map(lambda _: VMEM, outs),
        cost_estimate=pl.CostEstimate(flops=flops, bytes_accessed=moved, transcendentals=0),
        compiler_params=pltpu.CompilerParams(vmem_limit_bytes=LIMIT),
    )


def lanes(value_hi, value_lo, shape):
    lane = lax.broadcasted_iota(jnp.int32, shape, 1)
    return jnp.where(lane == 0, value_hi, jnp.where(lane == 1, value_lo, 0.0))


def split_sum(tile):
    total = jnp.sum(tile, axis=-1, keepdims=True)
    high = total.astype(BF16).astype(F32)
    return high, total - high


def prep_kernel(place, limits, routes, saved, gain, router, match, weight, scores, inv):
    z = place[0]
    slot = lax.broadcasted_iota(jnp.int32, (SLOTS, TOKENS), 0)
    expert = ((slot >> 4) + z) & (EXPERTS - 1)
    number = slot & (CAP - 1)
    limit = jnp.zeros((SLOTS, TOKENS), jnp.int32)
    for e in range(EXPERTS):
        limit = jnp.where(expert == e, limits[e], limit)
    allowed = number < limit
    earlier = (
        lax.broadcasted_iota(jnp.int32, (TOKENS, TOKENS), 0)
        < lax.broadcasted_iota(jnp.int32, (TOKENS, TOKENS), 1)
    ).astype(BF16)
    names = lax.broadcasted_iota(jnp.int32, (EXPERTS, TOKENS), 0)
    for m in range(2):
        values = saved[m].astype(F32)
        inv_rms = lax.rsqrt(jnp.mean(values * values, axis=-1, keepdims=True) + EPSILON)
        inv[m] = inv_rms
        normed = values * inv_rms * gain[...]
        logits = lax.dot_general(
            router[...], normed, NT, precision=HIGHEST, preferred_element_type=F32
        )
        score = jax.nn.sigmoid(logits)
        scores[m] = score
        picked = [routes[m, k : k + 1, :] == expert for k in range(2)]
        chosen = [
            jnp.sum(jnp.where(routes[m, k : k + 1, :] == names, score, 0.0), axis=0, keepdims=True)
            for k in range(2)
        ]
        totals = chosen[0] + chosen[1]
        counts = picked[0].astype(F32) + picked[1].astype(F32)
        before = jnp.dot(counts.astype(BF16), earlier, preferred_element_type=F32)
        kept = allowed & (before.astype(jnp.int32) == number)
        column = jnp.zeros((SLOTS, 1), F32)
        for k in range(2):
            hit = (picked[k] & kept).astype(F32)
            match[m, k] = hit
            share = (ROUTE_SCALE * chosen[k] / totals).astype(BF16).astype(F32)
            column = column + jnp.sum(hit * share, axis=-1, keepdims=True)
        weight[m] = jnp.broadcast_to(column, (SLOTS, 128)).astype(BF16)


def spread_kernel(first, second, match, weight, kept, *outs):
    for m, rows in enumerate((first, second)):
        kept[m] = rows[...]
        both = (match[m, 0] + match[m, 1]).astype(BF16)
        filled = jnp.dot(both, rows[...], preferred_element_type=F32).astype(BF16)
        for k in range(EXPERTS):
            outs[k][m * CAP : (m + 1) * CAP, :D] = filled[k * CAP : (k + 1) * CAP]
            outs[k][m * CAP : (m + 1) * CAP, D:] = weight[m, k * CAP : (k + 1) * CAP]


def stage_kernel(w_down, w_gate, w_up, packed):
    step = 512
    packed[:SLICE] = w_down[0]
    for at in range(0, D, step):
        packed[SLICE : 2 * SLICE, at : at + step] = w_gate[0, at : at + step].T
        packed[2 * SLICE :, at : at + step] = w_up[0, at : at + step].T


def pack_kernel(low, high, out):
    out[:UNIT] = low[...]
    out[UNIT:] = high[...]


def unit_kernel(shifts, place, mine, theirs, *refs):
    saved, weights = refs[0:2], refs[2:4]
    own, away, rows = refs[4:]
    n = len(shifts)
    z, x = place[0], place[1]
    size = UNIT * 2 * n
    half = size // 2
    rows[:half] = mine[...]
    rows[half:] = theirs[...]
    weight = rows[:, D:].astype(F32)[:, :1]
    total = jnp.zeros((size, 1), F32)
    grads = []
    for s in range(2):
        parts = [[], []]
        for side in range(2):
            for shift in shifts:
                source = (z + 8 - shift) & 7
                column = x if side == 0 else 1 - x
                for part in range(2):
                    parts[part].append(saved[s][source, column, part].reshape(UNIT, SLICE))
        gate = jnp.concatenate(parts[0], axis=0).astype(F32)
        up = jnp.concatenate(parts[1], axis=0).astype(F32)
        projected = lax.dot_general(
            rows[:, :D], weights[s][:SLICE], NT, preferred_element_type=F32
        )
        sig = jax.nn.sigmoid(gate)
        act = gate * sig
        total = total + jnp.sum(projected * (act * up), axis=-1, keepdims=True)
        grad = weight * projected
        gate_grad = (grad * up * sig * (1.0 + gate * (1.0 - sig))).astype(BF16)
        grads.append(jnp.concatenate([gate_grad, (grad * act).astype(BF16)], axis=1))
    step = 512
    for at in range(0, D, step):
        part = jnp.dot(grads[0], weights[0][SLICE:, at : at + step], preferred_element_type=F32)
        part = part + jnp.dot(
            grads[1], weights[1][SLICE:, at : at + step], preferred_element_type=F32
        )
        own[:, at : at + step] = part[:half]
        away[:, at : at + step] = part[half:].astype(BF16)
    high, low = split_sum(total)
    tile = lanes(high, low, (size, 128))
    own[:, D:] = tile[:half]
    away[:, D:] = tile[half:].astype(BF16)


def add_kernel(own, got, *outs):
    for i, out in enumerate(outs):
        at = slice(i * UNIT, (i + 1) * UNIT)
        out[:, :D] = (own[at, :D] + got[at, :D].astype(F32)).astype(BF16)
        high, low = split_sum(own[at, D:] + got[at, D:].astype(F32))
        out[:, D:] = lanes(high, low, (UNIT, 128)).astype(BF16)


def finish_kernel(
    own, got, b1, b2, b3, b4, b5, b6, b7, kept, saved, routes, match, scores, inv,
    gain, router, out, back,
):
    units = (None, b1, b2, b3, b4, b5, b6, b7)
    names = lax.broadcasted_iota(jnp.int32, (EXPERTS, TOKENS), 0)
    for m in range(2):
        at = slice(m * CAP, (m + 1) * CAP)
        back[:CAP] = (own[at, :D] + got[at, :D].astype(F32)).astype(BF16)
        dws = [own[at, D:] + got[at, D:].astype(F32)]
        for k in range(1, EXPERTS):
            back[k * CAP : (k + 1) * CAP] = units[k][at, :D]
            dws.append(units[k][at, D:].astype(F32))
        slot_dw = jnp.sum(jnp.concatenate(dws, axis=0), axis=-1, keepdims=True)
        score = scores[m]
        chosen, choice = [], []
        for k in range(2):
            mine = routes[m, k : k + 1, :] == names
            chosen.append(jnp.sum(jnp.where(mine, score, 0.0), axis=0, keepdims=True))
            choice.append(jnp.sum(match[m, k] * slot_dw, axis=0, keepdims=True))
        totals = chosen[0] + chosen[1]
        inner = (choice[0] * chosen[0] + choice[1] * chosen[1]) / (totals * totals)
        score_grad = jnp.zeros((EXPERTS, TOKENS), F32)
        for k in range(2):
            mine = routes[m, k : k + 1, :] == names
            slope = ROUTE_SCALE * (choice[k] / totals - inner)
            score_grad = score_grad + jnp.where(mine, slope, 0.0)
        score_grad = score_grad * score * (1.0 - score)
        both = (match[m, 0] + match[m, 1]).astype(BF16)
        total = lax.dot_general(both, back[...], TN, preferred_element_type=F32)
        total = total + lax.dot_general(
            score_grad, router[...], TN, precision=HIGHEST, preferred_element_type=F32
        )
        scaled = gain[...] * total
        values = saved[m].astype(F32)
        inv_rms = inv[m]
        mean = jnp.mean(values * scaled, axis=-1, keepdims=True)
        out[m] = (
            kept[m].astype(F32)
            + inv_rms * scaled
            - (inv_rms * inv_rms * inv_rms * mean) * values
        ).astype(BF16)


def shape(dims, dtype=BF16):
    return jax.ShapeDtypeStruct(dims, dtype)


def local(
    grads_sent, saved_in, routes, capacity, saved_pre, w_gate, w_up, w_down, router, norm_gain
):
    index = lax.axis_index("expert")
    core = index % 2
    place = jnp.stack([index // 4, (index // 2) % 2]).astype(jnp.int32)
    first, second = lax.optimization_barrier((grads_sent[0, 0], grads_sent[0, 1]))
    first, second = pipe_shift(first, -1), pipe_shift(second, 1)
    packed = call(stage_kernel, shape((3 * SLICE, D)), [VMEM] * 3, COST, 1000)(
        w_down, w_gate, w_up
    )
    pre = saved_pre[0].reshape(2, 8, 2, 2, CAP, 2, SLICE)
    pre = jnp.transpose(pre, (3, 1, 2, 5, 0, 4, 6))
    routes_t = jnp.transpose(routes[0], (0, 2, 1))
    router_t = router[0].T
    match, weight, scores, inv = call(
        prep_kernel,
        (
            shape((2, 2, SLOTS, TOKENS), F32),
            shape((2, SLOTS, 128)),
            shape((2, EXPERTS, TOKENS), F32),
            shape((2, TOKENS, 1), F32),
        ),
        [SMEM, SMEM] + [VMEM] * 4,
        COST,
        1000,
    )(place, capacity[0], routes_t, saved_in[0], norm_gain, router_t)
    pre_own = lax.dynamic_index_in_dim(pre, core, 0, keepdims=False)
    pre_other = lax.dynamic_index_in_dim(pre, 1 - core, 0, keepdims=False)
    first, second, packed, pre_own, pre_other, weight = lax.optimization_barrier(
        (first, second, packed, pre_own, pre_other, weight)
    )
    pre_other, weights = core_swap(pre_other), (packed, core_swap(packed))
    kept, *units = call(
        spread_kernel,
        (shape((2, TOKENS, D)),) + tuple(shape((UNIT, WIDE)) for _ in range(EXPERTS)),
        [VMEM] * 4,
        COST,
        1000,
    )(first, second, match, weight)
    def work(group, mine, theirs):
        n = len(group)
        return pl.pallas_call(
            functools.partial(unit_kernel, group),
            out_shape=(shape((UNIT * n, WIDE), F32), shape((UNIT * n, WIDE))),
            in_specs=[SMEM] + [VMEM] * 6,
            out_specs=(VMEM, VMEM),
            scratch_shapes=[pltpu.VMEM((2 * UNIT * n, WIDE), BF16)],
            cost_estimate=pl.CostEstimate(flops=WORK, bytes_accessed=1000, transcendentals=0),
            compiler_params=pltpu.CompilerParams(vmem_limit_bytes=LIMIT),
        )(place, mine, theirs, pre_own, pre_other, *weights)

    def add(group, own, got):
        return call(add_kernel, tuple(shape((UNIT, WIDE)) for _ in group), [VMEM] * 2, COST, 1000)(
            own, got
        )

    def pack(low, high):
        return call(pack_kernel, shape((2 * UNIT, WIDE)), [VMEM] * 2, COST, 1000)(low, high)

    v = {"u%d" % k: units[k] for k in range(EXPERTS)}

    def tie(names):
        names = names.split()
        v.update(zip(names, lax.optimization_barrier(tuple(v[n] for n in names))))

    def z_out(*shifts):
        for k in shifts:
            v["m%d" % k] = z_shift(v["u%d" % k], k)

    def z_back(*shifts):
        for k in shifts:
            v["b%d" % k] = z_shift(v["d%d" % k], -k)

    v["t0"] = x_swap(v["u0"])
    z_out(1, 7)
    tie("t0 u0 m1 m7 u3 u5")
    z_out(3, 5)
    v["p1"] = pack(v["m1"], v["m7"])
    v["t1"] = x_swap(v["p1"])
    v["own1"], v["away1"] = work((1, 7), v["p1"], v["t1"])
    tie("m3 m5 own1 away1 u2 u6 u4 t0 u0")
    z_out(4, 2, 6)
    v["p3"] = pack(v["m3"], v["m5"])
    v["t3"] = x_swap(v["p3"])
    v["got1"] = x_swap(v["away1"])
    v["own3"], v["away3"] = work((3, 5), v["p3"], v["t3"])
    tie("got1 own1 own3 away3 m4 m2 m6 t0 u0")
    v["d1"], v["d7"] = add((1, 7), v["own1"], v["got1"])
    z_back(1, 7)
    v["t4"] = x_swap(v["m4"])
    v["got3"] = x_swap(v["away3"])
    v["own4"], v["away4"] = work((4,), v["m4"], v["t4"])
    tie("b1 b7 own4 away4 got3 own3 m2 m6 t0 u0")
    v["d3"], v["d5"] = add((3, 5), v["own3"], v["got3"])
    z_back(3, 5)
    v["p2"] = pack(v["m2"], v["m6"])
    v["t2"] = x_swap(v["p2"])
    v["got4"] = x_swap(v["away4"])
    v["own2"], v["away2"] = work((2, 6), v["p2"], v["t2"])
    tie("b3 b5 own2 away2 got4 own4 t0 u0")
    (v["d4"],) = add((4,), v["own4"], v["got4"])
    z_back(4)
    v["got2"] = x_swap(v["away2"])
    v["own0"], v["away0"] = work((0,), v["u0"], v["t0"])
    tie("b4 got2 own2 own0 away0")
    v["got0"] = x_swap(v["away0"])
    v["d2"], v["d6"] = add((2, 6), v["own2"], v["got2"])
    z_back(2, 6)
    back = [(v["own0"], v["got0"])] + [v["b%d" % k] for k in range(1, EXPERTS)]
    out = pl.pallas_call(
        finish_kernel,
        out_shape=shape((2, TOKENS, D)),
        in_specs=[VMEM] * 17,
        out_specs=VMEM,
        scratch_shapes=[pltpu.VMEM((SLOTS, D), BF16)],
        cost_estimate=pl.CostEstimate(
            flops=COST, bytes_accessed=1000, transcendentals=0
        ),
        compiler_params=pltpu.CompilerParams(vmem_limit_bytes=LIMIT),
    )(
        *back[0],
        *back[1:],
        kept,
        saved_in[0],
        routes_t,
        match,
        scores,
        inv,
        norm_gain,
        router_t,
    )
    return out[None]


def solution(mesh):
    return jax.shard_map(
        local,
        mesh=mesh,
        in_specs=(
            P("pipe", None, "expert", None),
            P("pipe", None, "expert", None),
            P("pipe", None, "expert", None),
            P("pipe", None),
            P("pipe", None, None, None, None, "expert"),
            P("pipe", None, "expert"),
            P("pipe", None, "expert"),
            P("pipe", "expert", None),
            P("pipe", None, None),
            P("pipe", None),
        ),
        out_specs=P("pipe", None, "expert", None),
        check_vma=False,
    )
```

profile of v0, /device:TPU:32, one launch (start us, length us, event | category | flops | bytes accessed | tf_op | source)
XLA Modules:
  0.0 163.1 jit_solution(11205550667242619260)
XLA Ops:
  2.3 5.5 %collective-permute-start = (bf16[64,3584]{1,0:T(8,128)(2,1)}, bf16[64,3584]{1,0:T(8,128)(2,1)S(1)}, u32[]{:S(2)}, u32[]{:S(2)}) collective-permute-start(bf16[64,3584]{1,0:T(8,128)(2,1)} %get-tuple-element.89), channel_id=1, source_target_pairs={{0,224},{32,0},{64,32},{96,64},{128,96},{160,128},{192,160},{224,1... | collective-permute-start | bytes 1376264 | tf_op jit(solution)/shard_map/ppermute | solution.py:34
  16.9 2.7 %constant_dynamic-slice_fusion = (bf16[2,8,2,1,16,2,256]{6,5,4,3,2,1,0:T(2,128)(2,1)S(1)}, bf16[2,8,2,1,16,2,256]{6,5,4,3,2,1,0:T(2,128)(2,1)S(1)}) fusion(bf16[2,8,2,2,16,2,256]{6,5,4,3,2,1,0:T(2,128)(2,1)} %bitcast.31, s32[]{:T(128)S(6)} %select_n.27, s32[]{:T(128)S(6)} %select_n.26), kind=kLoop, calls=%fused_computation.5 | loop fusion | bytes 2097160 | tf_op jit(solution)/shard_map/dynamic-slice.1
  19.8 3.8 %collective-permute-done.1.second = bf16[64,3584]{1,0:T(8,128)(2,1)} collective-permute-done((bf16[64,3584]{1,0:T(8,128)(2,1)}, bf16[64,3584]{1,0:T(8,128)(2,1)}, u32[]{:S(2)}, u32[]{:S(2)}) %collective-permute-start.1) | collective-permute-done | bytes 458784 | tf_op jit(solution)/shard_map/ppermute | solution.py:34
  28.1 5.6 %collective-permute-done.3.low = bf16[32,3712]{1,0:T(8,128)(2,1)S(1)} collective-permute-done((bf16[32,3712]{1,0:T(8,128)(2,1)S(1)}, bf16[32,3712]{1,0:T(8,128)(2,1)S(1)}, u32[]{:S(2)}, u32[]{:S(2)}) %collective-permute-start.3) | collective-permute-done | bytes 237600 | tf_op jit(solution)/shard_map/ppermute | solution.py:39
  36.2 6.7 %collective-permute-start.5 = (bf16[32,3712]{1,0:T(8,128)(2,1)S(1)}, bf16[32,3712]{1,0:T(8,128)(2,1)S(1)}, u32[]{:S(2)}, u32[]{:S(2)}) collective-permute-start(bf16[32,3712]{1,0:T(8,128)(2,1)S(1)} %get-tuple-element.101), channel_id=1, source_target_pairs={{0,12},{1,13},{2,14},{3,15},{4,16},{5,17},{6,18},{7,19},{8,20},{9,... | collective-permute-start | bytes 712712 | tf_op jit(solution)/shard_map/ppermute | solution.py:39
  42.9 5.1 %collective-permute-done.7.theirs = bf16[64,3712]{1,0:T(8,128)(2,1)S(1)} collective-permute-done((bf16[64,3712]{1,0:T(8,128)(2,1)S(1)}, bf16[64,3712]{1,0:T(8,128)(2,1)S(1)}, u32[]{:S(2)}, u32[]{:S(2)}) %collective-permute-start.7) | collective-permute-done | bytes 475168 | tf_op jit(solution)/shard_map/ppermute | solution.py:43
  48.0 3.0 %shard_map.104 = (f32[64,3712]{1,0:T(8,128)S(1)}, bf16[64,3712]{1,0:T(8,128)(2,1)S(1)}) custom-call(s32[2]{0:T(128)S(1)} %pad_add_fusion.place, bf16[64,3712]{1,0:T(8,128)(2,1)S(1)} %shard_map.103.mine, bf16[64,3712]{1,0:T(8,128)(2,1)S(1)} %collective-permute-done.7.theirs, bf16[8,2,2,2,16,256]{5,4,3,2,1,0:T(8,128)(2,1)S(1)} %get-tuple-element.105.refs_0_, ...), custom_call_target="tpu_custom_call" | custom-call | flops 2000000000 | bytes 1000 | tf_op jit(solution)/shard_map/pallas_call | solution.py:280
  51.0 6.1 %collective-permute-done.5.low = bf16[32,3712]{1,0:T(8,128)(2,1)S(1)} collective-permute-done((bf16[32,3712]{1,0:T(8,128)(2,1)S(1)}, bf16[32,3712]{1,0:T(8,128)(2,1)S(1)}, u32[]{:S(2)}, u32[]{:S(2)}) %collective-permute-start.5) | collective-permute-done | bytes 237600 | tf_op jit(solution)/shard_map/ppermute | solution.py:39
  57.2 4.8 %collective-permute-done.6.high = bf16[32,3712]{1,0:T(8,128)(2,1)S(1)} collective-permute-done((bf16[32,3712]{1,0:T(8,128)(2,1)S(1)}, bf16[32,3712]{1,0:T(8,128)(2,1)S(1)}, u32[]{:S(2)}, u32[]{:S(2)}) %collective-permute-start.6) | collective-permute-done | bytes 237600 | tf_op jit(solution)/shard_map/ppermute | solution.py:39
  69.7 6.2 %collective-permute-done.11.theirs = bf16[64,3712]{1,0:T(8,128)(2,1)S(1)} collective-permute-done((bf16[64,3712]{1,0:T(8,128)(2,1)S(1)}, bf16[64,3712]{1,0:T(8,128)(2,1)S(1)}, u32[]{:S(2)}, u32[]{:S(2)}) %collective-permute-start.11) | collective-permute-done | bytes 475168 | tf_op jit(solution)/shard_map/ppermute | solution.py:43
  75.9 3.1 %shard_map.106 = (f32[64,3712]{1,0:T(8,128)S(1)}, bf16[64,3712]{1,0:T(8,128)(2,1)S(1)}) custom-call(s32[2]{0:T(128)S(1)} %pad_add_fusion.place, bf16[64,3712]{1,0:T(8,128)(2,1)S(1)} %shard_map.105.mine, bf16[64,3712]{1,0:T(8,128)(2,1)S(1)} %collective-permute-done.11.theirs, bf16[8,2,2,2,16,256]{5,4,3,2,1,0:T(8,128)(2,1)S(1)} %get-tuple-element.105.refs_0_, ...), custom_call_target="tpu_custom_call" | custom-call | flops 2000000000 | bytes 1000 | tf_op jit(solution)/shard_map/pallas_call | solution.py:280
  79.0 6.1 %collective-permute-done.13.low = bf16[32,3712]{1,0:T(8,128)(2,1)S(1)} collective-permute-done((bf16[32,3712]{1,0:T(8,128)(2,1)S(1)}, bf16[32,3712]{1,0:T(8,128)(2,1)S(1)}, u32[]{:S(2)}, u32[]{:S(2)}) %collective-permute-start.13) | collective-permute-done | bytes 237600 | tf_op jit(solution)/shard_map/ppermute | solution.py:39
  89.6 12.6 %collective-permute-done.17.theirs = bf16[32,3712]{1,0:T(8,128)(2,1)S(1)} collective-permute-done((bf16[32,3712]{1,0:T(8,128)(2,1)S(1)}, bf16[32,3712]{1,0:T(8,128)(2,1)S(1)}, u32[]{:S(2)}, u32[]{:S(2)}) %collective-permute-start.17) | collective-permute-done | bytes 237600 | tf_op jit(solution)/shard_map/ppermute | solution.py:43
  102.2 3.1 %shard_map.108 = (f32[32,3712]{1,0:T(8,128)S(1)}, bf16[32,3712]{1,0:T(8,128)(2,1)S(1)}) custom-call(s32[2]{0:T(128)S(1)} %pad_add_fusion.place, bf16[32,3712]{1,0:T(8,128)(2,1)S(1)} %collective-permute-done.12.mine, bf16[32,3712]{1,0:T(8,128)(2,1)S(1)} %collective-permute-done.17.theirs, bf16[8,2,2,2,16,256]{5,4,3,2,1,0:T(8,128)(2,1)S(1)} %get-tuple-element.105.refs_0_, ...), custom_call_target="tpu_custom_call" | custom-call | flops 2000000000 | bytes 1000 | tf_op jit(solution)/shard_map/pallas_call | solution.py:280
  107.0 3.9 %collective-permute-start.19 = (bf16[32,3712]{1,0:T(8,128)(2,1)S(1)}, bf16[32,3712]{1,0:T(8,128)(2,1)S(1)}, u32[]{:S(2)}, u32[]{:S(2)}) collective-permute-start(bf16[32,3712]{1,0:T(8,128)(2,1)S(1)} %get-tuple-element.141), channel_id=1, source_target_pairs={{0,20},{1,21},{2,22},{3,23},{4,24},{5,25},{6,26},{7,27},{8,28},{9,... | collective-permute-start | bytes 712712 | tf_op jit(solution)/shard_map/ppermute | solution.py:39
  113.0 6.1 %collective-permute-done.21.theirs = bf16[64,3712]{1,0:T(8,128)(2,1)S(1)} collective-permute-done((bf16[64,3712]{1,0:T(8,128)(2,1)S(1)}, bf16[64,3712]{1,0:T(8,128)(2,1)S(1)}, u32[]{:S(2)}, u32[]{:S(2)}) %collective-permute-start.21) | collective-permute-done | bytes 475168 | tf_op jit(solution)/shard_map/ppermute | solution.py:43
  119.1 3.0 %shard_map.111 = (f32[64,3712]{1,0:T(8,128)S(1)}, bf16[64,3712]{1,0:T(8,128)(2,1)S(1)}) custom-call(s32[2]{0:T(128)S(1)} %pad_add_fusion.place, bf16[64,3712]{1,0:T(8,128)(2,1)S(1)} %shard_map.110.mine, bf16[64,3712]{1,0:T(8,128)(2,1)S(1)} %collective-permute-done.21.theirs, bf16[8,2,2,2,16,256]{5,4,3,2,1,0:T(8,128)(2,1)S(1)} %get-tuple-element.105.refs_0_, ...), custom_call_target="tpu_custom_call" | custom-call | flops 2000000000 | bytes 1000 | tf_op jit(solution)/shard_map/pallas_call | solution.py:280
  125.6 6.0 %collective-permute-start.23 = (bf16[32,3712]{1,0:T(8,128)(2,1)S(1)}, bf16[32,3712]{1,0:T(8,128)(2,1)S(1)}, u32[]{:S(2)}, u32[]{:S(2)}) collective-permute-start(bf16[32,3712]{1,0:T(8,128)(2,1)S(1)} %shard_map.112), channel_id=1, source_target_pairs={{0,16},{1,17},{2,18},{3,19},{4,20},{5,21},{6,22},{7,23},{8,24},{9,... | collective-permute-start | bytes 712712 | tf_op jit(solution)/shard_map/ppermute | solution.py:39
  131.6 3.1 %shard_map.113 = (f32[32,3712]{1,0:T(8,128)S(1)}, bf16[32,3712]{1,0:T(8,128)(2,1)S(1)}) custom-call(s32[2]{0:T(128)S(1)} %pad_add_fusion.place, bf16[32,3712]{1,0:T(8,128)(2,1)S(1)} %get-tuple-element.155.mine, bf16[32,3712]{1,0:T(8,128)(2,1)S(1)} %collective-permute-done.2.theirs, bf16[8,2,2,2,16,256]{5,4,3,2,1,0:T(8,128)(2,1)S(1)} %get-tuple-element.105.refs_0_, ...), custom_call_target="tpu_custom_call" | custom-call | flops 2000000000 | bytes 1000 | tf_op jit(solution)/shard_map/pallas_call | solution.py:280
  134.7 6.2 %collective-permute-done.23.b4 = bf16[32,3712]{1,0:T(8,128)(2,1)S(1)} collective-permute-done((bf16[32,3712]{1,0:T(8,128)(2,1)S(1)}, bf16[32,3712]{1,0:T(8,128)(2,1)S(1)}, u32[]{:S(2)}, u32[]{:S(2)}) %collective-permute-start.23) | collective-permute-done | bytes 237600 | tf_op jit(solution)/shard_map/ppermute | solution.py:39
  142.3 4.8 %collective-permute-start.26 = (bf16[32,3712]{1,0:T(8,128)(2,1)S(1)}, bf16[32,3712]{1,0:T(8,128)(2,1)S(1)}, u32[]{:S(2)}, u32[]{:S(2)}) collective-permute-start(bf16[32,3712]{1,0:T(8,128)(2,1)S(1)} %get-tuple-element.164), channel_id=1, source_target_pairs={{0,24},{1,25},{2,26},{3,27},{4,28},{5,29},{6,30},{7,31},{8,0},{9,1... | collective-permute-start | bytes 712712 | tf_op jit(solution)/shard_map/ppermute | solution.py:39
  147.1 8.3 %collective-permute-done.26.b2 = bf16[32,3712]{1,0:T(8,128)(2,1)S(1)} collective-permute-done((bf16[32,3712]{1,0:T(8,128)(2,1)S(1)}, bf16[32,3712]{1,0:T(8,128)(2,1)S(1)}, u32[]{:S(2)}, u32[]{:S(2)}) %collective-permute-start.26) | collective-permute-done | bytes 237600 | tf_op jit(solution)/shard_map/ppermute | solution.py:39
  155.3 4.3 %collective-permute-done.27.b6 = bf16[32,3712]{1,0:T(8,128)(2,1)S(1)} collective-permute-done((bf16[32,3712]{1,0:T(8,128)(2,1)S(1)}, bf16[32,3712]{1,0:T(8,128)(2,1)S(1)}, u32[]{:S(2)}, u32[]{:S(2)}) %collective-permute-start.27) | collective-permute-done | bytes 237600 | tf_op jit(solution)/shard_map/ppermute | solution.py:39
  159.6 3.5 %shard_map.115 = bf16[2,64,3584]{2,1,0:T(8,128)(2,1)} custom-call(f32[32,3712]{1,0:T(8,128)S(1)} %get-tuple-element.159.own, bf16[32,3712]{1,0:T(8,128)(2,1)S(1)} %collective-permute-done.25.got, bf16[32,3712]{1,0:T(8,128)(2,1)S(1)} %collective-permute-done.15.b1, bf16[32,3712]{1,0:T(8,128)(2,1)S(1)} %collective-permute-done.26.b2, ...), custom_call_target="tpu_custom_call" | custom-call | flops 100000 | bytes 1000 | tf_op jit(solution)/shard_map/pallas_call | solution.py:348
  (72 shorter events, 39.4 us)
Async XLA Ops:
  2.3 17.5 %collective-permute-start = (bf16[64,3584]{1,0:T(8,128)(2,1)}, bf16[64,3584]{1,0:T(8,128)(2,1)S(1)}, u32[]{:S(2)}, u32[]{:S(2)}) collective-permute-start(bf16[64,3584]{1,0:T(8,128)(2,1)} %get-tuple-element.89), channel_id=1, source_target_pairs={{0,224},{32,0},{64,32},{96,64},{128,96},{160,128},{192,160},{224,1... | collective-permute-start | bytes 1376264 | tf_op jit(solution)/shard_map/ppermute | solution.py:34
  7.8 15.9 %collective-permute-start.1 = (bf16[64,3584]{1,0:T(8,128)(2,1)}, bf16[64,3584]{1,0:T(8,128)(2,1)}, u32[]{:S(2)}, u32[]{:S(2)}) collective-permute-start(bf16[64,3584]{1,0:T(8,128)(2,1)} %get-tuple-element.90), channel_id=1, source_target_pairs={{0,32},{32,64},{64,96},{96,128},{128,160},{160,192},{192,224},{224... | collective-permute-start | bytes 1376264 | tf_op jit(solution)/shard_map/ppermute | solution.py:34
  23.7 24.3 %collective-permute-start.9 = (bf16[768,3584]{1,0:T(8,128)(2,1)}, bf16[768,3584]{1,0:T(8,128)(2,1)S(1)}, u32[]{:S(2)}, u32[]{:S(2)}) collective-permute-start(bf16[768,3584]{1,0:T(8,128)(2,1)} %copy-done), channel_id=1, source_target_pairs={{0,1},{1,0},{2,3},{3,2},{4,5},{5,4},{6,7},{7,6},{8,9},{9,8},{10,11... | collective-permute-start | bytes 16515080 | tf_op jit(solution)/shard_map/ppermute | solution.py:47
  28.1 14.8 %collective-permute-start.8 = (bf16[8,2,2,2,16,256]{5,4,3,2,1,0:T(8,128)(2,1)S(1)}, bf16[8,2,2,2,16,256]{5,4,3,2,1,0:T(8,128)(2,1)S(1)}, u32[]{:S(2)}, u32[]{:S(2)}) collective-permute-start(bf16[8,2,2,2,16,256]{5,4,3,2,1,0:T(8,128)(2,1)S(1)} %get-tuple-element.106), channel_id=1, source_target_pairs={{0,1},{1,0},{2,3},{3,2},{4,5},{5,4},{6,7},{7,6},{8,9},{9,8},{10,11... | collective-permute-start | bytes 1572872 | tf_op jit(solution)/shard_map/ppermute | solution.py:47
  35.5 12.5 %collective-permute-start.7 = (bf16[64,3712]{1,0:T(8,128)(2,1)S(1)}, bf16[64,3712]{1,0:T(8,128)(2,1)S(1)}, u32[]{:S(2)}, u32[]{:S(2)}) collective-permute-start(bf16[64,3712]{1,0:T(8,128)(2,1)S(1)} %shard_map.103.mine), channel_id=1, source_target_pairs={{0,2},{1,3},{2,0},{3,1},{4,6},{5,7},{6,4},{7,5},{8,10},{9,11},{10,... | collective-permute-start | bytes 1425416 | tf_op jit(solution)/shard_map/ppermute | solution.py:43
  36.2 21.0 %collective-permute-start.5 = (bf16[32,3712]{1,0:T(8,128)(2,1)S(1)}, bf16[32,3712]{1,0:T(8,128)(2,1)S(1)}, u32[]{:S(2)}, u32[]{:S(2)}) collective-permute-start(bf16[32,3712]{1,0:T(8,128)(2,1)S(1)} %get-tuple-element.101), channel_id=1, source_target_pairs={{0,12},{1,13},{2,14},{3,15},{4,16},{5,17},{6,18},{7,19},{8,20},{9,... | collective-permute-start | bytes 712712 | tf_op jit(solution)/shard_map/ppermute | solution.py:39
  42.9 19.1 %collective-permute-start.6 = (bf16[32,3712]{1,0:T(8,128)(2,1)S(1)}, bf16[32,3712]{1,0:T(8,128)(2,1)S(1)}, u32[]{:S(2)}, u32[]{:S(2)}) collective-permute-start(bf16[32,3712]{1,0:T(8,128)(2,1)S(1)} %get-tuple-element.102), channel_id=1, source_target_pairs={{0,20},{1,21},{2,22},{3,23},{4,24},{5,25},{6,26},{7,27},{8,28},{9,... | collective-permute-start | bytes 712712 | tf_op jit(solution)/shard_map/ppermute | solution.py:39
  62.0 13.9 %collective-permute-start.11 = (bf16[64,3712]{1,0:T(8,128)(2,1)S(1)}, bf16[64,3712]{1,0:T(8,128)(2,1)S(1)}, u32[]{:S(2)}, u32[]{:S(2)}) collective-permute-start(bf16[64,3712]{1,0:T(8,128)(2,1)S(1)} %shard_map.105.mine), channel_id=1, source_target_pairs={{0,2},{1,3},{2,0},{3,1},{4,6},{5,7},{6,4},{7,5},{8,10},{9,11},{10,... | collective-permute-start | bytes 1425416 | tf_op jit(solution)/shard_map/ppermute | solution.py:43
  63.6 21.6 %collective-permute-start.10 = (bf16[64,3712]{1,0:T(8,128)(2,1)S(1)}, bf16[64,3712]{1,0:T(8,128)(2,1)S(1)}, u32[]{:S(2)}, u32[]{:S(2)}) collective-permute-start(bf16[64,3712]{1,0:T(8,128)(2,1)S(1)} %get-tuple-element.115), channel_id=1, source_target_pairs={{0,2},{1,3},{2,0},{3,1},{4,6},{5,7},{6,4},{7,5},{8,10},{9,11},{10,... | collective-permute-start | bytes 1425416 | tf_op jit(solution)/shard_map/ppermute | solution.py:43
  64.1 14.8 %collective-permute-start.12 = (bf16[32,3712]{1,0:T(8,128)(2,1)S(1)}, bf16[32,3712]{1,0:T(8,128)(2,1)S(1)}, u32[]{:S(2)}, u32[]{:S(2)}) collective-permute-start(bf16[32,3712]{1,0:T(8,128)(2,1)S(1)} %get-tuple-element.121), channel_id=1, source_target_pairs={{0,16},{1,17},{2,18},{3,19},{4,20},{5,21},{6,22},{7,23},{8,24},{9,... | collective-permute-start | bytes 712712 | tf_op jit(solution)/shard_map/ppermute | solution.py:39
  65.5 19.6 %collective-permute-start.13 = (bf16[32,3712]{1,0:T(8,128)(2,1)S(1)}, bf16[32,3712]{1,0:T(8,128)(2,1)S(1)}, u32[]{:S(2)}, u32[]{:S(2)}) collective-permute-start(bf16[32,3712]{1,0:T(8,128)(2,1)S(1)} %get-tuple-element.122), channel_id=1, source_target_pairs={{0,8},{1,9},{2,10},{3,11},{4,12},{5,13},{6,14},{7,15},{8,16},{9,17... | collective-permute-start | bytes 712712 | tf_op jit(solution)/shard_map/ppermute | solution.py:39
  67.1 18.0 %collective-permute-start.14 = (bf16[32,3712]{1,0:T(8,128)(2,1)S(1)}, bf16[32,3712]{1,0:T(8,128)(2,1)S(1)}, u32[]{:S(2)}, u32[]{:S(2)}) collective-permute-start(bf16[32,3712]{1,0:T(8,128)(2,1)S(1)} %get-tuple-element.123), channel_id=1, source_target_pairs={{0,24},{1,25},{2,26},{3,27},{4,28},{5,29},{6,30},{7,31},{8,0},{9,1... | collective-permute-start | bytes 712712 | tf_op jit(solution)/shard_map/ppermute | solution.py:39
  85.1 20.2 %collective-permute-start.18 = (bf16[64,3712]{1,0:T(8,128)(2,1)S(1)}, bf16[64,3712]{1,0:T(8,128)(2,1)S(1)}, u32[]{:S(2)}, u32[]{:S(2)}) collective-permute-start(bf16[64,3712]{1,0:T(8,128)(2,1)S(1)} %get-tuple-element.133), channel_id=1, source_target_pairs={{0,2},{1,3},{2,0},{3,1},{4,6},{5,7},{6,4},{7,5},{8,10},{9,11},{10,... | collective-permute-start | bytes 1425416 | tf_op jit(solution)/shard_map/ppermute | solution.py:43
  86.5 15.7 %collective-permute-start.17 = (bf16[32,3712]{1,0:T(8,128)(2,1)S(1)}, bf16[32,3712]{1,0:T(8,128)(2,1)S(1)}, u32[]{:S(2)}, u32[]{:S(2)}) collective-permute-start(bf16[32,3712]{1,0:T(8,128)(2,1)S(1)} %collective-permute-done.12.mine), channel_id=1, source_target_pairs={{0,2},{1,3},{2,0},{3,1},{4,6},{5,7},{6,4},{7,5},{8,10},{9,11},{10,... | collective-permute-start | bytes 712712 | tf_op jit(solution)/shard_map/ppermute | solution.py:43
  87.3 18.0 %collective-permute-start.15 = (bf16[32,3712]{1,0:T(8,128)(2,1)S(1)}, bf16[32,3712]{1,0:T(8,128)(2,1)S(1)}, u32[]{:S(2)}, u32[]{:S(2)}) collective-permute-start(bf16[32,3712]{1,0:T(8,128)(2,1)S(1)} %get-tuple-element.128), channel_id=1, source_target_pairs={{0,28},{1,29},{2,30},{3,31},{4,0},{5,1},{6,2},{7,3},{8,4},{9,5},{1... | collective-permute-start | bytes 712712 | tf_op jit(solution)/shard_map/ppermute | solution.py:39
  87.7 17.6 %collective-permute-start.16 = (bf16[32,3712]{1,0:T(8,128)(2,1)S(1)}, bf16[32,3712]{1,0:T(8,128)(2,1)S(1)}, u32[]{:S(2)}, u32[]{:S(2)}) collective-permute-start(bf16[32,3712]{1,0:T(8,128)(2,1)S(1)} %get-tuple-element.129), channel_id=1, source_target_pairs={{0,4},{1,5},{2,6},{3,7},{4,8},{5,9},{6,10},{7,11},{8,12},{9,13},{1... | collective-permute-start | bytes 712712 | tf_op jit(solution)/shard_map/ppermute | solution.py:39
  105.4 13.7 %collective-permute-start.21 = (bf16[64,3712]{1,0:T(8,128)(2,1)S(1)}, bf16[64,3712]{1,0:T(8,128)(2,1)S(1)}, u32[]{:S(2)}, u32[]{:S(2)}) collective-permute-start(bf16[64,3712]{1,0:T(8,128)(2,1)S(1)} %shard_map.110.mine), channel_id=1, source_target_pairs={{0,2},{1,3},{2,0},{3,1},{4,6},{5,7},{6,4},{7,5},{8,10},{9,11},{10,... | collective-permute-start | bytes 1425416 | tf_op jit(solution)/shard_map/ppermute | solution.py:43
  107.0 16.9 %collective-permute-start.19 = (bf16[32,3712]{1,0:T(8,128)(2,1)S(1)}, bf16[32,3712]{1,0:T(8,128)(2,1)S(1)}, u32[]{:S(2)}, u32[]{:S(2)}) collective-permute-start(bf16[32,3712]{1,0:T(8,128)(2,1)S(1)} %get-tuple-element.141), channel_id=1, source_target_pairs={{0,20},{1,21},{2,22},{3,23},{4,24},{5,25},{6,26},{7,27},{8,28},{9,... | collective-permute-start | bytes 712712 | tf_op jit(solution)/shard_map/ppermute | solution.py:39
  110.9 14.1 %collective-permute-start.20 = (bf16[32,3712]{1,0:T(8,128)(2,1)S(1)}, bf16[32,3712]{1,0:T(8,128)(2,1)S(1)}, u32[]{:S(2)}, u32[]{:S(2)}) collective-permute-start(bf16[32,3712]{1,0:T(8,128)(2,1)S(1)} %get-tuple-element.142), channel_id=1, source_target_pairs={{0,12},{1,13},{2,14},{3,15},{4,16},{5,17},{6,18},{7,19},{8,20},{9,... | collective-permute-start | bytes 712712 | tf_op jit(solution)/shard_map/ppermute | solution.py:39
  112.3 12.7 %collective-permute-start.22 = (bf16[32,3712]{1,0:T(8,128)(2,1)S(1)}, bf16[32,3712]{1,0:T(8,128)(2,1)S(1)}, u32[]{:S(2)}, u32[]{:S(2)}) collective-permute-start(bf16[32,3712]{1,0:T(8,128)(2,1)S(1)} %get-tuple-element.147), channel_id=1, source_target_pairs={{0,2},{1,3},{2,0},{3,1},{4,6},{5,7},{6,4},{7,5},{8,10},{9,11},{10,... | collective-permute-start | bytes 712712 | tf_op jit(solution)/shard_map/ppermute | solution.py:43
  125.0 15.9 %collective-permute-start.24 = (bf16[64,3712]{1,0:T(8,128)(2,1)S(1)}, bf16[64,3712]{1,0:T(8,128)(2,1)S(1)}, u32[]{:S(2)}, u32[]{:S(2)}) collective-permute-start(bf16[64,3712]{1,0:T(8,128)(2,1)S(1)} %get-tuple-element.153), channel_id=1, source_target_pairs={{0,2},{1,3},{2,0},{3,1},{4,6},{5,7},{6,4},{7,5},{8,10},{9,11},{10,... | collective-permute-start | bytes 1425416 | tf_op jit(solution)/shard_map/ppermute | solution.py:43
  125.6 15.3 %collective-permute-start.23 = (bf16[32,3712]{1,0:T(8,128)(2,1)S(1)}, bf16[32,3712]{1,0:T(8,128)(2,1)S(1)}, u32[]{:S(2)}, u32[]{:S(2)}) collective-permute-start(bf16[32,3712]{1,0:T(8,128)(2,1)S(1)} %shard_map.112), channel_id=1, source_target_pairs={{0,16},{1,17},{2,18},{3,19},{4,20},{5,21},{6,22},{7,23},{8,24},{9,... | collective-permute-start | bytes 712712 | tf_op jit(solution)/shard_map/ppermute | solution.py:39
  142.3 13.0 %collective-permute-start.26 = (bf16[32,3712]{1,0:T(8,128)(2,1)S(1)}, bf16[32,3712]{1,0:T(8,128)(2,1)S(1)}, u32[]{:S(2)}, u32[]{:S(2)}) collective-permute-start(bf16[32,3712]{1,0:T(8,128)(2,1)S(1)} %get-tuple-element.164), channel_id=1, source_target_pairs={{0,24},{1,25},{2,26},{3,27},{4,28},{5,29},{6,30},{7,31},{8,0},{9,1... | collective-permute-start | bytes 712712 | tf_op jit(solution)/shard_map/ppermute | solution.py:39
  147.1 12.5 %collective-permute-start.27 = (bf16[32,3712]{1,0:T(8,128)(2,1)S(1)}, bf16[32,3712]{1,0:T(8,128)(2,1)S(1)}, u32[]{:S(2)}, u32[]{:S(2)}) collective-permute-start(bf16[32,3712]{1,0:T(8,128)(2,1)S(1)} %get-tuple-element.168), channel_id=1, source_target_pairs={{0,8},{1,9},{2,10},{3,11},{4,12},{5,13},{6,14},{7,15},{8,16},{9,17... | collective-permute-start | bytes 712712 | tf_op jit(solution)/shard_map/ppermute | solution.py:39
  (14 other events, 92.3 us)
where the time goes:
time: 163 us
  waiting for transfers between devices  79.9 us (49%)
  starting transfers between devices  47.5 us (29%)
  Pallas kernels  24.8 us (15%)
  local copies, waits for them, and re-layouts  10.6 us (7%)
    ppermute x14, waiting for transfers between devices, z_shift(): return lax.ppermute(value, 'expert', pairs)  46 us
    ppermute x14, starting transfers between devices, z_shift(): return lax.ppermute(value, 'expert', pairs)  32.7 us
    ppermute x10, waiting for transfers between devices, x_swap(): return lax.ppermute(value, 'expert', [(i, i ^ 2) for i in range(32)])  30 us
    pallas_call x5, Pallas kernels, work(): pl.pallas_call(functools.partial(unit_kernel, group), out_shape=(shape((U...  15.4 us
    ppermute x10, starting transfers between devices, x_swap(): return lax.ppermute(value, 'expert', [(i, i ^ 2) for i in range(32)])  9.35 us
    ppermute x2, starting transfers between devices, pipe_shift(): return lax.ppermute(value, 'pipe', [(i, (i + by) % 8) for i in range(8)])  5.48 us
    unnamed x20, local copies, waits for them, and re-layouts  5.43 us
    ppermute x2, waiting for transfers between devices, pipe_shift(): return lax.ppermute(value, 'pipe', [(i, (i + by) % 8) for i in range(8)])  3.84 us
  transfers between devices with their start and end apart: 28, of which 15 were waited for; matrix products, arithmetic and copies ran while one was open for 2% of the time, Pallas kernels for 13%

commit v1 on v0

--- a/solution.py
+++ b/solution.py
@@ -24,7 +24,7 @@
 TN = (((0,), (0,)), ((), ()))
 COST = 100_000
 WORK = 2_000_000_000
-LIMIT = 24 * 1024 * 1024
+LIMIT = 16 * 1024 * 1024
 
 VMEM = pl.BlockSpec(memory_space=pltpu.VMEM)
 SMEM = pl.BlockSpec(memory_space=pltpu.SMEM)
@@ -108,17 +108,17 @@
             match[m, k] = hit
             share = (ROUTE_SCALE * chosen[k] / totals).astype(BF16).astype(F32)
             column = column + jnp.sum(hit * share, axis=-1, keepdims=True)
-        weight[m] = jnp.broadcast_to(column, (SLOTS, 128)).astype(BF16)
+        weight[m] = column
 
 
 def spread_kernel(first, second, match, weight, kept, *outs):
     for m, rows in enumerate((first, second)):
         kept[m] = rows[...]
         both = (match[m, 0] + match[m, 1]).astype(BF16)
-        filled = jnp.dot(both, rows[...], preferred_element_type=F32).astype(BF16)
+        filled = jnp.dot(both, rows[...], preferred_element_type=F32)
+        filled = (filled * weight[m]).astype(BF16)
         for k in range(EXPERTS):
-            outs[k][m * CAP : (m + 1) * CAP, :D] = filled[k * CAP : (k + 1) * CAP]
-            outs[k][m * CAP : (m + 1) * CAP, D:] = weight[m, k * CAP : (k + 1) * CAP]
+            outs[k][m * CAP : (m + 1) * CAP] = filled[k * CAP : (k + 1) * CAP]
 
 
 def stage_kernel(w_down, w_gate, w_up, packed):
@@ -143,7 +143,6 @@
     half = size // 2
     rows[:half] = mine[...]
     rows[half:] = theirs[...]
-    weight = rows[:, D:].astype(F32)[:, :1]
     total = jnp.zeros((size, 1), F32)
     grads = []
     for s in range(2):
@@ -157,14 +156,13 @@
         gate = jnp.concatenate(parts[0], axis=0).astype(F32)
         up = jnp.concatenate(parts[1], axis=0).astype(F32)
         projected = lax.dot_general(
-            rows[:, :D], weights[s][:SLICE], NT, preferred_element_type=F32
+            rows[...], weights[s][:SLICE], NT, preferred_element_type=F32
         )
         sig = jax.nn.sigmoid(gate)
         act = gate * sig
         total = total + jnp.sum(projected * (act * up), axis=-1, keepdims=True)
-        grad = weight * projected
-        gate_grad = (grad * up * sig * (1.0 + gate * (1.0 - sig))).astype(BF16)
-        grads.append(jnp.concatenate([gate_grad, (grad * act).astype(BF16)], axis=1))
+        gate_grad = (projected * up * sig * (1.0 + gate * (1.0 - sig))).astype(BF16)
+        grads.append(jnp.concatenate([gate_grad, (projected * act).astype(BF16)], axis=1))
     step = 512
     for at in range(0, D, step):
         part = jnp.dot(grads[0], weights[0][SLICE:, at : at + step], preferred_element_type=F32)
@@ -187,48 +185,86 @@
         out[:, D:] = lanes(high, low, (UNIT, 128)).astype(BF16)
 
 
-def finish_kernel(
-    own, got, b1, b2, b3, b4, b5, b6, b7, kept, saved, routes, match, scores, inv,
-    gain, router, out, back,
-):
-    units = (None, b1, b2, b3, b4, b5, b6, b7)
-    names = lax.broadcasted_iota(jnp.int32, (EXPERTS, TOKENS), 0)
+def add_two_kernel(own, got, own_next, got_next, low, high, last):
+    add_kernel(own, got, low, high)
+    add_kernel(own_next, got_next, last)
+
+
+def gather_kernel(own, got, b1, b7, b4, b3, b5, match, total, slot_dw, back):
+    units = {1: b1, 7: b7, 4: b4, 3: b3, 5: b5}
     for m in range(2):
         at = slice(m * CAP, (m + 1) * CAP)
         back[:CAP] = (own[at, :D] + got[at, :D].astype(F32)).astype(BF16)
         dws = [own[at, D:] + got[at, D:].astype(F32)]
         for k in range(1, EXPERTS):
-            back[k * CAP : (k + 1) * CAP] = units[k][at, :D]
-            dws.append(units[k][at, D:].astype(F32))
-        slot_dw = jnp.sum(jnp.concatenate(dws, axis=0), axis=-1, keepdims=True)
-        score = scores[m]
-        chosen, choice = [], []
-        for k in range(2):
-            mine = routes[m, k : k + 1, :] == names
-            chosen.append(jnp.sum(jnp.where(mine, score, 0.0), axis=0, keepdims=True))
-            choice.append(jnp.sum(match[m, k] * slot_dw, axis=0, keepdims=True))
-        totals = chosen[0] + chosen[1]
-        inner = (choice[0] * chosen[0] + choice[1] * chosen[1]) / (totals * totals)
-        score_grad = jnp.zeros((EXPERTS, TOKENS), F32)
-        for k in range(2):
-            mine = routes[m, k : k + 1, :] == names
-            slope = ROUTE_SCALE * (choice[k] / totals - inner)
-            score_grad = score_grad + jnp.where(mine, slope, 0.0)
-        score_grad = score_grad * score * (1.0 - score)
+            rows = slice(k * CAP, (k + 1) * CAP)
+            if k in units:
+                back[rows] = units[k][at, :D]
+                dws.append(units[k][at, D:].astype(F32))
+            else:
+                back[rows] = jnp.zeros((CAP, D), BF16)
+                dws.append(jnp.zeros((CAP, 128), F32))
+        slot_dw[m] = jnp.sum(jnp.concatenate(dws, axis=0), axis=-1, keepdims=True)
         both = (match[m, 0] + match[m, 1]).astype(BF16)
-        total = lax.dot_general(both, back[...], TN, preferred_element_type=F32)
-        total = total + lax.dot_general(
-            score_grad, router[...], TN, precision=HIGHEST, preferred_element_type=F32
+        total[m] = lax.dot_general(both, back[...], TN, preferred_element_type=F32)
+
+
+def finish_kernel(
+    b2, b6, some, some_dw, kept, saved, routes, match, weight, scores, inv, gain, router, out, back
+):
+    names = lax.broadcasted_iota(jnp.int32, (EXPERTS, TOKENS), 0)
+    low, high = slice(2 * CAP, 3 * CAP), slice(6 * CAP, 7 * CAP)
+    for m in range(2):
+        finish_part(
+            m, b2, b6, some, some_dw, kept, saved, routes, match, weight, scores, inv, gain,
+            router, out, back, names, low, high,
         )
-        scaled = gain[...] * total
-        values = saved[m].astype(F32)
-        inv_rms = inv[m]
-        mean = jnp.mean(values * scaled, axis=-1, keepdims=True)
-        out[m] = (
-            kept[m].astype(F32)
-            + inv_rms * scaled
-            - (inv_rms * inv_rms * inv_rms * mean) * values
-        ).astype(BF16)
+
+
+def finish_part(
+    m, b2, b6, some, some_dw, kept, saved, routes, match, weight, scores, inv, gain, router, out,
+    back, names, low, high,
+):
+    at = slice(m * CAP, (m + 1) * CAP)
+    back[:CAP] = b2[at, :D]
+    back[CAP:] = b6[at, :D]
+    late = [jnp.sum(unit[at, D:].astype(F32), axis=-1, keepdims=True) for unit in (b2, b6)]
+    slot_dw = some_dw[m]
+    slot_dw = jnp.concatenate(
+        [slot_dw[: low.start], late[0], slot_dw[low.stop : high.start], late[1], slot_dw[high.stop :]],
+        axis=0,
+    )
+    share = weight[m]
+    used = share > 0.0
+    slot_dw = jnp.where(used, slot_dw / jnp.where(used, share, 1.0), 0.0)
+    score = scores[m]
+    chosen, choice, picked = [], [], []
+    for k in range(2):
+        picked.append(routes[m, k : k + 1, :] == names)
+        chosen.append(jnp.sum(jnp.where(picked[k], score, 0.0), axis=0, keepdims=True))
+        choice.append(jnp.sum(match[m, k] * slot_dw, axis=0, keepdims=True))
+    totals = chosen[0] + chosen[1]
+    inner = (choice[0] * chosen[0] + choice[1] * chosen[1]) / (totals * totals)
+    score_grad = jnp.zeros((EXPERTS, TOKENS), F32)
+    for k in range(2):
+        slope = ROUTE_SCALE * (choice[k] / totals - inner)
+        score_grad = score_grad + jnp.where(picked[k], slope, 0.0)
+    score_grad = score_grad * score * (1.0 - score)
+    both = (match[m, 0] + match[m, 1]).astype(BF16)
+    both = jnp.concatenate([both[low], both[high]], axis=0)
+    total = some[m] + lax.dot_general(both, back[...], TN, preferred_element_type=F32)
+    total = total + lax.dot_general(
+        score_grad, router[...], TN, precision=HIGHEST, preferred_element_type=F32
+    )
+    scaled = gain[...] * total
+    values = saved[m].astype(F32)
+    inv_rms = inv[m]
+    mean = jnp.mean(values * scaled, axis=-1, keepdims=True)
+    out[m] = (
+        kept[m].astype(F32)
+        + inv_rms * scaled
+        - (inv_rms * inv_rms * inv_rms * mean) * values
+    ).astype(BF16)
 
 
 def shape(dims, dtype=BF16):
@@ -254,7 +290,7 @@
         prep_kernel,
         (
             shape((2, 2, SLOTS, TOKENS), F32),
-            shape((2, SLOTS, 128)),
+            shape((2, SLOTS, 1), F32),
             shape((2, EXPERTS, TOKENS), F32),
             shape((2, TOKENS, 1), F32),
         ),
@@ -270,7 +306,7 @@
     pre_other, weights = core_swap(pre_other), (packed, core_swap(packed))
     kept, *units = call(
         spread_kernel,
-        (shape((2, TOKENS, D)),) + tuple(shape((UNIT, WIDE)) for _ in range(EXPERTS)),
+        (shape((2, TOKENS, D)),) + tuple(shape((UNIT, D)) for _ in range(EXPERTS)),
         [VMEM] * 4,
         COST,
         1000,
@@ -282,7 +318,7 @@
             out_shape=(shape((UNIT * n, WIDE), F32), shape((UNIT * n, WIDE))),
             in_specs=[SMEM] + [VMEM] * 6,
             out_specs=(VMEM, VMEM),
-            scratch_shapes=[pltpu.VMEM((2 * UNIT * n, WIDE), BF16)],
+            scratch_shapes=[pltpu.VMEM((2 * UNIT * n, D), BF16)],
             cost_estimate=pl.CostEstimate(flops=WORK, bytes_accessed=1000, transcendentals=0),
             compiler_params=pltpu.CompilerParams(vmem_limit_bytes=LIMIT),
         )(place, mine, theirs, pre_own, pre_other, *weights)
@@ -293,12 +329,11 @@
         )
 
     def pack(low, high):
-        return call(pack_kernel, shape((2 * UNIT, WIDE)), [VMEM] * 2, COST, 1000)(low, high)
+        return call(pack_kernel, shape((2 * UNIT, D)), [VMEM] * 2, COST, 1000)(low, high)
 
     v = {"u%d" % k: units[k] for k in range(EXPERTS)}
 
-    def tie(names):
-        names = names.split()
+    def tie(*names):
         v.update(zip(names, lax.optimization_barrier(tuple(v[n] for n in names))))
 
     def z_out(*shifts):
@@ -309,59 +344,69 @@
         for k in shifts:
             v["b%d" % k] = z_shift(v["d%d" % k], -k)
 
+    z_out(1, 7)
     v["t0"] = x_swap(v["u0"])
-    z_out(1, 7)
-    tie("t0 u0 m1 m7 u3 u5")
-    z_out(3, 5)
+    tie("t0", "u0", "m1", "m7", "u4", "u3", "u5", "u2", "u6")
+    z_out(4)
     v["p1"] = pack(v["m1"], v["m7"])
     v["t1"] = x_swap(v["p1"])
     v["own1"], v["away1"] = work((1, 7), v["p1"], v["t1"])
-    tie("m3 m5 own1 away1 u2 u6 u4 t0 u0")
-    z_out(4, 2, 6)
+    tie("m4", "own1", "away1", "t0", "u0", "u3", "u5", "u2", "u6")
+    z_out(3, 5)
+    v["t4"] = x_swap(v["m4"])
+    v["got1"] = x_swap(v["away1"])
+    v["own4"], v["away4"] = work((4,), v["m4"], v["t4"])
+    tie("got1", "own1", "own4", "away4", "m3", "m5", "t0", "u0", "u2", "u6")
+    z_out(2, 6)
     v["p3"] = pack(v["m3"], v["m5"])
     v["t3"] = x_swap(v["p3"])
-    v["got1"] = x_swap(v["away1"])
+    v["got4"] = x_swap(v["away4"])
     v["own3"], v["away3"] = work((3, 5), v["p3"], v["t3"])
-    tie("got1 own1 own3 away3 m4 m2 m6 t0 u0")
-    v["d1"], v["d7"] = add((1, 7), v["own1"], v["got1"])
-    z_back(1, 7)
-    v["t4"] = x_swap(v["m4"])
+    tie("own3", "away3", "m2", "m6", "got4", "own4", "got1", "own1", "t0", "u0")
+    v["d1"], v["d7"], v["d4"] = call(
+        add_two_kernel, tuple(shape((UNIT, WIDE)) for _ in range(3)), [VMEM] * 4, COST, 1000
+    )(v["own1"], v["got1"], v["own4"], v["got4"])
+    z_back(1, 7, 4)
+    v["p2"] = pack(v["m2"], v["m6"])
+    v["t2"] = x_swap(v["p2"])
     v["got3"] = x_swap(v["away3"])
-    v["own4"], v["away4"] = work((4,), v["m4"], v["t4"])
-    tie("b1 b7 own4 away4 got3 own3 m2 m6 t0 u0")
+    v["own2"], v["away2"] = work((2, 6), v["p2"], v["t2"])
+    v["own0"], v["away0"] = work((0,), v["u0"], v["t0"])
+    tie("b1", "b7", "b4", "got3", "own3", "own2", "away2", "own0", "away0")
     v["d3"], v["d5"] = add((3, 5), v["own3"], v["got3"])
     z_back(3, 5)
-    v["p2"] = pack(v["m2"], v["m6"])
-    v["t2"] = x_swap(v["p2"])
-    v["got4"] = x_swap(v["away4"])
-    v["own2"], v["away2"] = work((2, 6), v["p2"], v["t2"])
-    tie("b3 b5 own2 away2 got4 own4 t0 u0")
-    (v["d4"],) = add((4,), v["own4"], v["got4"])
-    z_back(4)
     v["got2"] = x_swap(v["away2"])
-    v["own0"], v["away0"] = work((0,), v["u0"], v["t0"])
-    tie("b4 got2 own2 own0 away0")
     v["got0"] = x_swap(v["away0"])
+    tie("b3", "b5", "got2", "own2", "got0", "own0")
     v["d2"], v["d6"] = add((2, 6), v["own2"], v["got2"])
     z_back(2, 6)
-    back = [(v["own0"], v["got0"])] + [v["b%d" % k] for k in range(1, EXPERTS)]
+    some, some_dw = pl.pallas_call(
+        gather_kernel,
+        out_shape=(shape((2, TOKENS, D), F32), shape((2, SLOTS, 1), F32)),
+        in_specs=[VMEM] * 8,
+        out_specs=(VMEM, VMEM),
+        scratch_shapes=[pltpu.VMEM((SLOTS, D), BF16)],
+        cost_estimate=pl.CostEstimate(flops=COST, bytes_accessed=1000, transcendentals=0),
+        compiler_params=pltpu.CompilerParams(vmem_limit_bytes=LIMIT),
+    )(v["own0"], v["got0"], v["b1"], v["b7"], v["b4"], v["b3"], v["b5"], match)
     out = pl.pallas_call(
         finish_kernel,
         out_shape=shape((2, TOKENS, D)),
-        in_specs=[VMEM] * 17,
+        in_specs=[VMEM] * 13,
         out_specs=VMEM,
-        scratch_shapes=[pltpu.VMEM((SLOTS, D), BF16)],
-        cost_estimate=pl.CostEstimate(
-            flops=COST, bytes_accessed=1000, transcendentals=0
-        ),
+        scratch_shapes=[pltpu.VMEM((2 * CAP, D), BF16)],
+        cost_estimate=pl.CostEstimate(flops=COST, bytes_accessed=1000, transcendentals=0),
         compiler_params=pltpu.CompilerParams(vmem_limit_bytes=LIMIT),
     )(
-        *back[0],
-        *back[1:],
+        v["b2"],
+        v["b6"],
+        some,
+        some_dw,
         kept,
         saved_in[0],
         routes_t,
         match,
+        weight,
         scores,
         inv,
         norm_gain,

time: 163 us -> 154 us (0.945); the launches traced: 163 us -> 151 us
  waiting for transfers between devices: 79.9 us -> 67.1 us
    ppermute x14, waiting for transfers between devices: 46 us -> 38.2 us  [z_shift(): return lax.ppermute(value, 'expert', pairs)]
    ppermute x10, waiting for transfers between devices: 30 us -> 25 us  [x_swap(): return lax.ppermute(value, 'expert', [(i, i ^ 2) for i in range(32)])]
    pallas_call x5 -> x7, Pallas kernels: 4.34 us -> 4.99 us  [the longest x1 2.54 us: local(): call(prep_kernel, (shape((2, 2, SLOTS, TOKENS), F32), shape((2, SLOTS, 1)...]
  transfers between devices with their start and end apart: 28 -> 28, of which waited for: 15 -> 15; matrix products, arithmetic and copies ran while one was open for 2% -> 2% of each run, Pallas kernels for 13% -> 14%
where the time goes in v1:
time: 154 us; the launch traced here: 151 us
  waiting for transfers between devices  67.1 us (44%)
  starting transfers between devices  48.2 us (31%)
  Pallas kernels  25 us (16%)
  local copies, waits for them, and re-layouts  10.6 us (7%)
    ppermute x14, waiting for transfers between devices, z_shift(): return lax.ppermute(value, 'expert', pairs)  38.2 us
    ppermute x14, starting transfers between devices, z_shift(): return lax.ppermute(value, 'expert', pairs)  32.9 us
    ppermute x10, waiting for transfers between devices, x_swap(): return lax.ppermute(value, 'expert', [(i, i ^ 2) for i in range(32)])  25 us
    pallas_call x5, Pallas kernels, work(): pl.pallas_call(functools.partial(unit_kernel, group), out_shape=(shape((U...  15.2 us
    ppermute x10, starting transfers between devices, x_swap(): return lax.ppermute(value, 'expert', [(i, i ^ 2) for i in range(32)])  9.81 us
    ppermute x2, starting transfers between devices, pipe_shift(): return lax.ppermute(value, 'pipe', [(i, (i + by) % 8) for i in range(8)])  5.48 us
    unnamed x20, local copies, waits for them, and re-layouts  5.43 us
    ppermute x2, waiting for transfers between devices, pipe_shift(): return lax.ppermute(value, 'pipe', [(i, (i + by) % 8) for i in range(8)])  3.84 us
  transfers between devices with their start and end apart: 28, of which 15 were waited for; matrix products, arithmetic and copies ran while one was open for 2% of the time, Pallas kernels for 14%

profile of v1, /device:TPU:32, one launch (start us, length us, event | category | flops | bytes accessed | tf_op | source)
XLA Modules:
  0.0 151.2 jit_solution(5721959668125348938)
XLA Ops:
  2.3 5.5 %collective-permute-start = (bf16[64,3584]{1,0:T(8,128)(2,1)}, bf16[64,3584]{1,0:T(8,128)(2,1)S(1)}, u32[]{:S(2)}, u32[]{:S(2)}) collective-permute-start(bf16[64,3584]{1,0:T(8,128)(2,1)} %get-tuple-element.98), channel_id=1, source_target_pairs={{0,224},{32,0},{64,32},{96,64},{128,96},{160,128},{192,160},{224,1... | collective-permute-start | bytes 1376264 | tf_op jit(solution)/shard_map/ppermute | solution.py:34
  19.8 3.8 %collective-permute-done.1.second = bf16[64,3584]{1,0:T(8,128)(2,1)} collective-permute-done((bf16[64,3584]{1,0:T(8,128)(2,1)}, bf16[64,3584]{1,0:T(8,128)(2,1)}, u32[]{:S(2)}, u32[]{:S(2)}) %collective-permute-start.1) | collective-permute-done | bytes 458784 | tf_op jit(solution)/shard_map/ppermute | solution.py:34
  28.1 5.4 %collective-permute-done.3.low = bf16[32,3584]{1,0:T(8,128)(2,1)S(1)} collective-permute-done((bf16[32,3584]{1,0:T(8,128)(2,1)S(1)}, bf16[32,3584]{1,0:T(8,128)(2,1)S(1)}, u32[]{:S(2)}, u32[]{:S(2)}) %collective-permute-start.3) | collective-permute-done | bytes 229408 | tf_op jit(solution)/shard_map/ppermute | solution.py:39
  36.0 5.9 %collective-permute-start.5 = (bf16[32,3584]{1,0:T(8,128)(2,1)S(1)}, bf16[32,3584]{1,0:T(8,128)(2,1)S(1)}, u32[]{:S(2)}, u32[]{:S(2)}) collective-permute-start(bf16[32,3584]{1,0:T(8,128)(2,1)S(1)} %get-tuple-element.113), channel_id=1, source_target_pairs={{0,16},{1,17},{2,18},{3,19},{4,20},{5,21},{6,22},{7,23},{8,24},{9,... | collective-permute-start | bytes 688136 | tf_op jit(solution)/shard_map/ppermute | solution.py:39
  41.9 5.5 %collective-permute-done.6.theirs = bf16[64,3584]{1,0:T(8,128)(2,1)S(1)} collective-permute-done((bf16[64,3584]{1,0:T(8,128)(2,1)S(1)}, bf16[64,3584]{1,0:T(8,128)(2,1)S(1)}, u32[]{:S(2)}, u32[]{:S(2)}) %collective-permute-start.6) | collective-permute-done | bytes 458784 | tf_op jit(solution)/shard_map/ppermute | solution.py:43
  47.4 3.0 %shard_map.104 = (f32[64,3712]{1,0:T(8,128)S(1)}, bf16[64,3712]{1,0:T(8,128)(2,1)S(1)}) custom-call(s32[2]{0:T(128)S(1)} %pad_add_fusion.place, bf16[64,3584]{1,0:T(8,128)(2,1)S(1)} %shard_map.103.mine, bf16[64,3584]{1,0:T(8,128)(2,1)S(1)} %collective-permute-done.6.theirs, bf16[8,2,2,2,16,256]{5,4,3,2,1,0:T(8,128)(2,1)S(1)} %get-tuple-element.116.refs_0_, ...), custom_call_target="tpu_custom_call" | custom-call | flops 2000000000 | bytes 1000 | tf_op jit(solution)/shard_map/pallas_call | solution.py:316
  52.7 7.2 %collective-permute-start.11 = (bf16[32,3584]{1,0:T(8,128)(2,1)S(1)}, bf16[32,3584]{1,0:T(8,128)(2,1)S(1)}, u32[]{:S(2)}, u32[]{:S(2)}) collective-permute-start(bf16[32,3584]{1,0:T(8,128)(2,1)S(1)} %get-tuple-element.132), channel_id=1, source_target_pairs={{0,12},{1,13},{2,14},{3,15},{4,16},{5,17},{6,18},{7,19},{8,20},{9,... | collective-permute-start | bytes 688136 | tf_op jit(solution)/shard_map/ppermute | solution.py:39
  59.9 7.2 %collective-permute-done.10.theirs = bf16[32,3584]{1,0:T(8,128)(2,1)S(1)} collective-permute-done((bf16[32,3584]{1,0:T(8,128)(2,1)S(1)}, bf16[32,3584]{1,0:T(8,128)(2,1)S(1)}, u32[]{:S(2)}, u32[]{:S(2)}) %collective-permute-start.10) | collective-permute-done | bytes 229408 | tf_op jit(solution)/shard_map/ppermute | solution.py:43
  67.1 3.1 %shard_map.105 = (f32[32,3712]{1,0:T(8,128)S(1)}, bf16[32,3712]{1,0:T(8,128)(2,1)S(1)}) custom-call(s32[2]{0:T(128)S(1)} %pad_add_fusion.place, bf16[32,3584]{1,0:T(8,128)(2,1)S(1)} %collective-permute-done.5.mine, bf16[32,3584]{1,0:T(8,128)(2,1)S(1)} %collective-permute-done.10.theirs, bf16[8,2,2,2,16,256]{5,4,3,2,1,0:T(8,128)(2,1)S(1)} %get-tuple-element.116.refs_0_, ...), custom_call_target="tpu_custom_call" | custom-call | flops 2000000000 | bytes 1000 | tf_op jit(solution)/shard_map/pallas_call | solution.py:316
  70.2 3.0 %collective-permute-done.11.low = bf16[32,3584]{1,0:T(8,128)(2,1)S(1)} collective-permute-done((bf16[32,3584]{1,0:T(8,128)(2,1)S(1)}, bf16[32,3584]{1,0:T(8,128)(2,1)S(1)}, u32[]{:S(2)}, u32[]{:S(2)}) %collective-permute-start.11) | collective-permute-done | bytes 229408 | tf_op jit(solution)/shard_map/ppermute | solution.py:39
  73.2 3.5 %collective-permute-done.12.high = bf16[32,3584]{1,0:T(8,128)(2,1)S(1)} collective-permute-done((bf16[32,3584]{1,0:T(8,128)(2,1)S(1)}, bf16[32,3584]{1,0:T(8,128)(2,1)S(1)}, u32[]{:S(2)}, u32[]{:S(2)}) %collective-permute-start.12) | collective-permute-done | bytes 229408 | tf_op jit(solution)/shard_map/ppermute | solution.py:39
  80.1 2.9 %collective-permute-start.15 = (bf16[32,3584]{1,0:T(8,128)(2,1)S(1)}, bf16[32,3584]{1,0:T(8,128)(2,1)S(1)}, u32[]{:S(2)}, u32[]{:S(2)}) collective-permute-start(bf16[32,3584]{1,0:T(8,128)(2,1)S(1)} %get-tuple-element.143), channel_id=1, source_target_pairs={{0,24},{1,25},{2,26},{3,27},{4,28},{5,29},{6,30},{7,31},{8,0},{9,1... | collective-permute-start | bytes 688136 | tf_op jit(solution)/shard_map/ppermute | solution.py:39
  83.0 5.3 %collective-permute-done.13.theirs = bf16[64,3584]{1,0:T(8,128)(2,1)S(1)} collective-permute-done((bf16[64,3584]{1,0:T(8,128)(2,1)S(1)}, bf16[64,3584]{1,0:T(8,128)(2,1)S(1)}, u32[]{:S(2)}, u32[]{:S(2)}) %collective-permute-start.13) | collective-permute-done | bytes 458784 | tf_op jit(solution)/shard_map/ppermute | solution.py:43
  88.3 3.0 %shard_map.107 = (f32[64,3712]{1,0:T(8,128)S(1)}, bf16[64,3712]{1,0:T(8,128)(2,1)S(1)}) custom-call(s32[2]{0:T(128)S(1)} %pad_add_fusion.place, bf16[64,3584]{1,0:T(8,128)(2,1)S(1)} %shard_map.106.mine, bf16[64,3584]{1,0:T(8,128)(2,1)S(1)} %collective-permute-done.13.theirs, bf16[8,2,2,2,16,256]{5,4,3,2,1,0:T(8,128)(2,1)S(1)} %get-tuple-element.116.refs_0_, ...), custom_call_target="tpu_custom_call" | custom-call | flops 2000000000 | bytes 1000 | tf_op jit(solution)/shard_map/pallas_call | solution.py:316
  97.1 3.3 %collective-permute-start.19 = (bf16[32,3712]{1,0:T(8,128)(2,1)S(1)}, bf16[32,3712]{1,0:T(8,128)(2,1)S(1)}, u32[]{:S(2)}, u32[]{:S(2)}) collective-permute-start(bf16[32,3712]{1,0:T(8,128)(2,1)S(1)} %get-tuple-element.156), channel_id=1, source_target_pairs={{0,16},{1,17},{2,18},{3,19},{4,20},{5,21},{6,22},{7,23},{8,24},{9,... | collective-permute-start | bytes 712712 | tf_op jit(solution)/shard_map/ppermute | solution.py:39
  100.5 3.1 %shard_map.111 = (f32[32,3712]{1,0:T(8,128)S(1)}, bf16[32,3712]{1,0:T(8,128)(2,1)S(1)}) custom-call(s32[2]{0:T(128)S(1)} %pad_add_fusion.place, bf16[32,3584]{1,0:T(8,128)(2,1)S(1)} %get-tuple-element.163.mine, bf16[32,3584]{1,0:T(8,128)(2,1)S(1)} %collective-permute-done.2.theirs, bf16[8,2,2,2,16,256]{5,4,3,2,1,0:T(8,128)(2,1)S(1)} %get-tuple-element.116.refs_0_, ...), custom_call_target="tpu_custom_call" | custom-call | flops 2000000000 | bytes 1000 | tf_op jit(solution)/shard_map/pallas_call | solution.py:316
  106.2 3.0 %shard_map.110 = (f32[64,3712]{1,0:T(8,128)S(1)}, bf16[64,3712]{1,0:T(8,128)(2,1)S(1)}) custom-call(s32[2]{0:T(128)S(1)} %pad_add_fusion.place, bf16[64,3584]{1,0:T(8,128)(2,1)S(1)} %shard_map.109.mine, bf16[64,3584]{1,0:T(8,128)(2,1)S(1)} %collective-permute-done.21.theirs, bf16[8,2,2,2,16,256]{5,4,3,2,1,0:T(8,128)(2,1)S(1)} %get-tuple-element.116.refs_0_, ...), custom_call_target="tpu_custom_call" | custom-call | flops 2000000000 | bytes 1000 | tf_op jit(solution)/shard_map/pallas_call | solution.py:316
  109.3 4.4 %collective-permute-done.20.got = bf16[64,3712]{1,0:T(8,128)(2,1)S(1)} collective-permute-done((bf16[64,3712]{1,0:T(8,128)(2,1)S(1)}, bf16[64,3712]{1,0:T(8,128)(2,1)S(1)}, u32[]{:S(2)}, u32[]{:S(2)}) %collective-permute-start.20) | collective-permute-done | bytes 475168 | tf_op jit(solution)/shard_map/ppermute | solution.py:43
  114.1 4.8 %collective-permute-start.22 = (bf16[32,3712]{1,0:T(8,128)(2,1)S(1)}, bf16[32,3712]{1,0:T(8,128)(2,1)S(1)}, u32[]{:S(2)}, u32[]{:S(2)}) collective-permute-start(bf16[32,3712]{1,0:T(8,128)(2,1)S(1)} %get-tuple-element.169), channel_id=1, source_target_pairs={{0,20},{1,21},{2,22},{3,23},{4,24},{5,25},{6,26},{7,27},{8,28},{9,... | collective-permute-start | bytes 712712 | tf_op jit(solution)/shard_map/ppermute | solution.py:39
  121.0 11.1 %collective-permute-done.22.b3 = bf16[32,3712]{1,0:T(8,128)(2,1)S(1)} collective-permute-done((bf16[32,3712]{1,0:T(8,128)(2,1)S(1)}, bf16[32,3712]{1,0:T(8,128)(2,1)S(1)}, u32[]{:S(2)}, u32[]{:S(2)}) %collective-permute-start.22) | collective-permute-done | bytes 237600 | tf_op jit(solution)/shard_map/ppermute | solution.py:39
  132.1 3.3 %collective-permute-done.23.b5 = bf16[32,3712]{1,0:T(8,128)(2,1)S(1)} collective-permute-done((bf16[32,3712]{1,0:T(8,128)(2,1)S(1)}, bf16[32,3712]{1,0:T(8,128)(2,1)S(1)}, u32[]{:S(2)}, u32[]{:S(2)}) %collective-permute-start.23) | collective-permute-done | bytes 237600 | tf_op jit(solution)/shard_map/ppermute | solution.py:39
  135.7 2.9 %collective-permute-start.27 = (bf16[32,3712]{1,0:T(8,128)(2,1)S(1)}, bf16[32,3712]{1,0:T(8,128)(2,1)S(1)}, u32[]{:S(2)}, u32[]{:S(2)}) collective-permute-start(bf16[32,3712]{1,0:T(8,128)(2,1)S(1)} %get-tuple-element.178), channel_id=1, source_target_pairs={{0,8},{1,9},{2,10},{3,11},{4,12},{5,13},{6,14},{7,15},{8,16},{9,17... | collective-permute-start | bytes 712712 | tf_op jit(solution)/shard_map/ppermute | solution.py:39
  139.0 6.5 %collective-permute-done.26.b2 = bf16[32,3712]{1,0:T(8,128)(2,1)S(1)} collective-permute-done((bf16[32,3712]{1,0:T(8,128)(2,1)S(1)}, bf16[32,3712]{1,0:T(8,128)(2,1)S(1)}, u32[]{:S(2)}, u32[]{:S(2)}) %collective-permute-start.26) | collective-permute-done | bytes 237600 | tf_op jit(solution)/shard_map/ppermute | solution.py:39
  147.8 3.4 %shard_map.115 = bf16[2,64,3584]{2,1,0:T(8,128)(2,1)} custom-call(bf16[32,3712]{1,0:T(8,128)(2,1)S(1)} %collective-permute-done.26.b2, bf16[32,3712]{1,0:T(8,128)(2,1)S(1)} %collective-permute-done.27.b6, f32[2,64,3584]{2,1,0:T(8,128)S(1)} %get-tuple-element.186.some, f32[2,128,1]{2,1,0:T(8,128)S(1)} %get-tuple-element.187.some_dw, ...), custom_call_target="tpu_custom_call" | custom-call | flops 100000 | bytes 1000 | tf_op jit(solution)/shard_map/pallas_call | solution.py:392
  (72 shorter events, 40.8 us)
Async XLA Ops:
  2.3 17.5 %collective-permute-start = (bf16[64,3584]{1,0:T(8,128)(2,1)}, bf16[64,3584]{1,0:T(8,128)(2,1)S(1)}, u32[]{:S(2)}, u32[]{:S(2)}) collective-permute-start(bf16[64,3584]{1,0:T(8,128)(2,1)} %get-tuple-element.98), channel_id=1, source_target_pairs={{0,224},{32,0},{64,32},{96,64},{128,96},{160,128},{192,160},{224,1... | collective-permute-start | bytes 1376264 | tf_op jit(solution)/shard_map/ppermute | solution.py:34
  7.8 15.9 %collective-permute-start.1 = (bf16[64,3584]{1,0:T(8,128)(2,1)}, bf16[64,3584]{1,0:T(8,128)(2,1)}, u32[]{:S(2)}, u32[]{:S(2)}) collective-permute-start(bf16[64,3584]{1,0:T(8,128)(2,1)} %get-tuple-element.99), channel_id=1, source_target_pairs={{0,32},{32,64},{64,96},{96,128},{128,160},{160,192},{192,224},{224... | collective-permute-start | bytes 1376264 | tf_op jit(solution)/shard_map/ppermute | solution.py:34
  23.7 23.8 %collective-permute-start.8 = (bf16[768,3584]{1,0:T(8,128)(2,1)}, bf16[768,3584]{1,0:T(8,128)(2,1)S(1)}, u32[]{:S(2)}, u32[]{:S(2)}) collective-permute-start(bf16[768,3584]{1,0:T(8,128)(2,1)} %copy-done), channel_id=1, source_target_pairs={{0,1},{1,0},{2,3},{3,2},{4,5},{5,4},{6,7},{7,6},{8,9},{9,8},{10,11... | collective-permute-start | bytes 16515080 | tf_op jit(solution)/shard_map/ppermute | solution.py:47
  28.1 13.9 %collective-permute-start.7 = (bf16[8,2,2,2,16,256]{5,4,3,2,1,0:T(8,128)(2,1)S(1)}, bf16[8,2,2,2,16,256]{5,4,3,2,1,0:T(8,128)(2,1)S(1)}, u32[]{:S(2)}, u32[]{:S(2)}) collective-permute-start(bf16[8,2,2,2,16,256]{5,4,3,2,1,0:T(8,128)(2,1)S(1)} %get-tuple-element.117), channel_id=1, source_target_pairs={{0,1},{1,0},{2,3},{3,2},{4,5},{5,4},{6,7},{7,6},{8,9},{9,8},{10,11... | collective-permute-start | bytes 1572872 | tf_op jit(solution)/shard_map/ppermute | solution.py:47
  35.3 12.1 %collective-permute-start.6 = (bf16[64,3584]{1,0:T(8,128)(2,1)S(1)}, bf16[64,3584]{1,0:T(8,128)(2,1)S(1)}, u32[]{:S(2)}, u32[]{:S(2)}) collective-permute-start(bf16[64,3584]{1,0:T(8,128)(2,1)S(1)} %shard_map.103.mine), channel_id=1, source_target_pairs={{0,2},{1,3},{2,0},{3,1},{4,6},{5,7},{6,4},{7,5},{8,10},{9,11},{10,... | collective-permute-start | bytes 1376264 | tf_op jit(solution)/shard_map/ppermute | solution.py:43
  36.0 14.4 %collective-permute-start.5 = (bf16[32,3584]{1,0:T(8,128)(2,1)S(1)}, bf16[32,3584]{1,0:T(8,128)(2,1)S(1)}, u32[]{:S(2)}, u32[]{:S(2)}) collective-permute-start(bf16[32,3584]{1,0:T(8,128)(2,1)S(1)} %get-tuple-element.113), channel_id=1, source_target_pairs={{0,16},{1,17},{2,18},{3,19},{4,20},{5,21},{6,22},{7,23},{8,24},{9,... | collective-permute-start | bytes 688136 | tf_op jit(solution)/shard_map/ppermute | solution.py:39
  50.4 26.3 %collective-permute-start.9 = (bf16[64,3712]{1,0:T(8,128)(2,1)S(1)}, bf16[64,3712]{1,0:T(8,128)(2,1)S(1)}, u32[]{:S(2)}, u32[]{:S(2)}) collective-permute-start(bf16[64,3712]{1,0:T(8,128)(2,1)S(1)} %get-tuple-element.127), channel_id=1, source_target_pairs={{0,2},{1,3},{2,0},{3,1},{4,6},{5,7},{6,4},{7,5},{8,10},{9,11},{10,... | collective-permute-start | bytes 1425416 | tf_op jit(solution)/shard_map/ppermute | solution.py:43
  51.3 15.8 %collective-permute-start.10 = (bf16[32,3584]{1,0:T(8,128)(2,1)S(1)}, bf16[32,3584]{1,0:T(8,128)(2,1)S(1)}, u32[]{:S(2)}, u32[]{:S(2)}) collective-permute-start(bf16[32,3584]{1,0:T(8,128)(2,1)S(1)} %collective-permute-done.5.mine), channel_id=1, source_target_pairs={{0,2},{1,3},{2,0},{3,1},{4,6},{5,7},{6,4},{7,5},{8,10},{9,11},{10,... | collective-permute-start | bytes 688136 | tf_op jit(solution)/shard_map/ppermute | solution.py:43
  52.7 20.5 %collective-permute-start.11 = (bf16[32,3584]{1,0:T(8,128)(2,1)S(1)}, bf16[32,3584]{1,0:T(8,128)(2,1)S(1)}, u32[]{:S(2)}, u32[]{:S(2)}) collective-permute-start(bf16[32,3584]{1,0:T(8,128)(2,1)S(1)} %get-tuple-element.132), channel_id=1, source_target_pairs={{0,12},{1,13},{2,14},{3,15},{4,16},{5,17},{6,18},{7,19},{8,20},{9,... | collective-permute-start | bytes 688136 | tf_op jit(solution)/shard_map/ppermute | solution.py:39
  59.9 16.8 %collective-permute-start.12 = (bf16[32,3584]{1,0:T(8,128)(2,1)S(1)}, bf16[32,3584]{1,0:T(8,128)(2,1)S(1)}, u32[]{:S(2)}, u32[]{:S(2)}) collective-permute-start(bf16[32,3584]{1,0:T(8,128)(2,1)S(1)} %get-tuple-element.133), channel_id=1, source_target_pairs={{0,20},{1,21},{2,22},{3,23},{4,24},{5,25},{6,26},{7,27},{8,28},{9,... | collective-permute-start | bytes 688136 | tf_op jit(solution)/shard_map/ppermute | solution.py:39
  76.7 11.6 %collective-permute-start.13 = (bf16[64,3584]{1,0:T(8,128)(2,1)S(1)}, bf16[64,3584]{1,0:T(8,128)(2,1)S(1)}, u32[]{:S(2)}, u32[]{:S(2)}) collective-permute-start(bf16[64,3584]{1,0:T(8,128)(2,1)S(1)} %shard_map.106.mine), channel_id=1, source_target_pairs={{0,2},{1,3},{2,0},{3,1},{4,6},{5,7},{6,4},{7,5},{8,10},{9,11},{10,... | collective-permute-start | bytes 1376264 | tf_op jit(solution)/shard_map/ppermute | solution.py:43
  78.2 14.5 %collective-permute-start.16 = (bf16[32,3712]{1,0:T(8,128)(2,1)S(1)}, bf16[32,3712]{1,0:T(8,128)(2,1)S(1)}, u32[]{:S(2)}, u32[]{:S(2)}) collective-permute-start(bf16[32,3712]{1,0:T(8,128)(2,1)S(1)} %get-tuple-element.144), channel_id=1, source_target_pairs={{0,2},{1,3},{2,0},{3,1},{4,6},{5,7},{6,4},{7,5},{8,10},{9,11},{10,... | collective-permute-start | bytes 712712 | tf_op jit(solution)/shard_map/ppermute | solution.py:43
  78.9 12.4 %collective-permute-start.14 = (bf16[32,3584]{1,0:T(8,128)(2,1)S(1)}, bf16[32,3584]{1,0:T(8,128)(2,1)S(1)}, u32[]{:S(2)}, u32[]{:S(2)}) collective-permute-start(bf16[32,3584]{1,0:T(8,128)(2,1)S(1)} %get-tuple-element.142), channel_id=1, source_target_pairs={{0,8},{1,9},{2,10},{3,11},{4,12},{5,13},{6,14},{7,15},{8,16},{9,17... | collective-permute-start | bytes 688136 | tf_op jit(solution)/shard_map/ppermute | solution.py:39
  80.1 12.5 %collective-permute-start.15 = (bf16[32,3584]{1,0:T(8,128)(2,1)S(1)}, bf16[32,3584]{1,0:T(8,128)(2,1)S(1)}, u32[]{:S(2)}, u32[]{:S(2)}) collective-permute-start(bf16[32,3584]{1,0:T(8,128)(2,1)S(1)} %get-tuple-element.143), channel_id=1, source_target_pairs={{0,24},{1,25},{2,26},{3,27},{4,28},{5,29},{6,30},{7,31},{8,0},{9,1... | collective-permute-start | bytes 688136 | tf_op jit(solution)/shard_map/ppermute | solution.py:39
  92.7 13.5 %collective-permute-start.21 = (bf16[64,3584]{1,0:T(8,128)(2,1)S(1)}, bf16[64,3584]{1,0:T(8,128)(2,1)S(1)}, u32[]{:S(2)}, u32[]{:S(2)}) collective-permute-start(bf16[64,3584]{1,0:T(8,128)(2,1)S(1)} %shard_map.109.mine), channel_id=1, source_target_pairs={{0,2},{1,3},{2,0},{3,1},{4,6},{5,7},{6,4},{7,5},{8,10},{9,11},{10,... | collective-permute-start | bytes 1376264 | tf_op jit(solution)/shard_map/ppermute | solution.py:43
  93.4 20.3 %collective-permute-start.20 = (bf16[64,3712]{1,0:T(8,128)(2,1)S(1)}, bf16[64,3712]{1,0:T(8,128)(2,1)S(1)}, u32[]{:S(2)}, u32[]{:S(2)}) collective-permute-start(bf16[64,3712]{1,0:T(8,128)(2,1)S(1)} %get-tuple-element.157), channel_id=1, source_target_pairs={{0,2},{1,3},{2,0},{3,1},{4,6},{5,7},{6,4},{7,5},{8,10},{9,11},{10,... | collective-permute-start | bytes 1425416 | tf_op jit(solution)/shard_map/ppermute | solution.py:43
  95.0 14.2 %collective-permute-start.17 = (bf16[32,3712]{1,0:T(8,128)(2,1)S(1)}, bf16[32,3712]{1,0:T(8,128)(2,1)S(1)}, u32[]{:S(2)}, u32[]{:S(2)}) collective-permute-start(bf16[32,3712]{1,0:T(8,128)(2,1)S(1)} %get-tuple-element.154), channel_id=1, source_target_pairs={{0,28},{1,29},{2,30},{3,31},{4,0},{5,1},{6,2},{7,3},{8,4},{9,5},{1... | collective-permute-start | bytes 712712 | tf_op jit(solution)/shard_map/ppermute | solution.py:39
  95.1 14.1 %collective-permute-start.18 = (bf16[32,3712]{1,0:T(8,128)(2,1)S(1)}, bf16[32,3712]{1,0:T(8,128)(2,1)S(1)}, u32[]{:S(2)}, u32[]{:S(2)}) collective-permute-start(bf16[32,3712]{1,0:T(8,128)(2,1)S(1)} %get-tuple-element.155), channel_id=1, source_target_pairs={{0,4},{1,5},{2,6},{3,7},{4,8},{5,9},{6,10},{7,11},{8,12},{9,13},{1... | collective-permute-start | bytes 712712 | tf_op jit(solution)/shard_map/ppermute | solution.py:39
  97.1 12.1 %collective-permute-start.19 = (bf16[32,3712]{1,0:T(8,128)(2,1)S(1)}, bf16[32,3712]{1,0:T(8,128)(2,1)S(1)}, u32[]{:S(2)}, u32[]{:S(2)}) collective-permute-start(bf16[32,3712]{1,0:T(8,128)(2,1)S(1)} %get-tuple-element.156), channel_id=1, source_target_pairs={{0,16},{1,17},{2,18},{3,19},{4,20},{5,21},{6,22},{7,23},{8,24},{9,... | collective-permute-start | bytes 712712 | tf_op jit(solution)/shard_map/ppermute | solution.py:39
  113.7 21.8 %collective-permute-start.24 = (bf16[64,3712]{1,0:T(8,128)(2,1)S(1)}, bf16[64,3712]{1,0:T(8,128)(2,1)S(1)}, u32[]{:S(2)}, u32[]{:S(2)}) collective-permute-start(bf16[64,3712]{1,0:T(8,128)(2,1)S(1)} %get-tuple-element.171), channel_id=1, source_target_pairs={{0,2},{1,3},{2,0},{3,1},{4,6},{5,7},{6,4},{7,5},{8,10},{9,11},{10,... | collective-permute-start | bytes 1425416 | tf_op jit(solution)/shard_map/ppermute | solution.py:43
  114.1 18.0 %collective-permute-start.22 = (bf16[32,3712]{1,0:T(8,128)(2,1)S(1)}, bf16[32,3712]{1,0:T(8,128)(2,1)S(1)}, u32[]{:S(2)}, u32[]{:S(2)}) collective-permute-start(bf16[32,3712]{1,0:T(8,128)(2,1)S(1)} %get-tuple-element.169), channel_id=1, source_target_pairs={{0,20},{1,21},{2,22},{3,23},{4,24},{5,25},{6,26},{7,27},{8,28},{9,... | collective-permute-start | bytes 712712 | tf_op jit(solution)/shard_map/ppermute | solution.py:39
  118.9 16.5 %collective-permute-start.23 = (bf16[32,3712]{1,0:T(8,128)(2,1)S(1)}, bf16[32,3712]{1,0:T(8,128)(2,1)S(1)}, u32[]{:S(2)}, u32[]{:S(2)}) collective-permute-start(bf16[32,3712]{1,0:T(8,128)(2,1)S(1)} %get-tuple-element.170), channel_id=1, source_target_pairs={{0,12},{1,13},{2,14},{3,15},{4,16},{5,17},{6,18},{7,19},{8,20},{9,... | collective-permute-start | bytes 712712 | tf_op jit(solution)/shard_map/ppermute | solution.py:39
  119.2 16.2 %collective-permute-start.25 = (bf16[32,3712]{1,0:T(8,128)(2,1)S(1)}, bf16[32,3712]{1,0:T(8,128)(2,1)S(1)}, u32[]{:S(2)}, u32[]{:S(2)}) collective-permute-start(bf16[32,3712]{1,0:T(8,128)(2,1)S(1)} %get-tuple-element.173), channel_id=1, source_target_pairs={{0,2},{1,3},{2,0},{3,1},{4,6},{5,7},{6,4},{7,5},{8,10},{9,11},{10,... | collective-permute-start | bytes 712712 | tf_op jit(solution)/shard_map/ppermute | solution.py:43
  135.7 12.1 %collective-permute-start.27 = (bf16[32,3712]{1,0:T(8,128)(2,1)S(1)}, bf16[32,3712]{1,0:T(8,128)(2,1)S(1)}, u32[]{:S(2)}, u32[]{:S(2)}) collective-permute-start(bf16[32,3712]{1,0:T(8,128)(2,1)S(1)} %get-tuple-element.178), channel_id=1, source_target_pairs={{0,8},{1,9},{2,10},{3,11},{4,12},{5,13},{6,14},{7,15},{8,16},{9,17... | collective-permute-start | bytes 712712 | tf_op jit(solution)/shard_map/ppermute | solution.py:39
  (14 other events, 95.0 us)

commit v2 on v1

--- a/solution.py
+++ b/solution.py
@@ -69,8 +69,13 @@
     return high, total - high
 
 
-def prep_kernel(place, limits, routes, saved, gain, router, match, weight, scores, inv):
+def prep_kernel(
+    place, limits, routes, saved, gain, router, match, weight, scores, inv, parts
+):
     z = place[0]
+    high = router[...].astype(BF16).astype(F32)
+    low = router[...] - high
+    parts[...] = jnp.concatenate([high, high, low, jnp.zeros_like(low)], axis=0).astype(BF16)
     slot = lax.broadcasted_iota(jnp.int32, (SLOTS, TOKENS), 0)
     expert = ((slot >> 4) + z) & (EXPERTS - 1)
     number = slot & (CAP - 1)
@@ -109,6 +114,17 @@
             share = (ROUTE_SCALE * chosen[k] / totals).astype(BF16).astype(F32)
             column = column + jnp.sum(hit * share, axis=-1, keepdims=True)
         weight[m] = column
+
+
+def split_kernel(sent, first, second, sems):
+    copies = [
+        pltpu.make_async_copy(sent.at[0, m], out, sems.at[m])
+        for m, out in enumerate((first, second))
+    ]
+    for copy in copies:
+        copy.start()
+    for copy in copies:
+        copy.wait()
 
 
 def spread_kernel(first, second, match, weight, kept, *outs):
@@ -210,24 +226,25 @@
 
 
 def finish_kernel(
-    b2, b6, some, some_dw, kept, saved, routes, match, weight, scores, inv, gain, router, out, back
+    b2, b6, some, some_dw, kept, saved, routes, match, weight, scores, inv, gain, parts, out, back
 ):
     names = lax.broadcasted_iota(jnp.int32, (EXPERTS, TOKENS), 0)
     low, high = slice(2 * CAP, 3 * CAP), slice(6 * CAP, 7 * CAP)
+    back[2 * CAP :] = parts[...]
     for m in range(2):
         finish_part(
             m, b2, b6, some, some_dw, kept, saved, routes, match, weight, scores, inv, gain,
-            router, out, back, names, low, high,
+            out, back, names, low, high,
         )
 
 
 def finish_part(
-    m, b2, b6, some, some_dw, kept, saved, routes, match, weight, scores, inv, gain, router, out,
+    m, b2, b6, some, some_dw, kept, saved, routes, match, weight, scores, inv, gain, out,
     back, names, low, high,
 ):
     at = slice(m * CAP, (m + 1) * CAP)
     back[:CAP] = b2[at, :D]
-    back[CAP:] = b6[at, :D]
+    back[CAP : 2 * CAP] = b6[at, :D]
     late = [jnp.sum(unit[at, D:].astype(F32), axis=-1, keepdims=True) for unit in (b2, b6)]
     slot_dw = some_dw[m]
     slot_dw = jnp.concatenate(
@@ -250,12 +267,13 @@
         slope = ROUTE_SCALE * (choice[k] / totals - inner)
         score_grad = score_grad + jnp.where(picked[k], slope, 0.0)
     score_grad = score_grad * score * (1.0 - score)
-    both = (match[m, 0] + match[m, 1]).astype(BF16)
-    both = jnp.concatenate([both[low], both[high]], axis=0)
+    both = match[m, 0] + match[m, 1]
+    main = score_grad.astype(BF16).astype(F32)
+    rest = score_grad - main
+    both = jnp.concatenate(
+        [both[low], both[high], main, rest, main, jnp.zeros_like(main)], axis=0
+    ).astype(BF16)
     total = some[m] + lax.dot_general(both, back[...], TN, preferred_element_type=F32)
-    total = total + lax.dot_general(
-        score_grad, router[...], TN, precision=HIGHEST, preferred_element_type=F32
-    )
     scaled = gain[...] * total
     values = saved[m].astype(F32)
     inv_rms = inv[m]
@@ -277,7 +295,15 @@
     index = lax.axis_index("expert")
     core = index % 2
     place = jnp.stack([index // 4, (index // 2) % 2]).astype(jnp.int32)
-    first, second = lax.optimization_barrier((grads_sent[0, 0], grads_sent[0, 1]))
+    first, second = pl.pallas_call(
+        split_kernel,
+        out_shape=(shape((TOKENS, D)), shape((TOKENS, D))),
+        in_specs=[pl.BlockSpec(memory_space=pl.ANY)],
+        out_specs=(VMEM, VMEM),
+        scratch_shapes=[pltpu.SemaphoreType.DMA((2,))],
+        cost_estimate=pl.CostEstimate(flops=COST, bytes_accessed=1000, transcendentals=0),
+        compiler_params=pltpu.CompilerParams(vmem_limit_bytes=LIMIT),
+    )(grads_sent)
     first, second = pipe_shift(first, -1), pipe_shift(second, 1)
     packed = call(stage_kernel, shape((3 * SLICE, D)), [VMEM] * 3, COST, 1000)(
         w_down, w_gate, w_up
@@ -286,13 +312,14 @@
     pre = jnp.transpose(pre, (3, 1, 2, 5, 0, 4, 6))
     routes_t = jnp.transpose(routes[0], (0, 2, 1))
     router_t = router[0].T
-    match, weight, scores, inv = call(
+    match, weight, scores, inv, parts = call(
         prep_kernel,
         (
             shape((2, 2, SLOTS, TOKENS), F32),
             shape((2, SLOTS, 1), F32),
             shape((2, EXPERTS, TOKENS), F32),
             shape((2, TOKENS, 1), F32),
+            shape((4 * EXPERTS, D)),
         ),
         [SMEM, SMEM] + [VMEM] * 4,
         COST,
@@ -377,7 +404,7 @@
     z_back(3, 5)
     v["got2"] = x_swap(v["away2"])
     v["got0"] = x_swap(v["away0"])
-    tie("b3", "b5", "got2", "own2", "got0", "own0")
+    tie("got2", "own2")
     v["d2"], v["d6"] = add((2, 6), v["own2"], v["got2"])
     z_back(2, 6)
     some, some_dw = pl.pallas_call(
@@ -394,7 +421,7 @@
         out_shape=shape((2, TOKENS, D)),
         in_specs=[VMEM] * 13,
         out_specs=VMEM,
-        scratch_shapes=[pltpu.VMEM((2 * CAP, D), BF16)],
+        scratch_shapes=[pltpu.VMEM((2 * CAP + 4 * EXPERTS, D), BF16)],
         cost_estimate=pl.CostEstimate(flops=COST, bytes_accessed=1000, transcendentals=0),
         compiler_params=pltpu.CompilerParams(vmem_limit_bytes=LIMIT),
     )(
@@ -410,7 +437,7 @@
         scores,
         inv,
         norm_gain,
-        router_t,
+        parts,
     )
     return out[None]
 

time: 154 us -> 147 us (0.955); the launches traced: 151 us -> 147 us
  waiting for transfers between devices: 67.1 us -> 61.3 us
  starting transfers between devices: 48.2 us -> 51.9 us
  Pallas kernels: 25 us -> 23.1 us
    ppermute x14, waiting for transfers between devices: 38.2 us -> 30 us  [z_shift(): return lax.ppermute(value, 'expert', pairs)]
    ppermute x10, waiting for transfers between devices: 25 us -> 28.9 us  [x_swap(): return lax.ppermute(value, 'expert', [(i, i ^ 2) for i in range(32)])]
    ppermute x14, starting transfers between devices: 32.9 us -> 36.5 us  [z_shift(): return lax.ppermute(value, 'expert', pairs)]
    unnamed x20 -> x22, local copies, waits for them, and re-layouts: 5.43 us -> 8.11 us
    squeeze x1 -> x0, local copies, waits for them, and re-layouts: 2.28 us -> none  [local(): grads_sent[0, 1]]
where the time goes in v2:
time: 147 us
  waiting for transfers between devices  61.3 us (42%)
  starting transfers between devices  51.9 us (35%)
  Pallas kernels  23.1 us (16%)
  local copies, waits for them, and re-layouts  10.6 us (7%)
    ppermute x14, starting transfers between devices, z_shift(): return lax.ppermute(value, 'expert', pairs)  36.5 us
    ppermute x14, waiting for transfers between devices, z_shift(): return lax.ppermute(value, 'expert', pairs)  30 us
    ppermute x10, waiting for transfers between devices, x_swap(): return lax.ppermute(value, 'expert', [(i, i ^ 2) for i in range(32)])  28.9 us
    pallas_call x5, Pallas kernels, work(): pl.pallas_call(functools.partial(unit_kernel, group), out_shape=(shape((U...  15.1 us
    ppermute x10, starting transfers between devices, x_swap(): return lax.ppermute(value, 'expert', [(i, i ^ 2) for i in range(32)])  9.82 us
    unnamed x22, local copies, waits for them, and re-layouts  8.11 us
    ppermute x2, starting transfers between devices, pipe_shift(): return lax.ppermute(value, 'pipe', [(i, (i + by) % 8) for i in range(8)])  5.55 us
  transfers between devices with their start and end apart: 28, of which 15 were waited for; matrix products, arithmetic and copies ran while one was open for 2% of the time, Pallas kernels for 14%

profile of v2, /device:TPU:32, one launch (start us, length us, event | category | flops | bytes accessed | tf_op | source)
XLA Modules:
  0.0 147.2 jit_solution(15610630273187342173)
XLA Ops:
  1.7 5.6 %collective-permute-start = (bf16[64,3584]{1,0:T(8,128)(2,1)S(1)}, bf16[64,3584]{1,0:T(8,128)(2,1)S(1)}, u32[]{:S(2)}, u32[]{:S(2)}) collective-permute-start(bf16[64,3584]{1,0:T(8,128)(2,1)S(1)} %get-tuple-element.95), channel_id=1, source_target_pairs={{0,224},{32,0},{64,32},{96,64},{128,96},{160,128},{192,160},{224,1... | collective-permute-start | bytes 1376264 | tf_op jit(solution)/shard_map/ppermute | solution.py:34
  26.2 5.4 %collective-permute-done.3.low = bf16[32,3584]{1,0:T(8,128)(2,1)S(1)} collective-permute-done((bf16[32,3584]{1,0:T(8,128)(2,1)S(1)}, bf16[32,3584]{1,0:T(8,128)(2,1)S(1)}, u32[]{:S(2)}, u32[]{:S(2)}) %collective-permute-start.3) | collective-permute-done | bytes 229408 | tf_op jit(solution)/shard_map/ppermute | solution.py:39
  34.2 5.9 %collective-permute-start.5 = (bf16[32,3584]{1,0:T(8,128)(2,1)S(1)}, bf16[32,3584]{1,0:T(8,128)(2,1)S(1)}, u32[]{:S(2)}, u32[]{:S(2)}) collective-permute-start(bf16[32,3584]{1,0:T(8,128)(2,1)S(1)} %get-tuple-element.110), channel_id=1, source_target_pairs={{0,16},{1,17},{2,18},{3,19},{4,20},{5,21},{6,22},{7,23},{8,24},{9,... | collective-permute-start | bytes 688136 | tf_op jit(solution)/shard_map/ppermute | solution.py:39
  40.1 5.5 %collective-permute-done.6.theirs = bf16[64,3584]{1,0:T(8,128)(2,1)S(1)} collective-permute-done((bf16[64,3584]{1,0:T(8,128)(2,1)S(1)}, bf16[64,3584]{1,0:T(8,128)(2,1)S(1)}, u32[]{:S(2)}, u32[]{:S(2)}) %collective-permute-start.6) | collective-permute-done | bytes 458784 | tf_op jit(solution)/shard_map/ppermute | solution.py:43
  45.6 2.9 %shard_map.105 = (f32[64,3712]{1,0:T(8,128)S(1)}, bf16[64,3712]{1,0:T(8,128)(2,1)S(1)}) custom-call(s32[2]{0:T(128)S(1)} %pad_add_fusion.place, bf16[64,3584]{1,0:T(8,128)(2,1)S(1)} %shard_map.104.mine, bf16[64,3584]{1,0:T(8,128)(2,1)S(1)} %collective-permute-done.6.theirs, bf16[8,2,2,2,16,256]{5,4,3,2,1,0:T(8,128)(2,1)S(1)} %get-tuple-element.113.refs_0_, ...), custom_call_target="tpu_custom_call" | custom-call | flops 2000000000 | bytes 1000 | tf_op jit(solution)/shard_map/pallas_call | solution.py:343
  50.9 7.2 %collective-permute-start.11 = (bf16[32,3584]{1,0:T(8,128)(2,1)S(1)}, bf16[32,3584]{1,0:T(8,128)(2,1)S(1)}, u32[]{:S(2)}, u32[]{:S(2)}) collective-permute-start(bf16[32,3584]{1,0:T(8,128)(2,1)S(1)} %get-tuple-element.129), channel_id=1, source_target_pairs={{0,12},{1,13},{2,14},{3,15},{4,16},{5,17},{6,18},{7,19},{8,20},{9,... | collective-permute-start | bytes 688136 | tf_op jit(solution)/shard_map/ppermute | solution.py:39
  58.1 7.2 %collective-permute-done.10.theirs = bf16[32,3584]{1,0:T(8,128)(2,1)S(1)} collective-permute-done((bf16[32,3584]{1,0:T(8,128)(2,1)S(1)}, bf16[32,3584]{1,0:T(8,128)(2,1)S(1)}, u32[]{:S(2)}, u32[]{:S(2)}) %collective-permute-start.10) | collective-permute-done | bytes 229408 | tf_op jit(solution)/shard_map/ppermute | solution.py:43
  65.2 3.1 %shard_map.106 = (f32[32,3712]{1,0:T(8,128)S(1)}, bf16[32,3712]{1,0:T(8,128)(2,1)S(1)}) custom-call(s32[2]{0:T(128)S(1)} %pad_add_fusion.place, bf16[32,3584]{1,0:T(8,128)(2,1)S(1)} %collective-permute-done.5.mine, bf16[32,3584]{1,0:T(8,128)(2,1)S(1)} %collective-permute-done.10.theirs, bf16[8,2,2,2,16,256]{5,4,3,2,1,0:T(8,128)(2,1)S(1)} %get-tuple-element.113.refs_0_, ...), custom_call_target="tpu_custom_call" | custom-call | flops 2000000000 | bytes 1000 | tf_op jit(solution)/shard_map/pallas_call | solution.py:343
  68.4 3.0 %collective-permute-done.11.low = bf16[32,3584]{1,0:T(8,128)(2,1)S(1)} collective-permute-done((bf16[32,3584]{1,0:T(8,128)(2,1)S(1)}, bf16[32,3584]{1,0:T(8,128)(2,1)S(1)}, u32[]{:S(2)}, u32[]{:S(2)}) %collective-permute-start.11) | collective-permute-done | bytes 229408 | tf_op jit(solution)/shard_map/ppermute | solution.py:39
  71.3 3.4 %collective-permute-done.12.high = bf16[32,3584]{1,0:T(8,128)(2,1)S(1)} collective-permute-done((bf16[32,3584]{1,0:T(8,128)(2,1)S(1)}, bf16[32,3584]{1,0:T(8,128)(2,1)S(1)}, u32[]{:S(2)}, u32[]{:S(2)}) %collective-permute-start.12) | collective-permute-done | bytes 229408 | tf_op jit(solution)/shard_map/ppermute | solution.py:39
  78.3 2.8 %collective-permute-start.15 = (bf16[32,3584]{1,0:T(8,128)(2,1)S(1)}, bf16[32,3584]{1,0:T(8,128)(2,1)S(1)}, u32[]{:S(2)}, u32[]{:S(2)}) collective-permute-start(bf16[32,3584]{1,0:T(8,128)(2,1)S(1)} %get-tuple-element.140), channel_id=1, source_target_pairs={{0,24},{1,25},{2,26},{3,27},{4,28},{5,29},{6,30},{7,31},{8,0},{9,1... | collective-permute-start | bytes 688136 | tf_op jit(solution)/shard_map/ppermute | solution.py:39
  81.1 5.4 %collective-permute-done.13.theirs = bf16[64,3584]{1,0:T(8,128)(2,1)S(1)} collective-permute-done((bf16[64,3584]{1,0:T(8,128)(2,1)S(1)}, bf16[64,3584]{1,0:T(8,128)(2,1)S(1)}, u32[]{:S(2)}, u32[]{:S(2)}) %collective-permute-start.13) | collective-permute-done | bytes 458784 | tf_op jit(solution)/shard_map/ppermute | solution.py:43
  86.5 2.9 %shard_map.108 = (f32[64,3712]{1,0:T(8,128)S(1)}, bf16[64,3712]{1,0:T(8,128)(2,1)S(1)}) custom-call(s32[2]{0:T(128)S(1)} %pad_add_fusion.place, bf16[64,3584]{1,0:T(8,128)(2,1)S(1)} %shard_map.107.mine, bf16[64,3584]{1,0:T(8,128)(2,1)S(1)} %collective-permute-done.13.theirs, bf16[8,2,2,2,16,256]{5,4,3,2,1,0:T(8,128)(2,1)S(1)} %get-tuple-element.113.refs_0_, ...), custom_call_target="tpu_custom_call" | custom-call | flops 2000000000 | bytes 1000 | tf_op jit(solution)/shard_map/pallas_call | solution.py:343
  95.3 3.3 %collective-permute-start.19 = (bf16[32,3712]{1,0:T(8,128)(2,1)S(1)}, bf16[32,3712]{1,0:T(8,128)(2,1)S(1)}, u32[]{:S(2)}, u32[]{:S(2)}) collective-permute-start(bf16[32,3712]{1,0:T(8,128)(2,1)S(1)} %get-tuple-element.153), channel_id=1, source_target_pairs={{0,16},{1,17},{2,18},{3,19},{4,20},{5,21},{6,22},{7,23},{8,24},{9,... | collective-permute-start | bytes 712712 | tf_op jit(solution)/shard_map/ppermute | solution.py:39
  98.7 3.1 %shard_map.112 = (f32[32,3712]{1,0:T(8,128)S(1)}, bf16[32,3712]{1,0:T(8,128)(2,1)S(1)}) custom-call(s32[2]{0:T(128)S(1)} %pad_add_fusion.place, bf16[32,3584]{1,0:T(8,128)(2,1)S(1)} %get-tuple-element.160.mine, bf16[32,3584]{1,0:T(8,128)(2,1)S(1)} %collective-permute-done.2.theirs, bf16[8,2,2,2,16,256]{5,4,3,2,1,0:T(8,128)(2,1)S(1)} %get-tuple-element.113.refs_0_, ...), custom_call_target="tpu_custom_call" | custom-call | flops 2000000000 | bytes 1000 | tf_op jit(solution)/shard_map/pallas_call | solution.py:343
  101.8 2.6 %collective-permute-done.21.theirs = bf16[64,3584]{1,0:T(8,128)(2,1)S(1)} collective-permute-done((bf16[64,3584]{1,0:T(8,128)(2,1)S(1)}, bf16[64,3584]{1,0:T(8,128)(2,1)S(1)}, u32[]{:S(2)}, u32[]{:S(2)}) %collective-permute-start.21) | collective-permute-done | bytes 458784 | tf_op jit(solution)/shard_map/ppermute | solution.py:43
  104.4 2.9 %shard_map.111 = (f32[64,3712]{1,0:T(8,128)S(1)}, bf16[64,3712]{1,0:T(8,128)(2,1)S(1)}) custom-call(s32[2]{0:T(128)S(1)} %pad_add_fusion.place, bf16[64,3584]{1,0:T(8,128)(2,1)S(1)} %shard_map.110.mine, bf16[64,3584]{1,0:T(8,128)(2,1)S(1)} %collective-permute-done.21.theirs, bf16[8,2,2,2,16,256]{5,4,3,2,1,0:T(8,128)(2,1)S(1)} %get-tuple-element.113.refs_0_, ...), custom_call_target="tpu_custom_call" | custom-call | flops 2000000000 | bytes 1000 | tf_op jit(solution)/shard_map/pallas_call | solution.py:343
  107.4 4.4 %collective-permute-done.20.got = bf16[64,3712]{1,0:T(8,128)(2,1)S(1)} collective-permute-done((bf16[64,3712]{1,0:T(8,128)(2,1)S(1)}, bf16[64,3712]{1,0:T(8,128)(2,1)S(1)}, u32[]{:S(2)}, u32[]{:S(2)}) %collective-permute-start.20) | collective-permute-done | bytes 475168 | tf_op jit(solution)/shard_map/ppermute | solution.py:43
  114.0 4.8 %collective-permute-start.26 = (bf16[32,3712]{1,0:T(8,128)(2,1)S(1)}, bf16[32,3712]{1,0:T(8,128)(2,1)S(1)}, u32[]{:S(2)}, u32[]{:S(2)}) collective-permute-start(bf16[32,3712]{1,0:T(8,128)(2,1)S(1)} %get-tuple-element.177), channel_id=1, source_target_pairs={{0,20},{1,21},{2,22},{3,23},{4,24},{5,25},{6,26},{7,27},{8,28},{9,... | collective-permute-start | bytes 712712 | tf_op jit(solution)/shard_map/ppermute | solution.py:39
  119.1 3.8 %collective-permute-done.22.got = bf16[64,3712]{1,0:T(8,128)(2,1)S(1)} collective-permute-done((bf16[64,3712]{1,0:T(8,128)(2,1)S(1)}, bf16[64,3712]{1,0:T(8,128)(2,1)S(1)}, u32[]{:S(2)}, u32[]{:S(2)}) %collective-permute-start.22) | collective-permute-done | bytes 475168 | tf_op jit(solution)/shard_map/ppermute | solution.py:43
  123.1 5.0 %collective-permute-start.23 = (bf16[32,3712]{1,0:T(8,128)(2,1)S(1)}, bf16[32,3712]{1,0:T(8,128)(2,1)S(1)}, u32[]{:S(2)}, u32[]{:S(2)}) collective-permute-start(bf16[32,3712]{1,0:T(8,128)(2,1)S(1)} %get-tuple-element.168), channel_id=1, source_target_pairs={{0,24},{1,25},{2,26},{3,27},{4,28},{5,29},{6,30},{7,31},{8,0},{9,1... | collective-permute-start | bytes 712712 | tf_op jit(solution)/shard_map/ppermute | solution.py:39
  129.7 6.6 %collective-permute-done.26.b3 = bf16[32,3712]{1,0:T(8,128)(2,1)S(1)} collective-permute-done((bf16[32,3712]{1,0:T(8,128)(2,1)S(1)}, bf16[32,3712]{1,0:T(8,128)(2,1)S(1)}, u32[]{:S(2)}, u32[]{:S(2)}) %collective-permute-start.26) | collective-permute-done | bytes 237600 | tf_op jit(solution)/shard_map/ppermute | solution.py:39
  136.7 4.9 %collective-permute-done.23.b2 = bf16[32,3712]{1,0:T(8,128)(2,1)S(1)} collective-permute-done((bf16[32,3712]{1,0:T(8,128)(2,1)S(1)}, bf16[32,3712]{1,0:T(8,128)(2,1)S(1)}, u32[]{:S(2)}, u32[]{:S(2)}) %collective-permute-start.23) | collective-permute-done | bytes 237600 | tf_op jit(solution)/shard_map/ppermute | solution.py:39
  141.7 3.4 %collective-permute-done.24.b6 = bf16[32,3712]{1,0:T(8,128)(2,1)S(1)} collective-permute-done((bf16[32,3712]{1,0:T(8,128)(2,1)S(1)}, bf16[32,3712]{1,0:T(8,128)(2,1)S(1)}, u32[]{:S(2)}, u32[]{:S(2)}) %collective-permute-start.24) | collective-permute-done | bytes 237600 | tf_op jit(solution)/shard_map/ppermute | solution.py:39
  (74 shorter events, 41.6 us)
Async XLA Ops:
  1.7 18.7 %collective-permute-start = (bf16[64,3584]{1,0:T(8,128)(2,1)S(1)}, bf16[64,3584]{1,0:T(8,128)(2,1)S(1)}, u32[]{:S(2)}, u32[]{:S(2)}) collective-permute-start(bf16[64,3584]{1,0:T(8,128)(2,1)S(1)} %get-tuple-element.95), channel_id=1, source_target_pairs={{0,224},{32,0},{64,32},{96,64},{128,96},{160,128},{192,160},{224,1... | collective-permute-start | bytes 1376264 | tf_op jit(solution)/shard_map/ppermute | solution.py:34
  7.3 15.6 %collective-permute-start.1 = (bf16[64,3584]{1,0:T(8,128)(2,1)S(1)}, bf16[64,3584]{1,0:T(8,128)(2,1)S(1)}, u32[]{:S(2)}, u32[]{:S(2)}) collective-permute-start(bf16[64,3584]{1,0:T(8,128)(2,1)S(1)} %get-tuple-element.96), channel_id=1, source_target_pairs={{0,32},{32,64},{64,96},{96,128},{128,160},{160,192},{192,224},{224... | collective-permute-start | bytes 1376264 | tf_op jit(solution)/shard_map/ppermute | solution.py:34
  22.9 22.7 %collective-permute-start.8 = (bf16[768,3584]{1,0:T(8,128)(2,1)}, bf16[768,3584]{1,0:T(8,128)(2,1)S(1)}, u32[]{:S(2)}, u32[]{:S(2)}) collective-permute-start(bf16[768,3584]{1,0:T(8,128)(2,1)} %copy-done), channel_id=1, source_target_pairs={{0,1},{1,0},{2,3},{3,2},{4,5},{5,4},{6,7},{7,6},{8,9},{9,8},{10,11... | collective-permute-start | bytes 16515080 | tf_op jit(solution)/shard_map/ppermute | solution.py:47
  26.2 13.9 %collective-permute-start.7 = (bf16[8,2,2,2,16,256]{5,4,3,2,1,0:T(8,128)(2,1)S(1)}, bf16[8,2,2,2,16,256]{5,4,3,2,1,0:T(8,128)(2,1)S(1)}, u32[]{:S(2)}, u32[]{:S(2)}) collective-permute-start(bf16[8,2,2,2,16,256]{5,4,3,2,1,0:T(8,128)(2,1)S(1)} %get-tuple-element.114), channel_id=1, source_target_pairs={{0,1},{1,0},{2,3},{3,2},{4,5},{5,4},{6,7},{7,6},{8,9},{9,8},{10,11... | collective-permute-start | bytes 1572872 | tf_op jit(solution)/shard_map/ppermute | solution.py:47
  33.5 12.1 %collective-permute-start.6 = (bf16[64,3584]{1,0:T(8,128)(2,1)S(1)}, bf16[64,3584]{1,0:T(8,128)(2,1)S(1)}, u32[]{:S(2)}, u32[]{:S(2)}) collective-permute-start(bf16[64,3584]{1,0:T(8,128)(2,1)S(1)} %shard_map.104.mine), channel_id=1, source_target_pairs={{0,2},{1,3},{2,0},{3,1},{4,6},{5,7},{6,4},{7,5},{8,10},{9,11},{10,... | collective-permute-start | bytes 1376264 | tf_op jit(solution)/shard_map/ppermute | solution.py:43
  34.2 14.4 %collective-permute-start.5 = (bf16[32,3584]{1,0:T(8,128)(2,1)S(1)}, bf16[32,3584]{1,0:T(8,128)(2,1)S(1)}, u32[]{:S(2)}, u32[]{:S(2)}) collective-permute-start(bf16[32,3584]{1,0:T(8,128)(2,1)S(1)} %get-tuple-element.110), channel_id=1, source_target_pairs={{0,16},{1,17},{2,18},{3,19},{4,20},{5,21},{6,22},{7,23},{8,24},{9,... | collective-permute-start | bytes 688136 | tf_op jit(solution)/shard_map/ppermute | solution.py:39
  48.6 26.2 %collective-permute-start.9 = (bf16[64,3712]{1,0:T(8,128)(2,1)S(1)}, bf16[64,3712]{1,0:T(8,128)(2,1)S(1)}, u32[]{:S(2)}, u32[]{:S(2)}) collective-permute-start(bf16[64,3712]{1,0:T(8,128)(2,1)S(1)} %get-tuple-element.124), channel_id=1, source_target_pairs={{0,2},{1,3},{2,0},{3,1},{4,6},{5,7},{6,4},{7,5},{8,10},{9,11},{10,... | collective-permute-start | bytes 1425416 | tf_op jit(solution)/shard_map/ppermute | solution.py:43
  49.4 15.8 %collective-permute-start.10 = (bf16[32,3584]{1,0:T(8,128)(2,1)S(1)}, bf16[32,3584]{1,0:T(8,128)(2,1)S(1)}, u32[]{:S(2)}, u32[]{:S(2)}) collective-permute-start(bf16[32,3584]{1,0:T(8,128)(2,1)S(1)} %collective-permute-done.5.mine), channel_id=1, source_target_pairs={{0,2},{1,3},{2,0},{3,1},{4,6},{5,7},{6,4},{7,5},{8,10},{9,11},{10,... | collective-permute-start | bytes 688136 | tf_op jit(solution)/shard_map/ppermute | solution.py:43
  50.9 20.5 %collective-permute-start.11 = (bf16[32,3584]{1,0:T(8,128)(2,1)S(1)}, bf16[32,3584]{1,0:T(8,128)(2,1)S(1)}, u32[]{:S(2)}, u32[]{:S(2)}) collective-permute-start(bf16[32,3584]{1,0:T(8,128)(2,1)S(1)} %get-tuple-element.129), channel_id=1, source_target_pairs={{0,12},{1,13},{2,14},{3,15},{4,16},{5,17},{6,18},{7,19},{8,20},{9,... | collective-permute-start | bytes 688136 | tf_op jit(solution)/shard_map/ppermute | solution.py:39
  58.1 16.7 %collective-permute-start.12 = (bf16[32,3584]{1,0:T(8,128)(2,1)S(1)}, bf16[32,3584]{1,0:T(8,128)(2,1)S(1)}, u32[]{:S(2)}, u32[]{:S(2)}) collective-permute-start(bf16[32,3584]{1,0:T(8,128)(2,1)S(1)} %get-tuple-element.130), channel_id=1, source_target_pairs={{0,20},{1,21},{2,22},{3,23},{4,24},{5,25},{6,26},{7,27},{8,28},{9,... | collective-permute-start | bytes 688136 | tf_op jit(solution)/shard_map/ppermute | solution.py:39
  74.8 11.7 %collective-permute-start.13 = (bf16[64,3584]{1,0:T(8,128)(2,1)S(1)}, bf16[64,3584]{1,0:T(8,128)(2,1)S(1)}, u32[]{:S(2)}, u32[]{:S(2)}) collective-permute-start(bf16[64,3584]{1,0:T(8,128)(2,1)S(1)} %shard_map.107.mine), channel_id=1, source_target_pairs={{0,2},{1,3},{2,0},{3,1},{4,6},{5,7},{6,4},{7,5},{8,10},{9,11},{10,... | collective-permute-start | bytes 1376264 | tf_op jit(solution)/shard_map/ppermute | solution.py:43
  76.4 14.4 %collective-permute-start.16 = (bf16[32,3712]{1,0:T(8,128)(2,1)S(1)}, bf16[32,3712]{1,0:T(8,128)(2,1)S(1)}, u32[]{:S(2)}, u32[]{:S(2)}) collective-permute-start(bf16[32,3712]{1,0:T(8,128)(2,1)S(1)} %get-tuple-element.141), channel_id=1, source_target_pairs={{0,2},{1,3},{2,0},{3,1},{4,6},{5,7},{6,4},{7,5},{8,10},{9,11},{10,... | collective-permute-start | bytes 712712 | tf_op jit(solution)/shard_map/ppermute | solution.py:43
  76.9 12.5 %collective-permute-start.14 = (bf16[32,3584]{1,0:T(8,128)(2,1)S(1)}, bf16[32,3584]{1,0:T(8,128)(2,1)S(1)}, u32[]{:S(2)}, u32[]{:S(2)}) collective-permute-start(bf16[32,3584]{1,0:T(8,128)(2,1)S(1)} %get-tuple-element.139), channel_id=1, source_target_pairs={{0,8},{1,9},{2,10},{3,11},{4,12},{5,13},{6,14},{7,15},{8,16},{9,17... | collective-permute-start | bytes 688136 | tf_op jit(solution)/shard_map/ppermute | solution.py:39
  78.3 12.5 %collective-permute-start.15 = (bf16[32,3584]{1,0:T(8,128)(2,1)S(1)}, bf16[32,3584]{1,0:T(8,128)(2,1)S(1)}, u32[]{:S(2)}, u32[]{:S(2)}) collective-permute-start(bf16[32,3584]{1,0:T(8,128)(2,1)S(1)} %get-tuple-element.140), channel_id=1, source_target_pairs={{0,24},{1,25},{2,26},{3,27},{4,28},{5,29},{6,30},{7,31},{8,0},{9,1... | collective-permute-start | bytes 688136 | tf_op jit(solution)/shard_map/ppermute | solution.py:39
  90.9 13.5 %collective-permute-start.21 = (bf16[64,3584]{1,0:T(8,128)(2,1)S(1)}, bf16[64,3584]{1,0:T(8,128)(2,1)S(1)}, u32[]{:S(2)}, u32[]{:S(2)}) collective-permute-start(bf16[64,3584]{1,0:T(8,128)(2,1)S(1)} %shard_map.110.mine), channel_id=1, source_target_pairs={{0,2},{1,3},{2,0},{3,1},{4,6},{5,7},{6,4},{7,5},{8,10},{9,11},{10,... | collective-permute-start | bytes 1376264 | tf_op jit(solution)/shard_map/ppermute | solution.py:43
  91.5 20.3 %collective-permute-start.20 = (bf16[64,3712]{1,0:T(8,128)(2,1)S(1)}, bf16[64,3712]{1,0:T(8,128)(2,1)S(1)}, u32[]{:S(2)}, u32[]{:S(2)}) collective-permute-start(bf16[64,3712]{1,0:T(8,128)(2,1)S(1)} %get-tuple-element.154), channel_id=1, source_target_pairs={{0,2},{1,3},{2,0},{3,1},{4,6},{5,7},{6,4},{7,5},{8,10},{9,11},{10,... | collective-permute-start | bytes 1425416 | tf_op jit(solution)/shard_map/ppermute | solution.py:43
  93.2 14.1 %collective-permute-start.17 = (bf16[32,3712]{1,0:T(8,128)(2,1)S(1)}, bf16[32,3712]{1,0:T(8,128)(2,1)S(1)}, u32[]{:S(2)}, u32[]{:S(2)}) collective-permute-start(bf16[32,3712]{1,0:T(8,128)(2,1)S(1)} %get-tuple-element.151), channel_id=1, source_target_pairs={{0,28},{1,29},{2,30},{3,31},{4,0},{5,1},{6,2},{7,3},{8,4},{9,5},{1... | collective-permute-start | bytes 712712 | tf_op jit(solution)/shard_map/ppermute | solution.py:39
  93.3 14.1 %collective-permute-start.18 = (bf16[32,3712]{1,0:T(8,128)(2,1)S(1)}, bf16[32,3712]{1,0:T(8,128)(2,1)S(1)}, u32[]{:S(2)}, u32[]{:S(2)}) collective-permute-start(bf16[32,3712]{1,0:T(8,128)(2,1)S(1)} %get-tuple-element.152), channel_id=1, source_target_pairs={{0,4},{1,5},{2,6},{3,7},{4,8},{5,9},{6,10},{7,11},{8,12},{9,13},{1... | collective-permute-start | bytes 712712 | tf_op jit(solution)/shard_map/ppermute | solution.py:39
  95.3 12.1 %collective-permute-start.19 = (bf16[32,3712]{1,0:T(8,128)(2,1)S(1)}, bf16[32,3712]{1,0:T(8,128)(2,1)S(1)}, u32[]{:S(2)}, u32[]{:S(2)}) collective-permute-start(bf16[32,3712]{1,0:T(8,128)(2,1)S(1)} %get-tuple-element.153), channel_id=1, source_target_pairs={{0,16},{1,17},{2,18},{3,19},{4,20},{5,21},{6,22},{7,23},{8,24},{9,... | collective-permute-start | bytes 712712 | tf_op jit(solution)/shard_map/ppermute | solution.py:39
  112.1 17.5 %collective-permute-start.25 = (bf16[32,3712]{1,0:T(8,128)(2,1)S(1)}, bf16[32,3712]{1,0:T(8,128)(2,1)S(1)}, u32[]{:S(2)}, u32[]{:S(2)}) collective-permute-start(bf16[32,3712]{1,0:T(8,128)(2,1)S(1)} %get-tuple-element.171), channel_id=1, source_target_pairs={{0,2},{1,3},{2,0},{3,1},{4,6},{5,7},{6,4},{7,5},{8,10},{9,11},{10,... | collective-permute-start | bytes 712712 | tf_op jit(solution)/shard_map/ppermute | solution.py:43
  114.0 22.3 %collective-permute-start.26 = (bf16[32,3712]{1,0:T(8,128)(2,1)S(1)}, bf16[32,3712]{1,0:T(8,128)(2,1)S(1)}, u32[]{:S(2)}, u32[]{:S(2)}) collective-permute-start(bf16[32,3712]{1,0:T(8,128)(2,1)S(1)} %get-tuple-element.177), channel_id=1, source_target_pairs={{0,20},{1,21},{2,22},{3,23},{4,24},{5,25},{6,26},{7,27},{8,28},{9,... | collective-permute-start | bytes 712712 | tf_op jit(solution)/shard_map/ppermute | solution.py:39
  118.8 17.5 %collective-permute-start.27 = (bf16[32,3712]{1,0:T(8,128)(2,1)S(1)}, bf16[32,3712]{1,0:T(8,128)(2,1)S(1)}, u32[]{:S(2)}, u32[]{:S(2)}) collective-permute-start(bf16[32,3712]{1,0:T(8,128)(2,1)S(1)} %get-tuple-element.178), channel_id=1, source_target_pairs={{0,12},{1,13},{2,14},{3,15},{4,16},{5,17},{6,18},{7,19},{8,20},{9,... | collective-permute-start | bytes 712712 | tf_op jit(solution)/shard_map/ppermute | solution.py:39
  123.1 18.6 %collective-permute-start.23 = (bf16[32,3712]{1,0:T(8,128)(2,1)S(1)}, bf16[32,3712]{1,0:T(8,128)(2,1)S(1)}, u32[]{:S(2)}, u32[]{:S(2)}) collective-permute-start(bf16[32,3712]{1,0:T(8,128)(2,1)S(1)} %get-tuple-element.168), channel_id=1, source_target_pairs={{0,24},{1,25},{2,26},{3,27},{4,28},{5,29},{6,30},{7,31},{8,0},{9,1... | collective-permute-start | bytes 712712 | tf_op jit(solution)/shard_map/ppermute | solution.py:39
  128.1 17.0 %collective-permute-start.24 = (bf16[32,3712]{1,0:T(8,128)(2,1)S(1)}, bf16[32,3712]{1,0:T(8,128)(2,1)S(1)}, u32[]{:S(2)}, u32[]{:S(2)}) collective-permute-start(bf16[32,3712]{1,0:T(8,128)(2,1)S(1)} %get-tuple-element.169), channel_id=1, source_target_pairs={{0,8},{1,9},{2,10},{3,11},{4,12},{5,13},{6,14},{7,15},{8,16},{9,17... | collective-permute-start | bytes 712712 | tf_op jit(solution)/shard_map/ppermute | solution.py:39
  (15 other events, 88.2 us)

commit v3 on v2

--- a/solution.py
+++ b/solution.py
@@ -23,6 +23,7 @@
 NT = (((1,), (1,)), ((), ()))
 TN = (((0,), (0,)), ((), ()))
 COST = 100_000
+SLOW = 20_000_000_000
 WORK = 2_000_000_000
 LIMIT = 16 * 1024 * 1024
 
@@ -350,8 +351,8 @@
             compiler_params=pltpu.CompilerParams(vmem_limit_bytes=LIMIT),
         )(place, mine, theirs, pre_own, pre_other, *weights)
 
-    def add(group, own, got):
-        return call(add_kernel, tuple(shape((UNIT, WIDE)) for _ in group), [VMEM] * 2, COST, 1000)(
+    def add(group, own, got, cost=COST):
+        return call(add_kernel, tuple(shape((UNIT, WIDE)) for _ in group), [VMEM] * 2, cost, 1000)(
             own, got
         )
 
@@ -373,7 +374,7 @@
 
     z_out(1, 7)
     v["t0"] = x_swap(v["u0"])
-    tie("t0", "u0", "m1", "m7", "u4", "u3", "u5", "u2", "u6")
+    tie("m1", "m7", "u4", "u3", "u5", "u2", "u6", "t0", "u0")
     z_out(4)
     v["p1"] = pack(v["m1"], v["m7"])
     v["t1"] = x_swap(v["p1"])
@@ -399,10 +400,10 @@
     v["got3"] = x_swap(v["away3"])
     v["own2"], v["away2"] = work((2, 6), v["p2"], v["t2"])
     v["own0"], v["away0"] = work((0,), v["u0"], v["t0"])
-    tie("b1", "b7", "b4", "got3", "own3", "own2", "away2", "own0", "away0")
-    v["d3"], v["d5"] = add((3, 5), v["own3"], v["got3"])
+    v["got2"] = x_swap(v["away2"])
+    tie("b1", "b7", "b4", "got3", "own3", "own2", "own0", "away0")
+    v["d3"], v["d5"] = add((3, 5), v["own3"], v["got3"], SLOW)
     z_back(3, 5)
-    v["got2"] = x_swap(v["away2"])
     v["got0"] = x_swap(v["away0"])
     tie("got2", "own2")
     v["d2"], v["d6"] = add((2, 6), v["own2"], v["got2"])

time: 147 us -> 146 us (level)
  starting transfers between devices: 51.9 us -> 49.3 us
    ppermute x14, starting transfers between devices: 36.5 us -> 35 us  [z_shift(): return lax.ppermute(value, 'expert', pairs)]
where the time goes in v3:
time: 146 us
  waiting for transfers between devices  62.5 us (43%)
  starting transfers between devices  49.3 us (34%)
  Pallas kernels  23.1 us (16%)
  local copies, waits for them, and re-layouts  10.6 us (7%)
    ppermute x14, starting transfers between devices, z_shift(): return lax.ppermute(value, 'expert', pairs)  35 us
    ppermute x14, waiting for transfers between devices, z_shift(): return lax.ppermute(value, 'expert', pairs)  30.1 us
    ppermute x10, waiting for transfers between devices, x_swap(): return lax.ppermute(value, 'expert', [(i, i ^ 2) for i in range(32)])  30 us
    pallas_call x5, Pallas kernels, work(): pl.pallas_call(functools.partial(unit_kernel, group), out_shape=(shape((U...  15.1 us
    ppermute x10, starting transfers between devices, x_swap(): return lax.ppermute(value, 'expert', [(i, i ^ 2) for i in range(32)])  8.76 us
    unnamed x22, local copies, waits for them, and re-layouts  8.11 us
    ppermute x2, starting transfers between devices, pipe_shift(): return lax.ppermute(value, 'pipe', [(i, (i + by) % 8) for i in range(8)])  5.55 us
  transfers between devices with their start and end apart: 28, of which 15 were waited for; matrix products, arithmetic and copies ran while one was open for 2% of the time, Pallas kernels for 14%

profile of v3, /device:TPU:32, one launch (start us, length us, event | category | flops | bytes accessed | tf_op | source)
XLA Modules:
  0.0 145.8 jit_solution(9018982901133273637)
XLA Ops:
  1.7 5.6 %collective-permute-start = (bf16[64,3584]{1,0:T(8,128)(2,1)S(1)}, bf16[64,3584]{1,0:T(8,128)(2,1)S(1)}, u32[]{:S(2)}, u32[]{:S(2)}) collective-permute-start(bf16[64,3584]{1,0:T(8,128)(2,1)S(1)} %get-tuple-element.94), channel_id=1, source_target_pairs={{0,224},{32,0},{64,32},{96,64},{128,96},{160,128},{192,160},{224,1... | collective-permute-start | bytes 1376264 | tf_op jit(solution)/shard_map/ppermute | solution.py:35
  26.2 5.4 %collective-permute-done.2.low = bf16[32,3584]{1,0:T(8,128)(2,1)S(1)} collective-permute-done((bf16[32,3584]{1,0:T(8,128)(2,1)S(1)}, bf16[32,3584]{1,0:T(8,128)(2,1)S(1)}, u32[]{:S(2)}, u32[]{:S(2)}) %collective-permute-start.2) | collective-permute-done | bytes 229408 | tf_op jit(solution)/shard_map/ppermute | solution.py:40
  34.2 5.9 %collective-permute-start.5 = (bf16[32,3584]{1,0:T(8,128)(2,1)S(1)}, bf16[32,3584]{1,0:T(8,128)(2,1)S(1)}, u32[]{:S(2)}, u32[]{:S(2)}) collective-permute-start(bf16[32,3584]{1,0:T(8,128)(2,1)S(1)} %get-tuple-element.109), channel_id=1, source_target_pairs={{0,16},{1,17},{2,18},{3,19},{4,20},{5,21},{6,22},{7,23},{8,24},{9,... | collective-permute-start | bytes 688136 | tf_op jit(solution)/shard_map/ppermute | solution.py:40
  40.1 5.5 %collective-permute-done.6.theirs = bf16[64,3584]{1,0:T(8,128)(2,1)S(1)} collective-permute-done((bf16[64,3584]{1,0:T(8,128)(2,1)S(1)}, bf16[64,3584]{1,0:T(8,128)(2,1)S(1)}, u32[]{:S(2)}, u32[]{:S(2)}) %collective-permute-start.6) | collective-permute-done | bytes 458784 | tf_op jit(solution)/shard_map/ppermute | solution.py:44
  45.6 2.9 %shard_map.105 = (f32[64,3712]{1,0:T(8,128)S(1)}, bf16[64,3712]{1,0:T(8,128)(2,1)S(1)}) custom-call(s32[2]{0:T(128)S(1)} %pad_add_fusion.place, bf16[64,3584]{1,0:T(8,128)(2,1)S(1)} %shard_map.104.mine, bf16[64,3584]{1,0:T(8,128)(2,1)S(1)} %collective-permute-done.6.theirs, bf16[8,2,2,2,16,256]{5,4,3,2,1,0:T(8,128)(2,1)S(1)} %get-tuple-element.112.refs_0_, ...), custom_call_target="tpu_custom_call" | custom-call | flops 2000000000 | bytes 1000 | tf_op jit(solution)/shard_map/pallas_call | solution.py:344
  50.9 7.2 %collective-permute-start.11 = (bf16[32,3584]{1,0:T(8,128)(2,1)S(1)}, bf16[32,3584]{1,0:T(8,128)(2,1)S(1)}, u32[]{:S(2)}, u32[]{:S(2)}) collective-permute-start(bf16[32,3584]{1,0:T(8,128)(2,1)S(1)} %get-tuple-element.128), channel_id=1, source_target_pairs={{0,12},{1,13},{2,14},{3,15},{4,16},{5,17},{6,18},{7,19},{8,20},{9,... | collective-permute-start | bytes 688136 | tf_op jit(solution)/shard_map/ppermute | solution.py:40
  58.1 7.2 %collective-permute-done.10.theirs = bf16[32,3584]{1,0:T(8,128)(2,1)S(1)} collective-permute-done((bf16[32,3584]{1,0:T(8,128)(2,1)S(1)}, bf16[32,3584]{1,0:T(8,128)(2,1)S(1)}, u32[]{:S(2)}, u32[]{:S(2)}) %collective-permute-start.10) | collective-permute-done | bytes 229408 | tf_op jit(solution)/shard_map/ppermute | solution.py:44
  65.2 3.1 %shard_map.106 = (f32[32,3712]{1,0:T(8,128)S(1)}, bf16[32,3712]{1,0:T(8,128)(2,1)S(1)}) custom-call(s32[2]{0:T(128)S(1)} %pad_add_fusion.place, bf16[32,3584]{1,0:T(8,128)(2,1)S(1)} %collective-permute-done.5.mine, bf16[32,3584]{1,0:T(8,128)(2,1)S(1)} %collective-permute-done.10.theirs, bf16[8,2,2,2,16,256]{5,4,3,2,1,0:T(8,128)(2,1)S(1)} %get-tuple-element.112.refs_0_, ...), custom_call_target="tpu_custom_call" | custom-call | flops 2000000000 | bytes 1000 | tf_op jit(solution)/shard_map/pallas_call | solution.py:344
  68.4 3.0 %collective-permute-done.11.low = bf16[32,3584]{1,0:T(8,128)(2,1)S(1)} collective-permute-done((bf16[32,3584]{1,0:T(8,128)(2,1)S(1)}, bf16[32,3584]{1,0:T(8,128)(2,1)S(1)}, u32[]{:S(2)}, u32[]{:S(2)}) %collective-permute-start.11) | collective-permute-done | bytes 229408 | tf_op jit(solution)/shard_map/ppermute | solution.py:40
  71.3 3.4 %collective-permute-done.12.high = bf16[32,3584]{1,0:T(8,128)(2,1)S(1)} collective-permute-done((bf16[32,3584]{1,0:T(8,128)(2,1)S(1)}, bf16[32,3584]{1,0:T(8,128)(2,1)S(1)}, u32[]{:S(2)}, u32[]{:S(2)}) %collective-permute-start.12) | collective-permute-done | bytes 229408 | tf_op jit(solution)/shard_map/ppermute | solution.py:40
  78.3 2.8 %collective-permute-start.15 = (bf16[32,3584]{1,0:T(8,128)(2,1)S(1)}, bf16[32,3584]{1,0:T(8,128)(2,1)S(1)}, u32[]{:S(2)}, u32[]{:S(2)}) collective-permute-start(bf16[32,3584]{1,0:T(8,128)(2,1)S(1)} %get-tuple-element.139), channel_id=1, source_target_pairs={{0,24},{1,25},{2,26},{3,27},{4,28},{5,29},{6,30},{7,31},{8,0},{9,1... | collective-permute-start | bytes 688136 | tf_op jit(solution)/shard_map/ppermute | solution.py:40
  81.1 5.4 %collective-permute-done.13.theirs = bf16[64,3584]{1,0:T(8,128)(2,1)S(1)} collective-permute-done((bf16[64,3584]{1,0:T(8,128)(2,1)S(1)}, bf16[64,3584]{1,0:T(8,128)(2,1)S(1)}, u32[]{:S(2)}, u32[]{:S(2)}) %collective-permute-start.13) | collective-permute-done | bytes 458784 | tf_op jit(solution)/shard_map/ppermute | solution.py:44
  86.5 2.9 %shard_map.108 = (f32[64,3712]{1,0:T(8,128)S(1)}, bf16[64,3712]{1,0:T(8,128)(2,1)S(1)}) custom-call(s32[2]{0:T(128)S(1)} %pad_add_fusion.place, bf16[64,3584]{1,0:T(8,128)(2,1)S(1)} %shard_map.107.mine, bf16[64,3584]{1,0:T(8,128)(2,1)S(1)} %collective-permute-done.13.theirs, bf16[8,2,2,2,16,256]{5,4,3,2,1,0:T(8,128)(2,1)S(1)} %get-tuple-element.112.refs_0_, ...), custom_call_target="tpu_custom_call" | custom-call | flops 2000000000 | bytes 1000 | tf_op jit(solution)/shard_map/pallas_call | solution.py:344
  95.3 3.3 %collective-permute-start.21 = (bf16[32,3712]{1,0:T(8,128)(2,1)S(1)}, bf16[32,3712]{1,0:T(8,128)(2,1)S(1)}, u32[]{:S(2)}, u32[]{:S(2)}) collective-permute-start(bf16[32,3712]{1,0:T(8,128)(2,1)S(1)} %get-tuple-element.155), channel_id=1, source_target_pairs={{0,16},{1,17},{2,18},{3,19},{4,20},{5,21},{6,22},{7,23},{8,24},{9,... | collective-permute-start | bytes 712712 | tf_op jit(solution)/shard_map/ppermute | solution.py:40
  98.7 3.1 %shard_map.112 = (f32[32,3712]{1,0:T(8,128)S(1)}, bf16[32,3712]{1,0:T(8,128)(2,1)S(1)}) custom-call(s32[2]{0:T(128)S(1)} %pad_add_fusion.place, bf16[32,3584]{1,0:T(8,128)(2,1)S(1)} %get-tuple-element.159.mine, bf16[32,3584]{1,0:T(8,128)(2,1)S(1)} %collective-permute-done.4.theirs, bf16[8,2,2,2,16,256]{5,4,3,2,1,0:T(8,128)(2,1)S(1)} %get-tuple-element.112.refs_0_, ...), custom_call_target="tpu_custom_call" | custom-call | flops 2000000000 | bytes 1000 | tf_op jit(solution)/shard_map/pallas_call | solution.py:344
  101.8 2.6 %collective-permute-done.17.theirs = bf16[64,3584]{1,0:T(8,128)(2,1)S(1)} collective-permute-done((bf16[64,3584]{1,0:T(8,128)(2,1)S(1)}, bf16[64,3584]{1,0:T(8,128)(2,1)S(1)}, u32[]{:S(2)}, u32[]{:S(2)}) %collective-permute-start.17) | collective-permute-done | bytes 458784 | tf_op jit(solution)/shard_map/ppermute | solution.py:44
  104.4 2.9 %shard_map.110 = (f32[64,3712]{1,0:T(8,128)S(1)}, bf16[64,3712]{1,0:T(8,128)(2,1)S(1)}) custom-call(s32[2]{0:T(128)S(1)} %pad_add_fusion.place, bf16[64,3584]{1,0:T(8,128)(2,1)S(1)} %shard_map.109.mine, bf16[64,3584]{1,0:T(8,128)(2,1)S(1)} %collective-permute-done.17.theirs, bf16[8,2,2,2,16,256]{5,4,3,2,1,0:T(8,128)(2,1)S(1)} %get-tuple-element.112.refs_0_, ...), custom_call_target="tpu_custom_call" | custom-call | flops 2000000000 | bytes 1000 | tf_op jit(solution)/shard_map/pallas_call | solution.py:344
  108.0 6.6 %collective-permute-done.22.got = bf16[64,3712]{1,0:T(8,128)(2,1)S(1)} collective-permute-done((bf16[64,3712]{1,0:T(8,128)(2,1)S(1)}, bf16[64,3712]{1,0:T(8,128)(2,1)S(1)}, u32[]{:S(2)}, u32[]{:S(2)}) %collective-permute-start.22) | collective-permute-done | bytes 475168 | tf_op jit(solution)/shard_map/ppermute | solution.py:44
  114.8 3.9 %collective-permute-start.26 = (bf16[32,3712]{1,0:T(8,128)(2,1)S(1)}, bf16[32,3712]{1,0:T(8,128)(2,1)S(1)}, u32[]{:S(2)}, u32[]{:S(2)}) collective-permute-start(bf16[32,3712]{1,0:T(8,128)(2,1)S(1)} %get-tuple-element.175), channel_id=1, source_target_pairs={{0,20},{1,21},{2,22},{3,23},{4,24},{5,25},{6,26},{7,27},{8,28},{9,... | collective-permute-start | bytes 712712 | tf_op jit(solution)/shard_map/ppermute | solution.py:40
  120.2 2.7 %collective-permute-done.18.got = bf16[64,3712]{1,0:T(8,128)(2,1)S(1)} collective-permute-done((bf16[64,3712]{1,0:T(8,128)(2,1)S(1)}, bf16[64,3712]{1,0:T(8,128)(2,1)S(1)}, u32[]{:S(2)}, u32[]{:S(2)}) %collective-permute-start.18) | collective-permute-done | bytes 475168 | tf_op jit(solution)/shard_map/ppermute | solution.py:44
  123.0 2.9 %collective-permute-start.23 = (bf16[32,3712]{1,0:T(8,128)(2,1)S(1)}, bf16[32,3712]{1,0:T(8,128)(2,1)S(1)}, u32[]{:S(2)}, u32[]{:S(2)}) collective-permute-start(bf16[32,3712]{1,0:T(8,128)(2,1)S(1)} %get-tuple-element.166), channel_id=1, source_target_pairs={{0,24},{1,25},{2,26},{3,27},{4,28},{5,29},{6,30},{7,31},{8,0},{9,1... | collective-permute-start | bytes 712712 | tf_op jit(solution)/shard_map/ppermute | solution.py:40
  128.1 5.7 %collective-permute-done.26.b3 = bf16[32,3712]{1,0:T(8,128)(2,1)S(1)} collective-permute-done((bf16[32,3712]{1,0:T(8,128)(2,1)S(1)}, bf16[32,3712]{1,0:T(8,128)(2,1)S(1)}, u32[]{:S(2)}, u32[]{:S(2)}) %collective-permute-start.26) | collective-permute-done | bytes 237600 | tf_op jit(solution)/shard_map/ppermute | solution.py:40
  134.2 6.3 %collective-permute-done.23.b2 = bf16[32,3712]{1,0:T(8,128)(2,1)S(1)} collective-permute-done((bf16[32,3712]{1,0:T(8,128)(2,1)S(1)}, bf16[32,3712]{1,0:T(8,128)(2,1)S(1)}, u32[]{:S(2)}, u32[]{:S(2)}) %collective-permute-start.23) | collective-permute-done | bytes 237600 | tf_op jit(solution)/shard_map/ppermute | solution.py:40
  140.5 3.1 %collective-permute-done.24.b6 = bf16[32,3712]{1,0:T(8,128)(2,1)S(1)} collective-permute-done((bf16[32,3712]{1,0:T(8,128)(2,1)S(1)}, bf16[32,3712]{1,0:T(8,128)(2,1)S(1)}, u32[]{:S(2)}, u32[]{:S(2)}) %collective-permute-start.24) | collective-permute-done | bytes 237600 | tf_op jit(solution)/shard_map/ppermute | solution.py:40
  (74 shorter events, 42.0 us)
Async XLA Ops:
  1.7 18.7 %collective-permute-start = (bf16[64,3584]{1,0:T(8,128)(2,1)S(1)}, bf16[64,3584]{1,0:T(8,128)(2,1)S(1)}, u32[]{:S(2)}, u32[]{:S(2)}) collective-permute-start(bf16[64,3584]{1,0:T(8,128)(2,1)S(1)} %get-tuple-element.94), channel_id=1, source_target_pairs={{0,224},{32,0},{64,32},{96,64},{128,96},{160,128},{192,160},{224,1... | collective-permute-start | bytes 1376264 | tf_op jit(solution)/shard_map/ppermute | solution.py:35
  7.3 15.6 %collective-permute-start.1 = (bf16[64,3584]{1,0:T(8,128)(2,1)S(1)}, bf16[64,3584]{1,0:T(8,128)(2,1)S(1)}, u32[]{:S(2)}, u32[]{:S(2)}) collective-permute-start(bf16[64,3584]{1,0:T(8,128)(2,1)S(1)} %get-tuple-element.95), channel_id=1, source_target_pairs={{0,32},{32,64},{64,96},{96,128},{128,160},{160,192},{192,224},{224... | collective-permute-start | bytes 1376264 | tf_op jit(solution)/shard_map/ppermute | solution.py:35
  22.9 22.7 %collective-permute-start.8 = (bf16[768,3584]{1,0:T(8,128)(2,1)}, bf16[768,3584]{1,0:T(8,128)(2,1)S(1)}, u32[]{:S(2)}, u32[]{:S(2)}) collective-permute-start(bf16[768,3584]{1,0:T(8,128)(2,1)} %copy-done), channel_id=1, source_target_pairs={{0,1},{1,0},{2,3},{3,2},{4,5},{5,4},{6,7},{7,6},{8,9},{9,8},{10,11... | collective-permute-start | bytes 16515080 | tf_op jit(solution)/shard_map/ppermute | solution.py:48
  26.2 13.9 %collective-permute-start.7 = (bf16[8,2,2,2,16,256]{5,4,3,2,1,0:T(8,128)(2,1)S(1)}, bf16[8,2,2,2,16,256]{5,4,3,2,1,0:T(8,128)(2,1)S(1)}, u32[]{:S(2)}, u32[]{:S(2)}) collective-permute-start(bf16[8,2,2,2,16,256]{5,4,3,2,1,0:T(8,128)(2,1)S(1)} %get-tuple-element.113), channel_id=1, source_target_pairs={{0,1},{1,0},{2,3},{3,2},{4,5},{5,4},{6,7},{7,6},{8,9},{9,8},{10,11... | collective-permute-start | bytes 1572872 | tf_op jit(solution)/shard_map/ppermute | solution.py:48
  33.5 12.1 %collective-permute-start.6 = (bf16[64,3584]{1,0:T(8,128)(2,1)S(1)}, bf16[64,3584]{1,0:T(8,128)(2,1)S(1)}, u32[]{:S(2)}, u32[]{:S(2)}) collective-permute-start(bf16[64,3584]{1,0:T(8,128)(2,1)S(1)} %shard_map.104.mine), channel_id=1, source_target_pairs={{0,2},{1,3},{2,0},{3,1},{4,6},{5,7},{6,4},{7,5},{8,10},{9,11},{10,... | collective-permute-start | bytes 1376264 | tf_op jit(solution)/shard_map/ppermute | solution.py:44
  34.2 14.4 %collective-permute-start.5 = (bf16[32,3584]{1,0:T(8,128)(2,1)S(1)}, bf16[32,3584]{1,0:T(8,128)(2,1)S(1)}, u32[]{:S(2)}, u32[]{:S(2)}) collective-permute-start(bf16[32,3584]{1,0:T(8,128)(2,1)S(1)} %get-tuple-element.109), channel_id=1, source_target_pairs={{0,16},{1,17},{2,18},{3,19},{4,20},{5,21},{6,22},{7,23},{8,24},{9,... | collective-permute-start | bytes 688136 | tf_op jit(solution)/shard_map/ppermute | solution.py:40
  48.6 26.2 %collective-permute-start.9 = (bf16[64,3712]{1,0:T(8,128)(2,1)S(1)}, bf16[64,3712]{1,0:T(8,128)(2,1)S(1)}, u32[]{:S(2)}, u32[]{:S(2)}) collective-permute-start(bf16[64,3712]{1,0:T(8,128)(2,1)S(1)} %get-tuple-element.123), channel_id=1, source_target_pairs={{0,2},{1,3},{2,0},{3,1},{4,6},{5,7},{6,4},{7,5},{8,10},{9,11},{10,... | collective-permute-start | bytes 1425416 | tf_op jit(solution)/shard_map/ppermute | solution.py:44
  49.4 15.8 %collective-permute-start.10 = (bf16[32,3584]{1,0:T(8,128)(2,1)S(1)}, bf16[32,3584]{1,0:T(8,128)(2,1)S(1)}, u32[]{:S(2)}, u32[]{:S(2)}) collective-permute-start(bf16[32,3584]{1,0:T(8,128)(2,1)S(1)} %collective-permute-done.5.mine), channel_id=1, source_target_pairs={{0,2},{1,3},{2,0},{3,1},{4,6},{5,7},{6,4},{7,5},{8,10},{9,11},{10,... | collective-permute-start | bytes 688136 | tf_op jit(solution)/shard_map/ppermute | solution.py:44
  50.9 20.5 %collective-permute-start.11 = (bf16[32,3584]{1,0:T(8,128)(2,1)S(1)}, bf16[32,3584]{1,0:T(8,128)(2,1)S(1)}, u32[]{:S(2)}, u32[]{:S(2)}) collective-permute-start(bf16[32,3584]{1,0:T(8,128)(2,1)S(1)} %get-tuple-element.128), channel_id=1, source_target_pairs={{0,12},{1,13},{2,14},{3,15},{4,16},{5,17},{6,18},{7,19},{8,20},{9,... | collective-permute-start | bytes 688136 | tf_op jit(solution)/shard_map/ppermute | solution.py:40
  58.1 16.7 %collective-permute-start.12 = (bf16[32,3584]{1,0:T(8,128)(2,1)S(1)}, bf16[32,3584]{1,0:T(8,128)(2,1)S(1)}, u32[]{:S(2)}, u32[]{:S(2)}) collective-permute-start(bf16[32,3584]{1,0:T(8,128)(2,1)S(1)} %get-tuple-element.129), channel_id=1, source_target_pairs={{0,20},{1,21},{2,22},{3,23},{4,24},{5,25},{6,26},{7,27},{8,28},{9,... | collective-permute-start | bytes 688136 | tf_op jit(solution)/shard_map/ppermute | solution.py:40
  76.4 14.4 %collective-permute-start.16 = (bf16[32,3712]{1,0:T(8,128)(2,1)S(1)}, bf16[32,3712]{1,0:T(8,128)(2,1)S(1)}, u32[]{:S(2)}, u32[]{:S(2)}) collective-permute-start(bf16[32,3712]{1,0:T(8,128)(2,1)S(1)} %get-tuple-element.140), channel_id=1, source_target_pairs={{0,2},{1,3},{2,0},{3,1},{4,6},{5,7},{6,4},{7,5},{8,10},{9,11},{10,... | collective-permute-start | bytes 712712 | tf_op jit(solution)/shard_map/ppermute | solution.py:44
  76.9 12.5 %collective-permute-start.14 = (bf16[32,3584]{1,0:T(8,128)(2,1)S(1)}, bf16[32,3584]{1,0:T(8,128)(2,1)S(1)}, u32[]{:S(2)}, u32[]{:S(2)}) collective-permute-start(bf16[32,3584]{1,0:T(8,128)(2,1)S(1)} %get-tuple-element.138), channel_id=1, source_target_pairs={{0,8},{1,9},{2,10},{3,11},{4,12},{5,13},{6,14},{7,15},{8,16},{9,17... | collective-permute-start | bytes 688136 | tf_op jit(solution)/shard_map/ppermute | solution.py:40
  78.3 12.5 %collective-permute-start.15 = (bf16[32,3584]{1,0:T(8,128)(2,1)S(1)}, bf16[32,3584]{1,0:T(8,128)(2,1)S(1)}, u32[]{:S(2)}, u32[]{:S(2)}) collective-permute-start(bf16[32,3584]{1,0:T(8,128)(2,1)S(1)} %get-tuple-element.139), channel_id=1, source_target_pairs={{0,24},{1,25},{2,26},{3,27},{4,28},{5,29},{6,30},{7,31},{8,0},{9,1... | collective-permute-start | bytes 688136 | tf_op jit(solution)/shard_map/ppermute | solution.py:40
  90.9 13.5 %collective-permute-start.17 = (bf16[64,3584]{1,0:T(8,128)(2,1)S(1)}, bf16[64,3584]{1,0:T(8,128)(2,1)S(1)}, u32[]{:S(2)}, u32[]{:S(2)}) collective-permute-start(bf16[64,3584]{1,0:T(8,128)(2,1)S(1)} %shard_map.109.mine), channel_id=1, source_target_pairs={{0,2},{1,3},{2,0},{3,1},{4,6},{5,7},{6,4},{7,5},{8,10},{9,11},{10,... | collective-permute-start | bytes 1376264 | tf_op jit(solution)/shard_map/ppermute | solution.py:44
  91.5 23.1 %collective-permute-start.22 = (bf16[64,3712]{1,0:T(8,128)(2,1)S(1)}, bf16[64,3712]{1,0:T(8,128)(2,1)S(1)}, u32[]{:S(2)}, u32[]{:S(2)}) collective-permute-start(bf16[64,3712]{1,0:T(8,128)(2,1)S(1)} %get-tuple-element.156), channel_id=1, source_target_pairs={{0,2},{1,3},{2,0},{3,1},{4,6},{5,7},{6,4},{7,5},{8,10},{9,11},{10,... | collective-permute-start | bytes 1425416 | tf_op jit(solution)/shard_map/ppermute | solution.py:44
  93.2 14.8 %collective-permute-start.19 = (bf16[32,3712]{1,0:T(8,128)(2,1)S(1)}, bf16[32,3712]{1,0:T(8,128)(2,1)S(1)}, u32[]{:S(2)}, u32[]{:S(2)}) collective-permute-start(bf16[32,3712]{1,0:T(8,128)(2,1)S(1)} %get-tuple-element.153), channel_id=1, source_target_pairs={{0,28},{1,29},{2,30},{3,31},{4,0},{5,1},{6,2},{7,3},{8,4},{9,5},{1... | collective-permute-start | bytes 712712 | tf_op jit(solution)/shard_map/ppermute | solution.py:40
  93.3 14.7 %collective-permute-start.20 = (bf16[32,3712]{1,0:T(8,128)(2,1)S(1)}, bf16[32,3712]{1,0:T(8,128)(2,1)S(1)}, u32[]{:S(2)}, u32[]{:S(2)}) collective-permute-start(bf16[32,3712]{1,0:T(8,128)(2,1)S(1)} %get-tuple-element.154), channel_id=1, source_target_pairs={{0,4},{1,5},{2,6},{3,7},{4,8},{5,9},{6,10},{7,11},{8,12},{9,13},{1... | collective-permute-start | bytes 712712 | tf_op jit(solution)/shard_map/ppermute | solution.py:40
  95.3 12.7 %collective-permute-start.21 = (bf16[32,3712]{1,0:T(8,128)(2,1)S(1)}, bf16[32,3712]{1,0:T(8,128)(2,1)S(1)}, u32[]{:S(2)}, u32[]{:S(2)}) collective-permute-start(bf16[32,3712]{1,0:T(8,128)(2,1)S(1)} %get-tuple-element.155), channel_id=1, source_target_pairs={{0,16},{1,17},{2,18},{3,19},{4,20},{5,21},{6,22},{7,23},{8,24},{9,... | collective-permute-start | bytes 712712 | tf_op jit(solution)/shard_map/ppermute | solution.py:40
  107.4 15.5 %collective-permute-start.18 = (bf16[64,3712]{1,0:T(8,128)(2,1)S(1)}, bf16[64,3712]{1,0:T(8,128)(2,1)S(1)}, u32[]{:S(2)}, u32[]{:S(2)}) collective-permute-start(bf16[64,3712]{1,0:T(8,128)(2,1)S(1)} %get-tuple-element.148), channel_id=1, source_target_pairs={{0,2},{1,3},{2,0},{3,1},{4,6},{5,7},{6,4},{7,5},{8,10},{9,11},{10,... | collective-permute-start | bytes 1425416 | tf_op jit(solution)/shard_map/ppermute | solution.py:44
  114.8 19.0 %collective-permute-start.26 = (bf16[32,3712]{1,0:T(8,128)(2,1)S(1)}, bf16[32,3712]{1,0:T(8,128)(2,1)S(1)}, u32[]{:S(2)}, u32[]{:S(2)}) collective-permute-start(bf16[32,3712]{1,0:T(8,128)(2,1)S(1)} %get-tuple-element.175), channel_id=1, source_target_pairs={{0,20},{1,21},{2,22},{3,23},{4,24},{5,25},{6,26},{7,27},{8,28},{9,... | collective-permute-start | bytes 712712 | tf_op jit(solution)/shard_map/ppermute | solution.py:40
  118.7 15.1 %collective-permute-start.27 = (bf16[32,3712]{1,0:T(8,128)(2,1)S(1)}, bf16[32,3712]{1,0:T(8,128)(2,1)S(1)}, u32[]{:S(2)}, u32[]{:S(2)}) collective-permute-start(bf16[32,3712]{1,0:T(8,128)(2,1)S(1)} %get-tuple-element.176), channel_id=1, source_target_pairs={{0,12},{1,13},{2,14},{3,15},{4,16},{5,17},{6,18},{7,19},{8,20},{9,... | collective-permute-start | bytes 712712 | tf_op jit(solution)/shard_map/ppermute | solution.py:40
  119.9 13.9 %collective-permute-start.25 = (bf16[32,3712]{1,0:T(8,128)(2,1)S(1)}, bf16[32,3712]{1,0:T(8,128)(2,1)S(1)}, u32[]{:S(2)}, u32[]{:S(2)}) collective-permute-start(bf16[32,3712]{1,0:T(8,128)(2,1)S(1)} %get-tuple-element.169), channel_id=1, source_target_pairs={{0,2},{1,3},{2,0},{3,1},{4,6},{5,7},{6,4},{7,5},{8,10},{9,11},{10,... | collective-permute-start | bytes 712712 | tf_op jit(solution)/shard_map/ppermute | solution.py:44
  123.0 17.4 %collective-permute-start.23 = (bf16[32,3712]{1,0:T(8,128)(2,1)S(1)}, bf16[32,3712]{1,0:T(8,128)(2,1)S(1)}, u32[]{:S(2)}, u32[]{:S(2)}) collective-permute-start(bf16[32,3712]{1,0:T(8,128)(2,1)S(1)} %get-tuple-element.166), channel_id=1, source_target_pairs={{0,24},{1,25},{2,26},{3,27},{4,28},{5,29},{6,30},{7,31},{8,0},{9,1... | collective-permute-start | bytes 712712 | tf_op jit(solution)/shard_map/ppermute | solution.py:40
  125.9 17.7 %collective-permute-start.24 = (bf16[32,3712]{1,0:T(8,128)(2,1)S(1)}, bf16[32,3712]{1,0:T(8,128)(2,1)S(1)}, u32[]{:S(2)}, u32[]{:S(2)}) collective-permute-start(bf16[32,3712]{1,0:T(8,128)(2,1)S(1)} %get-tuple-element.167), channel_id=1, source_target_pairs={{0,8},{1,9},{2,10},{3,11},{4,12},{5,13},{6,14},{7,15},{8,16},{9,17... | collective-permute-start | bytes 712712 | tf_op jit(solution)/shard_map/ppermute | solution.py:40
  (15 other events, 88.8 us)

commit v4 on v3

--- a/solution.py
+++ b/solution.py
@@ -339,7 +339,7 @@
         COST,
         1000,
     )(first, second, match, weight)
-    def work(group, mine, theirs):
+    def work(group, mine, theirs, cost=WORK):
         n = len(group)
         return pl.pallas_call(
             functools.partial(unit_kernel, group),
@@ -347,7 +347,7 @@
             in_specs=[SMEM] + [VMEM] * 6,
             out_specs=(VMEM, VMEM),
             scratch_shapes=[pltpu.VMEM((2 * UNIT * n, D), BF16)],
-            cost_estimate=pl.CostEstimate(flops=WORK, bytes_accessed=1000, transcendentals=0),
+            cost_estimate=pl.CostEstimate(flops=cost, bytes_accessed=1000, transcendentals=0),
             compiler_params=pltpu.CompilerParams(vmem_limit_bytes=LIMIT),
         )(place, mine, theirs, pre_own, pre_other, *weights)
 
@@ -379,11 +379,11 @@
     v["p1"] = pack(v["m1"], v["m7"])
     v["t1"] = x_swap(v["p1"])
     v["own1"], v["away1"] = work((1, 7), v["p1"], v["t1"])
-    tie("m4", "own1", "away1", "t0", "u0", "u3", "u5", "u2", "u6")
+    v["got1"] = x_swap(v["away1"])
+    tie("m4", "own1", "t0", "u0", "u3", "u5", "u2", "u6")
     z_out(3, 5)
     v["t4"] = x_swap(v["m4"])
-    v["got1"] = x_swap(v["away1"])
-    v["own4"], v["away4"] = work((4,), v["m4"], v["t4"])
+    v["own4"], v["away4"] = work((4,), v["m4"], v["t4"], SLOW)
     tie("got1", "own1", "own4", "away4", "m3", "m5", "t0", "u0", "u2", "u6")
     z_out(2, 6)
     v["p3"] = pack(v["m3"], v["m5"])

time: 146 us -> 145 us (level)
  waiting for transfers between devices: 62.5 us -> 58.4 us
  starting transfers between devices: 49.3 us -> 52.4 us
    ppermute x10, waiting for transfers between devices: 30 us -> 18.7 us  [x_swap(): return lax.ppermute(value, 'expert', [(i, i ^ 2) for i in range(32)])]
    ppermute x14, waiting for transfers between devices: 30.1 us -> 37.3 us  [z_shift(): return lax.ppermute(value, 'expert', pairs)]
    ppermute x14, starting transfers between devices: 35 us -> 37.4 us  [z_shift(): return lax.ppermute(value, 'expert', pairs)]
  transfers between devices with their start and end apart: 28 -> 28, of which waited for: 15 -> 16; matrix products, arithmetic and copies ran while one was open for 2% -> 2% of each run, Pallas kernels for 14% -> 14%
where the time goes in v4:
time: 145 us
  waiting for transfers between devices  58.4 us (40%)
  starting transfers between devices  52.4 us (36%)
  Pallas kernels  23.1 us (16%)
  local copies, waits for them, and re-layouts  10.6 us (7%)
    ppermute x14, starting transfers between devices, z_shift(): return lax.ppermute(value, 'expert', pairs)  37.4 us
    ppermute x14, waiting for transfers between devices, z_shift(): return lax.ppermute(value, 'expert', pairs)  37.3 us
    ppermute x10, waiting for transfers between devices, x_swap(): return lax.ppermute(value, 'expert', [(i, i ^ 2) for i in range(32)])  18.7 us
    pallas_call x5, Pallas kernels, work(): pl.pallas_call(functools.partial(unit_kernel, group), out_shape=(shape((U...  15.1 us
    ppermute x10, starting transfers between devices, x_swap(): return lax.ppermute(value, 'expert', [(i, i ^ 2) for i in range(32)])  9.47 us
    unnamed x22, local copies, waits for them, and re-layouts  8.11 us
    ppermute x2, starting transfers between devices, pipe_shift(): return lax.ppermute(value, 'pipe', [(i, (i + by) % 8) for i in range(8)])  5.55 us
  transfers between devices with their start and end apart: 28, of which 16 were waited for; matrix products, arithmetic and copies ran while one was open for 2% of the time, Pallas kernels for 14%

profile of v4, /device:TPU:32, one launch (start us, length us, event | category | flops | bytes accessed | tf_op | source)
XLA Modules:
  0.0 144.9 jit_solution(2591213448469643011)
XLA Ops:
  1.7 5.6 %collective-permute-start = (bf16[64,3584]{1,0:T(8,128)(2,1)S(1)}, bf16[64,3584]{1,0:T(8,128)(2,1)S(1)}, u32[]{:S(2)}, u32[]{:S(2)}) collective-permute-start(bf16[64,3584]{1,0:T(8,128)(2,1)S(1)} %get-tuple-element.93), channel_id=1, source_target_pairs={{0,224},{32,0},{64,32},{96,64},{128,96},{160,128},{192,160},{224,1... | collective-permute-start | bytes 1376264 | tf_op jit(solution)/shard_map/ppermute | solution.py:35
  13.0 2.4 %copy-done = bf16[768,3584]{1,0:T(8,128)(2,1)} copy-done((bf16[768,3584]{1,0:T(8,128)(2,1)}, bf16[768,3584]{1,0:T(8,128)(2,1)S(1)}, u32[]{:S(2)}) %copy-start) | copy-done | bytes 5505048
  15.4 2.5 %shard_map.102 = (f32[2,2,128,64]{3,2,1,0:T(8,128)S(1)}, f32[2,128,1]{2,1,0:T(8,128)S(1)}, f32[2,8,64]{2,1,0:T(8,128)S(1)}, f32[2,64,1]{2,1,0:T(8,128)S(1)}, bf16[32,3584]{1,0:T(8,128)(2,1)S(1)}) custom-call(s32[2]{0:T(128)S(1)} %pad_add_fusion.place, s32[8]{0:T(128)S(1)} %bitcast.25, s32[2,2,64]{2,1,0:T(2,128)S(1)} %bitcast.23, ...), custom_call_target="tpu_custom_call" | custom-call | flops 100000 | bytes 1000 | tf_op jit(solution)/shard_map/pallas_call | solution.py:316
  20.5 2.4 %collective-permute-done.1.second = bf16[64,3584]{1,0:T(8,128)(2,1)S(1)} collective-permute-done((bf16[64,3584]{1,0:T(8,128)(2,1)S(1)}, bf16[64,3584]{1,0:T(8,128)(2,1)S(1)}, u32[]{:S(2)}, u32[]{:S(2)}) %collective-permute-start.1) | collective-permute-done | bytes 458784 | tf_op jit(solution)/shard_map/ppermute | solution.py:35
  26.2 5.4 %collective-permute-done.2.low = bf16[32,3584]{1,0:T(8,128)(2,1)S(1)} collective-permute-done((bf16[32,3584]{1,0:T(8,128)(2,1)S(1)}, bf16[32,3584]{1,0:T(8,128)(2,1)S(1)}, u32[]{:S(2)}, u32[]{:S(2)}) %collective-permute-start.2) | collective-permute-done | bytes 229408 | tf_op jit(solution)/shard_map/ppermute | solution.py:40
  34.2 5.9 %collective-permute-start.9 = (bf16[32,3584]{1,0:T(8,128)(2,1)S(1)}, bf16[32,3584]{1,0:T(8,128)(2,1)S(1)}, u32[]{:S(2)}, u32[]{:S(2)}) collective-permute-start(bf16[32,3584]{1,0:T(8,128)(2,1)S(1)} %get-tuple-element.114), channel_id=1, source_target_pairs={{0,16},{1,17},{2,18},{3,19},{4,20},{5,21},{6,22},{7,23},{8,24},{9,... | collective-permute-start | bytes 688136 | tf_op jit(solution)/shard_map/ppermute | solution.py:40
  40.1 5.5 %collective-permute-done.5.theirs = bf16[64,3584]{1,0:T(8,128)(2,1)S(1)} collective-permute-done((bf16[64,3584]{1,0:T(8,128)(2,1)S(1)}, bf16[64,3584]{1,0:T(8,128)(2,1)S(1)}, u32[]{:S(2)}, u32[]{:S(2)}) %collective-permute-start.5) | collective-permute-done | bytes 458784 | tf_op jit(solution)/shard_map/ppermute | solution.py:44
  45.6 2.9 %shard_map.105 = (f32[64,3712]{1,0:T(8,128)S(1)}, bf16[64,3712]{1,0:T(8,128)(2,1)S(1)}) custom-call(s32[2]{0:T(128)S(1)} %pad_add_fusion.place, bf16[64,3584]{1,0:T(8,128)(2,1)S(1)} %shard_map.104.mine, bf16[64,3584]{1,0:T(8,128)(2,1)S(1)} %collective-permute-done.5.theirs, bf16[8,2,2,2,16,256]{5,4,3,2,1,0:T(8,128)(2,1)S(1)} %get-tuple-element.110.refs_0_, ...), custom_call_target="tpu_custom_call" | custom-call | flops 2000000000 | bytes 1000 | tf_op jit(solution)/shard_map/pallas_call | solution.py:344
  49.4 8.1 %collective-permute-start.11 = (bf16[32,3584]{1,0:T(8,128)(2,1)S(1)}, bf16[32,3584]{1,0:T(8,128)(2,1)S(1)}, u32[]{:S(2)}, u32[]{:S(2)}) collective-permute-start(bf16[32,3584]{1,0:T(8,128)(2,1)S(1)} %get-tuple-element.126), channel_id=1, source_target_pairs={{0,12},{1,13},{2,14},{3,15},{4,16},{5,17},{6,18},{7,19},{8,20},{9,... | collective-permute-start | bytes 688136 | tf_op jit(solution)/shard_map/ppermute | solution.py:40
  58.1 3.1 %shard_map.106 = (f32[32,3712]{1,0:T(8,128)S(1)}, bf16[32,3712]{1,0:T(8,128)(2,1)S(1)}) custom-call(s32[2]{0:T(128)S(1)} %pad_add_fusion.place, bf16[32,3584]{1,0:T(8,128)(2,1)S(1)} %collective-permute-done.9.mine, bf16[32,3584]{1,0:T(8,128)(2,1)S(1)} %collective-permute-done.10.theirs, bf16[8,2,2,2,16,256]{5,4,3,2,1,0:T(8,128)(2,1)S(1)} %get-tuple-element.110.refs_0_, ...), custom_call_target="tpu_custom_call" | custom-call | flops 20000000000 | bytes 1000 | tf_op jit(solution)/shard_map/pallas_call | solution.py:344
  61.2 10.1 %collective-permute-done.11.low = bf16[32,3584]{1,0:T(8,128)(2,1)S(1)} collective-permute-done((bf16[32,3584]{1,0:T(8,128)(2,1)S(1)}, bf16[32,3584]{1,0:T(8,128)(2,1)S(1)}, u32[]{:S(2)}, u32[]{:S(2)}) %collective-permute-start.11) | collective-permute-done | bytes 229408 | tf_op jit(solution)/shard_map/ppermute | solution.py:40
  71.3 3.2 %collective-permute-done.12.high = bf16[32,3584]{1,0:T(8,128)(2,1)S(1)} collective-permute-done((bf16[32,3584]{1,0:T(8,128)(2,1)S(1)}, bf16[32,3584]{1,0:T(8,128)(2,1)S(1)}, u32[]{:S(2)}, u32[]{:S(2)}) %collective-permute-start.12) | collective-permute-done | bytes 229408 | tf_op jit(solution)/shard_map/ppermute | solution.py:40
  76.7 4.1 %collective-permute-start.15 = (bf16[32,3584]{1,0:T(8,128)(2,1)S(1)}, bf16[32,3584]{1,0:T(8,128)(2,1)S(1)}, u32[]{:S(2)}, u32[]{:S(2)}) collective-permute-start(bf16[32,3584]{1,0:T(8,128)(2,1)S(1)} %get-tuple-element.137), channel_id=1, source_target_pairs={{0,24},{1,25},{2,26},{3,27},{4,28},{5,29},{6,30},{7,31},{8,0},{9,1... | collective-permute-start | bytes 688136 | tf_op jit(solution)/shard_map/ppermute | solution.py:40
  80.8 4.8 %collective-permute-done.13.theirs = bf16[64,3584]{1,0:T(8,128)(2,1)S(1)} collective-permute-done((bf16[64,3584]{1,0:T(8,128)(2,1)S(1)}, bf16[64,3584]{1,0:T(8,128)(2,1)S(1)}, u32[]{:S(2)}, u32[]{:S(2)}) %collective-permute-start.13) | collective-permute-done | bytes 458784 | tf_op jit(solution)/shard_map/ppermute | solution.py:44
  85.6 2.9 %shard_map.108 = (f32[64,3712]{1,0:T(8,128)S(1)}, bf16[64,3712]{1,0:T(8,128)(2,1)S(1)}) custom-call(s32[2]{0:T(128)S(1)} %pad_add_fusion.place, bf16[64,3584]{1,0:T(8,128)(2,1)S(1)} %shard_map.107.mine, bf16[64,3584]{1,0:T(8,128)(2,1)S(1)} %collective-permute-done.13.theirs, bf16[8,2,2,2,16,256]{5,4,3,2,1,0:T(8,128)(2,1)S(1)} %get-tuple-element.110.refs_0_, ...), custom_call_target="tpu_custom_call" | custom-call | flops 2000000000 | bytes 1000 | tf_op jit(solution)/shard_map/pallas_call | solution.py:344
  94.9 3.2 %collective-permute-start.21 = (bf16[32,3712]{1,0:T(8,128)(2,1)S(1)}, bf16[32,3712]{1,0:T(8,128)(2,1)S(1)}, u32[]{:S(2)}, u32[]{:S(2)}) collective-permute-start(bf16[32,3712]{1,0:T(8,128)(2,1)S(1)} %get-tuple-element.153), channel_id=1, source_target_pairs={{0,16},{1,17},{2,18},{3,19},{4,20},{5,21},{6,22},{7,23},{8,24},{9,... | collective-permute-start | bytes 712712 | tf_op jit(solution)/shard_map/ppermute | solution.py:40
  98.1 3.1 %shard_map.112 = (f32[32,3712]{1,0:T(8,128)S(1)}, bf16[32,3712]{1,0:T(8,128)(2,1)S(1)}) custom-call(s32[2]{0:T(128)S(1)} %pad_add_fusion.place, bf16[32,3584]{1,0:T(8,128)(2,1)S(1)} %get-tuple-element.157.mine, bf16[32,3584]{1,0:T(8,128)(2,1)S(1)} %collective-permute-done.4.theirs, bf16[8,2,2,2,16,256]{5,4,3,2,1,0:T(8,128)(2,1)S(1)} %get-tuple-element.110.refs_0_, ...), custom_call_target="tpu_custom_call" | custom-call | flops 2000000000 | bytes 1000 | tf_op jit(solution)/shard_map/pallas_call | solution.py:344
  103.1 2.9 %shard_map.110 = (f32[64,3712]{1,0:T(8,128)S(1)}, bf16[64,3712]{1,0:T(8,128)(2,1)S(1)}) custom-call(s32[2]{0:T(128)S(1)} %pad_add_fusion.place, bf16[64,3584]{1,0:T(8,128)(2,1)S(1)} %shard_map.109.mine, bf16[64,3584]{1,0:T(8,128)(2,1)S(1)} %collective-permute-done.17.theirs, bf16[8,2,2,2,16,256]{5,4,3,2,1,0:T(8,128)(2,1)S(1)} %get-tuple-element.110.refs_0_, ...), custom_call_target="tpu_custom_call" | custom-call | flops 2000000000 | bytes 1000 | tf_op jit(solution)/shard_map/pallas_call | solution.py:344
  108.0 3.7 %collective-permute-done.22.got = bf16[64,3712]{1,0:T(8,128)(2,1)S(1)} collective-permute-done((bf16[64,3712]{1,0:T(8,128)(2,1)S(1)}, bf16[64,3712]{1,0:T(8,128)(2,1)S(1)}, u32[]{:S(2)}, u32[]{:S(2)}) %collective-permute-start.22) | collective-permute-done | bytes 475168 | tf_op jit(solution)/shard_map/ppermute | solution.py:44
  111.8 5.7 %collective-permute-start.26 = (bf16[32,3712]{1,0:T(8,128)(2,1)S(1)}, bf16[32,3712]{1,0:T(8,128)(2,1)S(1)}, u32[]{:S(2)}, u32[]{:S(2)}) collective-permute-start(bf16[32,3712]{1,0:T(8,128)(2,1)S(1)} %get-tuple-element.173), channel_id=1, source_target_pairs={{0,20},{1,21},{2,22},{3,23},{4,24},{5,25},{6,26},{7,27},{8,28},{9,... | collective-permute-start | bytes 712712 | tf_op jit(solution)/shard_map/ppermute | solution.py:40
  120.8 4.6 %collective-permute-start.23 = (bf16[32,3712]{1,0:T(8,128)(2,1)S(1)}, bf16[32,3712]{1,0:T(8,128)(2,1)S(1)}, u32[]{:S(2)}, u32[]{:S(2)}) collective-permute-start(bf16[32,3712]{1,0:T(8,128)(2,1)S(1)} %get-tuple-element.164), channel_id=1, source_target_pairs={{0,24},{1,25},{2,26},{3,27},{4,28},{5,29},{6,30},{7,31},{8,0},{9,1... | collective-permute-start | bytes 712712 | tf_op jit(solution)/shard_map/ppermute | solution.py:40
  126.6 7.4 %collective-permute-done.26.b3 = bf16[32,3712]{1,0:T(8,128)(2,1)S(1)} collective-permute-done((bf16[32,3712]{1,0:T(8,128)(2,1)S(1)}, bf16[32,3712]{1,0:T(8,128)(2,1)S(1)}, u32[]{:S(2)}, u32[]{:S(2)}) %collective-permute-start.26) | collective-permute-done | bytes 237600 | tf_op jit(solution)/shard_map/ppermute | solution.py:40
  134.4 4.8 %collective-permute-done.23.b2 = bf16[32,3712]{1,0:T(8,128)(2,1)S(1)} collective-permute-done((bf16[32,3712]{1,0:T(8,128)(2,1)S(1)}, bf16[32,3712]{1,0:T(8,128)(2,1)S(1)}, u32[]{:S(2)}, u32[]{:S(2)}) %collective-permute-start.23) | collective-permute-done | bytes 237600 | tf_op jit(solution)/shard_map/ppermute | solution.py:40
  139.2 3.5 %collective-permute-done.24.b6 = bf16[32,3712]{1,0:T(8,128)(2,1)S(1)} collective-permute-done((bf16[32,3712]{1,0:T(8,128)(2,1)S(1)}, bf16[32,3712]{1,0:T(8,128)(2,1)S(1)}, u32[]{:S(2)}, u32[]{:S(2)}) %collective-permute-start.24) | collective-permute-done | bytes 237600 | tf_op jit(solution)/shard_map/ppermute | solution.py:40
  (74 shorter events, 36.7 us)
Async XLA Ops:
  1.7 18.7 %collective-permute-start = (bf16[64,3584]{1,0:T(8,128)(2,1)S(1)}, bf16[64,3584]{1,0:T(8,128)(2,1)S(1)}, u32[]{:S(2)}, u32[]{:S(2)}) collective-permute-start(bf16[64,3584]{1,0:T(8,128)(2,1)S(1)} %get-tuple-element.93), channel_id=1, source_target_pairs={{0,224},{32,0},{64,32},{96,64},{128,96},{160,128},{192,160},{224,1... | collective-permute-start | bytes 1376264 | tf_op jit(solution)/shard_map/ppermute | solution.py:35
  7.3 15.6 %collective-permute-start.1 = (bf16[64,3584]{1,0:T(8,128)(2,1)S(1)}, bf16[64,3584]{1,0:T(8,128)(2,1)S(1)}, u32[]{:S(2)}, u32[]{:S(2)}) collective-permute-start(bf16[64,3584]{1,0:T(8,128)(2,1)S(1)} %get-tuple-element.94), channel_id=1, source_target_pairs={{0,32},{32,64},{64,96},{96,128},{128,160},{160,192},{192,224},{224... | collective-permute-start | bytes 1376264 | tf_op jit(solution)/shard_map/ppermute | solution.py:35
  22.9 22.7 %collective-permute-start.7 = (bf16[768,3584]{1,0:T(8,128)(2,1)}, bf16[768,3584]{1,0:T(8,128)(2,1)S(1)}, u32[]{:S(2)}, u32[]{:S(2)}) collective-permute-start(bf16[768,3584]{1,0:T(8,128)(2,1)} %copy-done), channel_id=1, source_target_pairs={{0,1},{1,0},{2,3},{3,2},{4,5},{5,4},{6,7},{7,6},{8,9},{9,8},{10,11... | collective-permute-start | bytes 16515080 | tf_op jit(solution)/shard_map/ppermute | solution.py:48
  26.2 13.9 %collective-permute-start.6 = (bf16[8,2,2,2,16,256]{5,4,3,2,1,0:T(8,128)(2,1)S(1)}, bf16[8,2,2,2,16,256]{5,4,3,2,1,0:T(8,128)(2,1)S(1)}, u32[]{:S(2)}, u32[]{:S(2)}) collective-permute-start(bf16[8,2,2,2,16,256]{5,4,3,2,1,0:T(8,128)(2,1)S(1)} %get-tuple-element.111), channel_id=1, source_target_pairs={{0,1},{1,0},{2,3},{3,2},{4,5},{5,4},{6,7},{7,6},{8,9},{9,8},{10,11... | collective-permute-start | bytes 1572872 | tf_op jit(solution)/shard_map/ppermute | solution.py:48
  33.5 12.1 %collective-permute-start.5 = (bf16[64,3584]{1,0:T(8,128)(2,1)S(1)}, bf16[64,3584]{1,0:T(8,128)(2,1)S(1)}, u32[]{:S(2)}, u32[]{:S(2)}) collective-permute-start(bf16[64,3584]{1,0:T(8,128)(2,1)S(1)} %shard_map.104.mine), channel_id=1, source_target_pairs={{0,2},{1,3},{2,0},{3,1},{4,6},{5,7},{6,4},{7,5},{8,10},{9,11},{10,... | collective-permute-start | bytes 1376264 | tf_op jit(solution)/shard_map/ppermute | solution.py:44
  34.2 14.4 %collective-permute-start.9 = (bf16[32,3584]{1,0:T(8,128)(2,1)S(1)}, bf16[32,3584]{1,0:T(8,128)(2,1)S(1)}, u32[]{:S(2)}, u32[]{:S(2)}) collective-permute-start(bf16[32,3584]{1,0:T(8,128)(2,1)S(1)} %get-tuple-element.114), channel_id=1, source_target_pairs={{0,16},{1,17},{2,18},{3,19},{4,20},{5,21},{6,22},{7,23},{8,24},{9,... | collective-permute-start | bytes 688136 | tf_op jit(solution)/shard_map/ppermute | solution.py:40
  49.4 21.9 %collective-permute-start.11 = (bf16[32,3584]{1,0:T(8,128)(2,1)S(1)}, bf16[32,3584]{1,0:T(8,128)(2,1)S(1)}, u32[]{:S(2)}, u32[]{:S(2)}) collective-permute-start(bf16[32,3584]{1,0:T(8,128)(2,1)S(1)} %get-tuple-element.126), channel_id=1, source_target_pairs={{0,12},{1,13},{2,14},{3,15},{4,16},{5,17},{6,18},{7,19},{8,20},{9,... | collective-permute-start | bytes 688136 | tf_op jit(solution)/shard_map/ppermute | solution.py:40
  57.5 17.0 %collective-permute-start.12 = (bf16[32,3584]{1,0:T(8,128)(2,1)S(1)}, bf16[32,3584]{1,0:T(8,128)(2,1)S(1)}, u32[]{:S(2)}, u32[]{:S(2)}) collective-permute-start(bf16[32,3584]{1,0:T(8,128)(2,1)S(1)} %get-tuple-element.127), channel_id=1, source_target_pairs={{0,20},{1,21},{2,22},{3,23},{4,24},{5,25},{6,26},{7,27},{8,28},{9,... | collective-permute-start | bytes 688136 | tf_op jit(solution)/shard_map/ppermute | solution.py:40
  57.5 17.0 %collective-permute-start.8 = (bf16[64,3712]{1,0:T(8,128)(2,1)S(1)}, bf16[64,3712]{1,0:T(8,128)(2,1)S(1)}, u32[]{:S(2)}, u32[]{:S(2)}) collective-permute-start(bf16[64,3712]{1,0:T(8,128)(2,1)S(1)} %get-tuple-element.113), channel_id=1, source_target_pairs={{0,2},{1,3},{2,0},{3,1},{4,6},{5,7},{6,4},{7,5},{8,10},{9,11},{10,... | collective-permute-start | bytes 1425416 | tf_op jit(solution)/shard_map/ppermute | solution.py:44
  74.6 11.1 %collective-permute-start.13 = (bf16[64,3584]{1,0:T(8,128)(2,1)S(1)}, bf16[64,3584]{1,0:T(8,128)(2,1)S(1)}, u32[]{:S(2)}, u32[]{:S(2)}) collective-permute-start(bf16[64,3584]{1,0:T(8,128)(2,1)S(1)} %shard_map.107.mine), channel_id=1, source_target_pairs={{0,2},{1,3},{2,0},{3,1},{4,6},{5,7},{6,4},{7,5},{8,10},{9,11},{10,... | collective-permute-start | bytes 1376264 | tf_op jit(solution)/shard_map/ppermute | solution.py:44
  75.6 14.7 %collective-permute-start.16 = (bf16[32,3712]{1,0:T(8,128)(2,1)S(1)}, bf16[32,3712]{1,0:T(8,128)(2,1)S(1)}, u32[]{:S(2)}, u32[]{:S(2)}) collective-permute-start(bf16[32,3712]{1,0:T(8,128)(2,1)S(1)} %get-tuple-element.138), channel_id=1, source_target_pairs={{0,2},{1,3},{2,0},{3,1},{4,6},{5,7},{6,4},{7,5},{8,10},{9,11},{10,... | collective-permute-start | bytes 712712 | tf_op jit(solution)/shard_map/ppermute | solution.py:44
  76.7 11.9 %collective-permute-start.14 = (bf16[32,3584]{1,0:T(8,128)(2,1)S(1)}, bf16[32,3584]{1,0:T(8,128)(2,1)S(1)}, u32[]{:S(2)}, u32[]{:S(2)}) collective-permute-start(bf16[32,3584]{1,0:T(8,128)(2,1)S(1)} %get-tuple-element.136), channel_id=1, source_target_pairs={{0,8},{1,9},{2,10},{3,11},{4,12},{5,13},{6,14},{7,15},{8,16},{9,17... | collective-permute-start | bytes 688136 | tf_op jit(solution)/shard_map/ppermute | solution.py:40
  76.7 12.4 %collective-permute-start.15 = (bf16[32,3584]{1,0:T(8,128)(2,1)S(1)}, bf16[32,3584]{1,0:T(8,128)(2,1)S(1)}, u32[]{:S(2)}, u32[]{:S(2)}) collective-permute-start(bf16[32,3584]{1,0:T(8,128)(2,1)S(1)} %get-tuple-element.137), channel_id=1, source_target_pairs={{0,24},{1,25},{2,26},{3,27},{4,28},{5,29},{6,30},{7,31},{8,0},{9,1... | collective-permute-start | bytes 688136 | tf_op jit(solution)/shard_map/ppermute | solution.py:40
  90.3 12.7 %collective-permute-start.17 = (bf16[64,3584]{1,0:T(8,128)(2,1)S(1)}, bf16[64,3584]{1,0:T(8,128)(2,1)S(1)}, u32[]{:S(2)}, u32[]{:S(2)}) collective-permute-start(bf16[64,3584]{1,0:T(8,128)(2,1)S(1)} %shard_map.109.mine), channel_id=1, source_target_pairs={{0,2},{1,3},{2,0},{3,1},{4,6},{5,7},{6,4},{7,5},{8,10},{9,11},{10,... | collective-permute-start | bytes 1376264 | tf_op jit(solution)/shard_map/ppermute | solution.py:44
  91.3 20.3 %collective-permute-start.22 = (bf16[64,3712]{1,0:T(8,128)(2,1)S(1)}, bf16[64,3712]{1,0:T(8,128)(2,1)S(1)}, u32[]{:S(2)}, u32[]{:S(2)}) collective-permute-start(bf16[64,3712]{1,0:T(8,128)(2,1)S(1)} %get-tuple-element.154), channel_id=1, source_target_pairs={{0,2},{1,3},{2,0},{3,1},{4,6},{5,7},{6,4},{7,5},{8,10},{9,11},{10,... | collective-permute-start | bytes 1425416 | tf_op jit(solution)/shard_map/ppermute | solution.py:44
  92.7 14.7 %collective-permute-start.19 = (bf16[32,3712]{1,0:T(8,128)(2,1)S(1)}, bf16[32,3712]{1,0:T(8,128)(2,1)S(1)}, u32[]{:S(2)}, u32[]{:S(2)}) collective-permute-start(bf16[32,3712]{1,0:T(8,128)(2,1)S(1)} %get-tuple-element.151), channel_id=1, source_target_pairs={{0,28},{1,29},{2,30},{3,31},{4,0},{5,1},{6,2},{7,3},{8,4},{9,5},{1... | collective-permute-start | bytes 712712 | tf_op jit(solution)/shard_map/ppermute | solution.py:40
  92.8 14.6 %collective-permute-start.20 = (bf16[32,3712]{1,0:T(8,128)(2,1)S(1)}, bf16[32,3712]{1,0:T(8,128)(2,1)S(1)}, u32[]{:S(2)}, u32[]{:S(2)}) collective-permute-start(bf16[32,3712]{1,0:T(8,128)(2,1)S(1)} %get-tuple-element.152), channel_id=1, source_target_pairs={{0,4},{1,5},{2,6},{3,7},{4,8},{5,9},{6,10},{7,11},{8,12},{9,13},{1... | collective-permute-start | bytes 712712 | tf_op jit(solution)/shard_map/ppermute | solution.py:40
  94.9 13.1 %collective-permute-start.21 = (bf16[32,3712]{1,0:T(8,128)(2,1)S(1)}, bf16[32,3712]{1,0:T(8,128)(2,1)S(1)}, u32[]{:S(2)}, u32[]{:S(2)}) collective-permute-start(bf16[32,3712]{1,0:T(8,128)(2,1)S(1)} %get-tuple-element.153), channel_id=1, source_target_pairs={{0,16},{1,17},{2,18},{3,19},{4,20},{5,21},{6,22},{7,23},{8,24},{9,... | collective-permute-start | bytes 712712 | tf_op jit(solution)/shard_map/ppermute | solution.py:40
  106.0 14.6 %collective-permute-start.18 = (bf16[64,3712]{1,0:T(8,128)(2,1)S(1)}, bf16[64,3712]{1,0:T(8,128)(2,1)S(1)}, u32[]{:S(2)}, u32[]{:S(2)}) collective-permute-start(bf16[64,3712]{1,0:T(8,128)(2,1)S(1)} %get-tuple-element.146), channel_id=1, source_target_pairs={{0,2},{1,3},{2,0},{3,1},{4,6},{5,7},{6,4},{7,5},{8,10},{9,11},{10,... | collective-permute-start | bytes 1425416 | tf_op jit(solution)/shard_map/ppermute | solution.py:44
  111.8 22.2 %collective-permute-start.26 = (bf16[32,3712]{1,0:T(8,128)(2,1)S(1)}, bf16[32,3712]{1,0:T(8,128)(2,1)S(1)}, u32[]{:S(2)}, u32[]{:S(2)}) collective-permute-start(bf16[32,3712]{1,0:T(8,128)(2,1)S(1)} %get-tuple-element.173), channel_id=1, source_target_pairs={{0,20},{1,21},{2,22},{3,23},{4,24},{5,25},{6,26},{7,27},{8,28},{9,... | collective-permute-start | bytes 712712 | tf_op jit(solution)/shard_map/ppermute | solution.py:40
  117.5 16.5 %collective-permute-start.27 = (bf16[32,3712]{1,0:T(8,128)(2,1)S(1)}, bf16[32,3712]{1,0:T(8,128)(2,1)S(1)}, u32[]{:S(2)}, u32[]{:S(2)}) collective-permute-start(bf16[32,3712]{1,0:T(8,128)(2,1)S(1)} %get-tuple-element.174), channel_id=1, source_target_pairs={{0,12},{1,13},{2,14},{3,15},{4,16},{5,17},{6,18},{7,19},{8,20},{9,... | collective-permute-start | bytes 712712 | tf_op jit(solution)/shard_map/ppermute | solution.py:40
  117.7 16.2 %collective-permute-start.25 = (bf16[32,3712]{1,0:T(8,128)(2,1)S(1)}, bf16[32,3712]{1,0:T(8,128)(2,1)S(1)}, u32[]{:S(2)}, u32[]{:S(2)}) collective-permute-start(bf16[32,3712]{1,0:T(8,128)(2,1)S(1)} %get-tuple-element.167), channel_id=1, source_target_pairs={{0,2},{1,3},{2,0},{3,1},{4,6},{5,7},{6,4},{7,5},{8,10},{9,11},{10,... | collective-permute-start | bytes 712712 | tf_op jit(solution)/shard_map/ppermute | solution.py:44
  120.8 18.4 %collective-permute-start.23 = (bf16[32,3712]{1,0:T(8,128)(2,1)S(1)}, bf16[32,3712]{1,0:T(8,128)(2,1)S(1)}, u32[]{:S(2)}, u32[]{:S(2)}) collective-permute-start(bf16[32,3712]{1,0:T(8,128)(2,1)S(1)} %get-tuple-element.164), channel_id=1, source_target_pairs={{0,24},{1,25},{2,26},{3,27},{4,28},{5,29},{6,30},{7,31},{8,0},{9,1... | collective-permute-start | bytes 712712 | tf_op jit(solution)/shard_map/ppermute | solution.py:40
  125.4 17.3 %collective-permute-start.24 = (bf16[32,3712]{1,0:T(8,128)(2,1)S(1)}, bf16[32,3712]{1,0:T(8,128)(2,1)S(1)}, u32[]{:S(2)}, u32[]{:S(2)}) collective-permute-start(bf16[32,3712]{1,0:T(8,128)(2,1)S(1)} %get-tuple-element.165), channel_id=1, source_target_pairs={{0,8},{1,9},{2,10},{3,11},{4,12},{5,13},{6,14},{7,15},{8,16},{9,17... | collective-permute-start | bytes 712712 | tf_op jit(solution)/shard_map/ppermute | solution.py:40
  (15 other events, 86.6 us)
